TPU v7x, 32 devices: a whole 2x2x4 slice. The times are simulated.
32 devices in a mesh: group: 2 (over y), mem: 8 (over z, x), col: 2 (over core).
Axes of the slice: x: 2, y: 2, z: 4, core: 2. Of those that a mesh axis runs over, the one named last changes fastest.
Arguments:
- grads: bfloat16 [4096, 2048], P(('group', 'mem')), parts along dimension 0, may hold values from -6 to 6
- values: bfloat16 [4096, 512], P('mem', 'col'), may hold values from -0.25 to 0.25
- expand_weight: bfloat16 [4, 512, 2048], P(None, 'col', 'mem'), may hold values from -0.125 to 0.125
- row_factors: float32 [4096, 16], P(('group', 'mem')), parts along dimension 0, may hold values from -5 to 5
- col_factors: float32 [4096, 16], P(('group', 'mem')), parts along dimension 0, may hold values from -5 to 5
- core: float32 [2, 2], replicated, may hold values from -3 to 3
- pair_index: int32 [2, 2048], P(None, ('group', 'mem')), parts along dimension 1, may hold values from 0 to 16383, as said below
- counts: int32 [128], P(('group', 'mem')), parts along dimension 0, may hold values from 1 to 16, as said below
Outputs:
- value_grad: float32 [8192, 512], P(('group', 'mem'), 'col'), parts along dimension 0
- row_grad: float32 [4096, 16], P(('group', 'mem')), parts along dimension 0
- col_grad: float32 [4096, 16], P(('group', 'mem')), parts along dimension 0
- core_grad: float32 [4, 2], P('group'), parts along dimension 0
There are 2 independent parts, one for each index of `group`. A program takes and returns all parts, laid end to end along the dimension named above; an argument that names none is the same for every part. Nothing has to cross between parts.
Inputs may be any that keep to these rules, and one draw needn't show every extreme that they name: `counts`: every block has at least 2 live rows; one owner has 16 live rows from every source, and each source fills one block completely. Padding rows hold zeros. Value rows lie below 512, tokens below 256. `pair_index`: row 0 lies below 16384, row 1 below 512.
All inputs are finite; a program needn't handle non-finite values.
Results may differ from a plain program's by a relative error of at most 0.0051.
Values may be sent and summed in bfloat16 or wider, within the bound.
No kernel may reach another device: no remote copies, remote signals or barrier semaphores. Data moves between devices by JAX's collectives and lax.ppermute only.
A program may use at most 64 MiB of HBM per device.

v0:
```python
import jax
import jax.numpy as jnp
from jax import lax
from jax.sharding import PartitionSpec as P

E = 4
RANK = 2
NR = 8
NC = 8
KC = 64


def local(grads, values, expand_weight, row_factors, col_factors, core, pair_index, counts):
    nmem = lax.axis_size("mem")
    tokens = grads.shape[0]
    width = values.shape[1]
    vrows = values.shape[0]
    rows = pair_index.shape[1]
    cap = rows // nmem
    high = lax.Precision.HIGHEST
    expanded = jnp.einsum(
        "tn,evn->tev",
        grads,
        lax.all_gather(expand_weight, "mem", axis=2, tiled=True),
        preferred_element_type=jnp.float32,
    ).astype(jnp.bfloat16)
    code = pair_index[0]
    local_row = pair_index[1]
    within = jnp.tile(jnp.arange(cap, dtype=jnp.int32), nmem)
    owner = jnp.repeat(jnp.arange(nmem, dtype=jnp.int32), cap)
    live = within < counts[owner]
    token = code // (NR * NC)
    row_cand = code // NC % NR
    col_cand = code % NC
    a_p = row_factors.reshape(tokens, NR, RANK)[token, row_cand]
    b_p = col_factors.reshape(tokens, NC, RANK)[token, col_cand]
    core_b = jnp.dot(b_p, core.T, precision=high)
    core_a = jnp.dot(a_p, core, precision=high)
    score = jnp.where(live, jnp.sum(a_p * core_b, -1), 0.0).astype(jnp.bfloat16)
    proj = local_row % KC % E
    pair_grad = jnp.where(live[:, None], expanded[token, proj], jnp.zeros((), jnp.bfloat16))
    got_row = lax.all_to_all(
        local_row.reshape(nmem, cap), "mem", split_axis=0, concat_axis=0, tiled=True
    ).reshape(rows)
    fetched = lax.all_to_all(
        values[got_row].reshape(nmem, cap, width), "mem", split_axis=0, concat_axis=0, tiled=True
    ).reshape(rows, width)
    own_contrib = (score.astype(jnp.float32)[:, None] * pair_grad.astype(jnp.float32)).astype(
        jnp.bfloat16
    )
    contrib = lax.all_to_all(
        own_contrib.reshape(nmem, cap, width), "mem", split_axis=0, concat_axis=0, tiled=True
    ).reshape(rows, width)
    dscore = jnp.einsum("pv,pv->p", pair_grad, fetched, preferred_element_type=jnp.float32)
    block = min(2048, rows)

    def add_block(step, total):
        onehot = (jnp.arange(vrows, dtype=jnp.int32)[:, None] == got_row[None, :]).astype(
            jnp.bfloat16
        )
        return total + jnp.dot(onehot, contrib, preferred_element_type=jnp.float32)

    value_grad = lax.fori_loop(0, rows // block, add_block, jnp.zeros((vrows, width), jnp.float32))
    dscore = lax.psum(dscore, "col")
    row_grad = jax.ops.segment_sum(
        dscore[:, None] * core_b, token * NR + row_cand, num_segments=tokens * NR
    )
    col_grad = jax.ops.segment_sum(
        dscore[:, None] * core_a, token * NC + col_cand, num_segments=tokens * NC
    )
    row_grad = row_grad.reshape(tokens, NR * RANK)
    col_grad = col_grad.reshape(tokens, NC * RANK)
    core_part = jnp.dot((dscore[:, None] * a_p).T, b_p, precision=high)
    core_grad = lax.psum(core_part, "mem")
    return (value_grad, row_grad, col_grad, core_grad)


def solution(mesh):
    return jax.shard_map(
        local,
        mesh=mesh,
        in_specs=(
            P(("group", "mem"), None),
            P("mem", "col"),
            P(None, "col", "mem"),
            P(("group", "mem"), None),
            P(("group", "mem"), None),
            P(),
            P(None, ("group", "mem")),
            P(("group", "mem")),
        ),
        out_specs=(
            P(("group", "mem"), "col"),
            P(("group", "mem"), None),
            P(("group", "mem"), None),
            P("group", None),
        ),
        check_vma=False,
    )
```

profile of v0, /device:TPU:0, one launch (start us, length us, event | category | flops | bytes accessed | tf_op | source)
XLA Modules:
  0.0 136.2 jit_solution(3247081697077438788)
XLA Ops:
  7.2 0.0 copy-start
  7.2 0.0 copy-start.1
  7.2 0.0 all-gather.2.cloned.1.call-start
  7.2 0.7 all-gather.2.cloned.1.call-update
  7.9 0.7 slice_reduce_fusion
  8.6 0.7 all_to_all.12
  9.3 7.3 %all-to-all-start = ((s32[8,1,16]{2,1,0:T(1,128)}), s32[8,1,16]{2,1,0:T(1,128)S(1)}, u32[]{:S(2)}, u32[]{:S(2)}) async-start(s32[8,1,16]{2,1,0:T(1,128)} %bitcast), calls=%async_computation | async-start | bytes 8192 | tf_op jit(solution)/shard_map/all_to_all | solution.py:42
  16.6 0.1 tile.13
  16.6 0.1 reshape.466
  16.7 1.6 %fusion.32 = (s32[1]{0:T(128)}, s32[1]{0:T(128)}, s32[1]{0:T(128)}, s32[1]{0:T(128)}, s32[1]{0:T(128)}, /*index=5*/s32[1]{0:T(128)}, s32[1]{0:T(128)}, s32[1]{0:T(128)}) fusion(s32[8]{0:T(128)} %param.15), kind=kLoop, calls=%fused_computation.83 | loop fusion | bytes 64 | tf_op jit(solution)/shard_map/gather | solution.py:31
  18.3 0.7 add_bitcast_fusion
  19.0 5.0 %fusion.31 = (pred[128]{0:T(512)(128)(4,1)S(1)}, s32[128]{0:T(128)S(1)}) fusion(s32[128]{0:T(128)S(1)} %tile.13, s32[]{:T(128)} %bitcast.9, s32[]{:T(128)} %bitcast.8, s32[]{:T(128)} %bitcast.7, s32[]{:T(128)} %bitcast.6, s32[]{:T(128)} %bitcast.5, s32[]{:T(128)} %bitcast.4, s32[]{:T(128)} %bitcast.3, s32[]{:T(128)} %bitcast.2, s32[128,1]{0,1:T(1,128)S(1)} %reshape.466), kind=kLoop, calls=%fused_computation.82 | loop fusion | flops 2304 | bytes 1696 | tf_op jit(solution)/shard_map/lt | solution.py:31
  24.0 0.8 add_bitcast_fusion.1
  24.8 0.7 reshape.467
  25.6 0.4 copy.27
  26.0 1.0 gather_fusion
  27.0 0.1 copy.29
  27.0 0.8 reshape.468
  27.8 0.4 copy.28
  28.2 0.1 gather.20
  28.3 1.0 gather_fusion.1
  29.3 0.0 all-to-all-done
  29.3 0.1 reshape.470
  29.4 0.0 copy-done.1
  29.4 1.5 %gather_fusion.3 = bf16[128,256]{1,0:T(8,128)(2,1)} fusion(bf16[512,256]{1,0:T(8,128)(2,1)S(1)} %copy-done.1, s32[1024]{0:T(1024)S(1)} %pad_clamp_fusion), kind=kCustom, calls=%fused_computation.3 | custom fusion | bytes 131584 | tf_op jit(solution)/shard_map/gather | solution.py:46
  30.8 6.0 %all-to-all-start.2 = ((bf16[8,16,256]{2,1,0:T(8,128)(2,1)}), bf16[8,16,256]{2,1,0:T(8,128)(2,1)S(1)}, u32[]{:S(2)}, u32[]{:S(2)}) async-start(bf16[8,16,256]{2,1,0:T(8,128)(2,1)} %bitcast.21), calls=%async_computation.2 | async-start | bytes 131072 | tf_op jit(solution)/shard_map/all_to_all | solution.py:45
  36.9 0.5 broadcast.646
  37.4 0.7 reduce.11
  38.0 0.1 eq.28
  38.1 0.0 copy-start.2
  38.1 50.6 %all-gather.2.cloned.1.call-done = bf16[4,256,2048]{2,1,0:T(8,128)(2,1)} async-done(((bf16[4,256,256]{2,1,0:T(8,128)(2,1)}), bf16[4,256,2048]{2,1,0:T(8,128)(2,1)}) %all-gather.2.cloned.1.call-update) | async-done | bytes 4194320 | tf_op jit(solution)/shard_map/all_gather | solution.py:24
  88.7 0.0 copy-done
  88.7 3.5 %convolution_convert_fusion = bf16[256,4,256]{2,0,1:T(8,128)(2,1)S(1)} fusion(bf16[4,256,2048]{2,1,0:T(8,128)(2,1)} %all-gather.2.cloned.1.call-done, bf16[256,2048]{1,0:T(8,128)(2,1)S(1)} %copy-done), kind=kOutput, calls=%fused_computation.6 | convolution fusion | flops 1074003968 | bytes 5767168 | tf_op jit(solution)/shard_map/tn,evn->tev/dot_general | solution.py:21
  92.2 0.4 copy.30
  92.6 1.1 gather_fusion.2
  93.7 0.0 all-to-all-done.2
  93.7 0.2 fusion.6
  93.9 2.5 %psum.14 = f32[128]{0:T(128)S(1)} all-reduce(f32[128]{0:T(128)S(1)} %fusion.6), channel_id=1, replica_groups=mesh['group'=2,'mem'=8,'col'=2] {'col'}, use_global_device_ids=true, to_apply=%region_1.2 | all-reduce | flops 128 | bytes 1024 | tf_op jit(solution)/shard_map/psum | solution.py:64
  96.4 0.2 fusion.9
  96.5 0.0 copy-done.2
  96.5 0.2 broadcast_multiply_fusion
  96.8 0.1 reduce_sum.12
  96.9 0.7 multiply_convert_fusion
  97.6 3.4 %all-to-all-start.1 = ((bf16[8,16,256]{2,1,0:T(8,128)(2,1)}), bf16[8,16,256]{2,1,0:T(8,128)(2,1)S(1)}, u32[]{:S(2)}, u32[]{:S(2)}) async-start(bf16[8,16,256]{2,1,0:T(8,128)(2,1)} %multiply_convert_fusion), calls=%async_computation.1 | async-start | bytes 131072 | tf_op jit(solution)/shard_map/all_to_all | solution.py:51
  101.0 0.1 copy.31
  101.1 1.3 scatter_custom_fusion
  102.4 0.3 reshape.473
  102.7 0.7 copy.34
  103.4 22.3 %psum.15 = f32[2,2]{1,0:T(2,128)} all-reduce(f32[2,2]{1,0:T(2,128)S(1)} %fusion.9), channel_id=1, replica_groups=mesh['group'=2,'mem'=8,'col'=2] {'mem'}, use_global_device_ids=true, to_apply=%region_4.5 | all-reduce | flops 4 | bytes 32 | tf_op jit(solution)/shard_map/psum | solution.py:74
  125.7 0.2 convolution_multiply_fusion
  125.9 0.2 copy.32
  126.1 1.3 scatter_custom_fusion.1
  127.3 0.3 reshape.474
  127.7 0.7 copy.35
  128.3 0.0 all-to-all-done.1
  128.3 1.0 fusion.5
  (6 shorter events, 0.0 us)
Async XLA Ops:
  7.2 81.6 %copy-start = (bf16[256,2048]{1,0:T(8,128)(2,1)S(1)}, bf16[256,2048]{1,0:T(8,128)(2,1)}, u32[]{:S(2)}) copy-start(bf16[256,2048]{1,0:T(8,128)(2,1)} %param.8) | copy-start | bytes 3145732
  7.2 22.2 %copy-start.1 = (bf16[512,256]{1,0:T(8,128)(2,1)S(1)}, bf16[512,256]{1,0:T(8,128)(2,1)}, u32[]{:S(2)}) copy-start(bf16[512,256]{1,0:T(8,128)(2,1)} %param.9) | copy-start | bytes 786436
  7.2 81.5 %all-gather.2.cloned.1.call-start = ((), (), s32[]{:S(2)}) async-start(), calls=%async_computation.3 | async-start | bytes 4718592 | tf_op jit(solution)/shard_map/all_gather | solution.py:24
  9.3 20.0 %all-to-all-start = ((s32[8,1,16]{2,1,0:T(1,128)}), s32[8,1,16]{2,1,0:T(1,128)S(1)}, u32[]{:S(2)}, u32[]{:S(2)}) async-start(s32[8,1,16]{2,1,0:T(1,128)} %bitcast), calls=%async_computation | async-start | bytes 8192 | tf_op jit(solution)/shard_map/all_to_all | solution.py:42
  30.8 62.9 %all-to-all-start.2 = ((bf16[8,16,256]{2,1,0:T(8,128)(2,1)}), bf16[8,16,256]{2,1,0:T(8,128)(2,1)S(1)}, u32[]{:S(2)}, u32[]{:S(2)}) async-start(bf16[8,16,256]{2,1,0:T(8,128)(2,1)} %bitcast.21), calls=%async_computation.2 | async-start | bytes 131072 | tf_op jit(solution)/shard_map/all_to_all | solution.py:45
  38.1 58.4 %copy-start.2 = (f32[2,2]{1,0:T(2,128)S(1)}, f32[2,2]{1,0:T(2,128)}, u32[]{:S(2)}) copy-start(f32[2,2]{1,0:T(2,128)} %param.13) | copy-start | bytes 52
  97.6 30.7 %all-to-all-start.1 = ((bf16[8,16,256]{2,1,0:T(8,128)(2,1)}), bf16[8,16,256]{2,1,0:T(8,128)(2,1)S(1)}, u32[]{:S(2)}, u32[]{:S(2)}) async-start(bf16[8,16,256]{2,1,0:T(8,128)(2,1)} %multiply_convert_fusion), calls=%async_computation.1 | async-start | bytes 131072 | tf_op jit(solution)/shard_map/all_to_all | solution.py:51
Sparse Core Ops, SparseCore 0:
  10.1 78.6 all-gather.1
where the time goes:
time: 137 us; the launch traced here: 136 us
  waiting for transfers between devices  51.3 us (37%)
  blocking collectives  24.8 us (18%)
  starting transfers between devices  16.6 us (12%)
  between operations  14.2 us (10%)
  local copies, waits for them, and re-layouts  13.6 us (10%)
  other arithmetic  10.6 us (8%)
  matrix products  5.08 us (4%)
    all_gather x1, waiting for transfers between devices, local(): lax.all_gather(expand_weight, 'mem', axis=2, tiled=True)  50.6 us
    psum x1, blocking collectives, local(): core_grad = lax.psum(core_part, 'mem')  22.3 us
    all_to_all x1, starting transfers between devices, local(): lax.all_to_all(local_row.reshape(nmem, cap), 'mem', split_axis=0, concat_...  7.25 us
    all_to_all x1, starting transfers between devices, local(): lax.all_to_all(values[got_row].reshape(nmem, cap, width), 'mem', split_ax...  6 us
    lt x1, other arithmetic, local(): live = within < counts[owner]  4.99 us
    dot_general x1, matrix products, local(): jnp.einsum('tn,evn->tev', grads, lax.all_gather(expand_weight, 'mem', axi...  3.46 us
    all_to_all x1, starting transfers between devices, local(): lax.all_to_all(own_contrib.reshape(nmem, cap, width), 'mem', split_axis=0...  3.35 us
  transfers between devices with their start and end apart: 4, of which 1 were waited for; matrix products, arithmetic and copies ran while one was open for 19% of the time, Pallas kernels for 0%

commit v1 on v0

--- a/solution.py
+++ b/solution.py
@@ -1,6 +1,11 @@
+import functools
+
 import jax
 import jax.numpy as jnp
 from jax import lax
+from jax.experimental import pallas as pl
+from jax.experimental.pallas import tpu as pltpu
+from jax.sharding import Mesh
 from jax.sharding import PartitionSpec as P
 
 E = 4
@@ -8,9 +13,15 @@
 NR = 8
 NC = 8
 KC = 64
-
-
-def local(grads, values, expand_weight, row_factors, col_factors, core, pair_index, counts):
+HIGH = lax.Precision.HIGHEST
+F32 = jnp.float32
+BF16 = jnp.bfloat16
+
+SCORE, ROW_HIGH, ROW_LOW, OUTER, OUTER_REST = 0, 1, 2, 16, 20
+RECORD = 64
+
+
+def local_weights(grads, values, expand_weight, row_factors, col_factors, core, pair_index, counts):
     nmem = lax.axis_size("mem")
     tokens = grads.shape[0]
     width = values.shape[1]
@@ -75,25 +86,314 @@
     return (value_grad, row_grad, col_grad, core_grad)
 
 
+def iota(shape, dim):
+    return lax.broadcasted_iota(jnp.int32, shape, dim)
+
+
+def dot_nt(x, y, precision=None):
+    return lax.dot_general(
+        x, y, (((1,), (1,)), ((), ())), precision=precision, preferred_element_type=F32
+    )
+
+
+def prepare_kernel(far, pair, counts, core, row_fac, col_fac, grads, send, scaled, hits):
+    nmem = 2 * far
+    rows = pair.shape[1]
+    cap = rows // nmem
+    half = cap // 2
+    tokens, depth = grads.shape
+    shard = depth // nmem
+    code = pair[0:1, :]
+    local_row = pair[1:2, :]
+    lane = iota((1, rows), 1)
+    owner = lane // cap
+    limit = jnp.zeros((1, rows), jnp.int32)
+    for o in range(nmem):
+        limit = jnp.where(owner == o, counts[o], limit)
+    live = lane % cap < limit
+    token = code // (NR * NC)
+    row_cand = code // NC % NR
+    col_cand = code % NC
+    hit = iota((tokens, rows), 0) == token
+    hits[...] = jnp.where(hit, 1.0, 0.0).astype(BF16)
+    factors = jnp.concatenate([row_fac[...], col_fac[...]], axis=0)
+    found = jnp.dot(factors, jnp.where(hit, 1.0, 0.0), precision=HIGH, preferred_element_type=F32)
+    at = iota(found.shape, 0)
+    split = NR * RANK
+
+    def pick(place):
+        return jnp.sum(jnp.where(at == place, found, 0.0), axis=0, keepdims=True)
+
+    a0, a1 = pick(row_cand * RANK), pick(row_cand * RANK + 1)
+    b0, b1 = pick(split + col_cand * RANK), pick(split + col_cand * RANK + 1)
+    c00, c01, c10, c11 = core[0, 0], core[0, 1], core[1, 0], core[1, 1]
+    core_b0, core_b1 = c00 * b0 + c01 * b1, c10 * b0 + c11 * b1
+    core_a0, core_a1 = c00 * a0 + c10 * a1, c01 * a0 + c11 * a1
+    score = jnp.where(live, a0 * core_b0 + a1 * core_b1, 0.0)
+    even = at % RANK == 0
+    of_row = jnp.where(at // RANK == row_cand, jnp.where(even, core_b0, core_b1), 0.0)
+    of_col = jnp.where((at - split) // RANK == col_cand, jnp.where(even, core_a0, core_a1), 0.0)
+    scaled[...] = jnp.where(at < split, of_row, of_col)
+
+    field = iota((2 * RECORD, rows), 0) % RECORD
+    record = jnp.where(field == SCORE, score, 0.0)
+    record = jnp.where(field == ROW_HIGH, (local_row // KC).astype(F32), record)
+    record = jnp.where(field == ROW_LOW, (local_row % KC).astype(F32), record)
+    for k, outer in enumerate((a0 * b0, a0 * b1, a1 * b0, a1 * b1)):
+        top = outer.astype(BF16).astype(F32)
+        record = jnp.where(field == OUTER + k, top, record)
+        record = jnp.where(field == OUTER_REST + k, outer - top, record)
+    record = record.astype(BF16)
+
+    mine = rows // 2
+    part = mine // 2
+    q = iota((mine, rows), 0)
+    base = (q % part // half * 2 + q // part) * cap + q % half
+    pair_lane = iota((mine, rows), 1)
+
+    def order(which):
+        return jnp.where(pair_lane == base + which * half, 1.0, 0.0).astype(BF16)
+
+    first, second = dot_nt(order(0), record), dot_nt(order(1), record)
+    records = jnp.where(iota(first.shape, 1) < RECORD, first, second).astype(BF16)
+    live_hits = jnp.where(jnp.logical_and(hit, live), 1.0, 0.0).astype(BF16)
+    chosen = dot_nt(order(lax.axis_index("col")), live_hits).astype(BF16)
+    taken = jnp.dot(chosen, grads[...], preferred_element_type=F32).astype(BF16)
+    for z in range(far):
+        for x in range(2):
+            d = z * 2 + x
+            other = z * 2 + 1 - x
+            block = taken[x * part : (x + 1) * part]
+            send[d, :, 0:shard] = block[:, d * shard : (d + 1) * shard]
+            send[d, :, shard : 2 * shard] = block[:, other * shard : (other + 1) * shard]
+            send[d, :, 2 * shard :] = records[x * part : (x + 1) * part]
+
+
+def project_kernel(far, got, own, own_col, own_near, own_both, out):
+    nmem, part, wide = got.shape
+    shard = own.shape[2]
+    half = part // far
+    pairs = nmem * part
+    col = lax.axis_index("col")
+    x_own = got[:, :, 0:shard].reshape(pairs, shard)
+    x_near = got[:, :, shard : 2 * shard].reshape(pairs, shard)
+    record = got[:, :, 2 * shard :].reshape(pairs, 2 * RECORD).astype(F32)
+    low = jnp.where(iota(record.shape, 1) == col * RECORD + ROW_LOW, record, 0.0)
+    proj = jnp.sum(low, axis=1, keepdims=True).astype(jnp.int32) % E
+    for at, w_own, w_near in ((col, own, own_near), (1 - col, own_col, own_both)):
+        total = None
+        for e in range(E):
+            here = dot_nt(x_own, w_own[e]) + dot_nt(x_near, w_near[e])
+            total = here if total is None else jnp.where(proj == e, here, total)
+        total = total.reshape(nmem, far, half, total.shape[1])
+        for z in range(far):
+            out[z * 2 + at] = total[:, z].reshape(nmem * half, total.shape[3]).astype(BF16)
+
+
+def lookup_kernel(far, got, values, onehot, fetched, records):
+    nmem, part, wide = got.shape
+    half = part // far
+    z = lax.axis_index("far")
+    record = got[...].astype(F32).reshape(nmem, far, half, wide)
+    here = record[:, 0]
+    for k in range(1, far):
+        here = jnp.where(z == k, record[:, k], here)
+    here = here.reshape(nmem * half, wide)
+    both = jnp.concatenate([here, pltpu.roll(here, wide - RECORD, 1)], axis=0)
+    records[...] = both
+    row = (KC * both[:, ROW_HIGH : ROW_HIGH + 1] + both[:, ROW_LOW : ROW_LOW + 1]).astype(jnp.int32)
+    hot = jnp.where(iota(onehot.shape, 1) == row, 1.0, 0.0).astype(BF16)
+    onehot[...] = hot
+    fetched[...] = jnp.dot(hot, values[...], preferred_element_type=F32).astype(BF16)
+
+
+def reduce_kernel(far, parts, fetched, records, contrib, back):
+    nmem = 2 * far
+    rows = fetched.shape[0]
+    half = rows // nmem // 2
+    sums = []
+    for which in range(2):
+        total = parts[which].astype(F32)
+        for z in range(1, far):
+            total = total + parts[z * 2 + which].astype(F32)
+        sums.append(total)
+    pair_grad = jnp.concatenate(sums, axis=0).astype(BF16).astype(F32)
+    record = records[...]
+    contrib[...] = (record[:, SCORE : SCORE + 1] * pair_grad).astype(BF16)
+    dscore = jnp.sum(pair_grad * fetched[...].astype(F32), axis=1, keepdims=True)
+    me = lax.axis_index("far") * 2 + lax.axis_index("near")
+    q = iota(record.shape, 0)
+    place = me * (2 * half) + q // (rows // 2) * half + q % half
+    spread = jnp.where(iota(record.shape, 1) == place, dscore, 0.0)
+    spread = spread.reshape(2, nmem, half, record.shape[1])
+    spread = jnp.sum(spread[0] + spread[1], axis=1)
+    outer = jnp.sum(dscore * record, axis=0, keepdims=True)
+    line = iota((8, record.shape[1]), 0)
+    for s in range(nmem):
+        block = jnp.where(line == 0, spread[s : s + 1], jnp.where(line == 1, outer, 0.0))
+        back[2 * s] = block
+        back[2 * s + 1] = block
+
+
+def value_kernel(onehot, contrib, out):
+    out[...] = lax.dot_general(
+        onehot[...], contrib[...], (((0,), (0,)), ((), ())), preferred_element_type=F32
+    )
+
+
+def finish_kernel(back, scaled, hits, row_out, col_out, core_out):
+    total = jnp.sum(back[...], axis=0)
+    dscore = total[0:1]
+    outer = total[1:2]
+    grads = dot_nt(scaled[...] * dscore, hits[...].astype(F32), HIGH)
+    split = row_out.shape[0]
+    row_out[...] = grads[:split]
+    col_out[...] = grads[split:]
+    lane = iota(outer.shape, 1)
+    r, s = iota((RANK, RANK), 0), iota((RANK, RANK), 1)
+    result = jnp.zeros((RANK, RANK), F32)
+    for k in range(RANK * RANK):
+        mask = jnp.logical_or(lane == OUTER + k, lane == OUTER_REST + k)
+        value = jnp.sum(jnp.where(mask, outer, 0.0), axis=1, keepdims=True)
+        result = jnp.where(r * RANK + s == k, value, result)
+    core_out[...] = result
+
+
+VMEM = pl.BlockSpec(memory_space=pltpu.VMEM)
+SMEM = pl.BlockSpec(memory_space=pltpu.SMEM)
+
+
+def call(kernel, name, outs, ins, flops, moved, limit=24):
+    return pl.pallas_call(
+        kernel,
+        name=name,
+        out_shape=outs,
+        in_specs=ins,
+        out_specs=jax.tree.map(lambda _: VMEM, outs),
+        cost_estimate=pl.CostEstimate(flops=flops, bytes_accessed=moved, transcendentals=0),
+        compiler_params=pltpu.CompilerParams(vmem_limit_bytes=limit << 20),
+    )
+
+
+def shape(dims, kind):
+    return jax.ShapeDtypeStruct(dims, kind)
+
+
+def local_pairs(grads, values, expand_weight, row_factors, col_factors, core, pair_index, counts):
+    far = lax.axis_size("far")
+    nmem = 2 * far
+    tokens, depth = grads.shape
+    vrows, width = values.shape
+    rows = pair_index.shape[1]
+    shard = depth // nmem
+    swap = [(0, 1), (1, 0)]
+    own_near = lax.ppermute(expand_weight, "near", swap)
+    own_col = lax.ppermute(expand_weight, "col", swap)
+    own_both = lax.ppermute(own_near, "col", swap)
+    part = rows // 4
+    wide = 2 * shard + 2 * RECORD
+    send, scaled, hits = call(
+        functools.partial(prepare_kernel, far),
+        "prepare",
+        (
+            shape((nmem, part, wide), BF16),
+            shape((NR * RANK + NC * RANK, rows), F32),
+            shape((tokens, rows), BF16),
+        ),
+        [VMEM, SMEM, SMEM, VMEM, VMEM, VMEM],
+        rows * tokens * depth,
+        2 * tokens * depth,
+    )(pair_index, counts, core, row_factors.T, col_factors.T, grads)
+    got = lax.all_to_all(send, ("far", "near"), split_axis=0, concat_axis=0, tiled=True)
+    parts = call(
+        functools.partial(project_kernel, far),
+        "project",
+        shape((2 * far, rows // 2, width), BF16),
+        [VMEM] * 5,
+        4 * E * nmem * part * shard * width * 2,
+        8 * E * width * shard,
+    )(got, expand_weight, own_col, own_near, own_both)
+    parts = lax.all_to_all(parts, ("far", "col"), split_axis=0, concat_axis=0, tiled=True)
+    onehot, fetched, records = call(
+        functools.partial(lookup_kernel, far),
+        "lookup",
+        (
+            shape((rows, vrows), BF16),
+            shape((rows, width), BF16),
+            shape((rows, 2 * RECORD), F32),
+        ),
+        [VMEM, VMEM],
+        2 * rows * vrows * width,
+        2 * vrows * width,
+    )(got[:, :, 2 * shard :], values)
+    contrib, back = call(
+        functools.partial(reduce_kernel, far),
+        "reduce",
+        (shape((rows, width), BF16), shape((2 * nmem, 8, 2 * RECORD), F32)),
+        [VMEM] * 3,
+        8 * rows * width,
+        10 * rows * width,
+    )(parts, fetched, records)
+    back = lax.all_to_all(back, ("far", "near", "col"), split_axis=0, concat_axis=0, tiled=True)
+    value_grad = call(
+        value_kernel,
+        "value_rows",
+        shape((vrows, width), F32),
+        [VMEM] * 2,
+        2 * rows * vrows * width,
+        4 * vrows * width,
+    )(onehot, contrib)
+    row_grad, col_grad, core_grad = call(
+        finish_kernel,
+        "finish",
+        (
+            shape((NR * RANK, tokens), F32),
+            shape((NC * RANK, tokens), F32),
+            shape((RANK, RANK), F32),
+        ),
+        [VMEM] * 3,
+        2 * rows * tokens * 64,
+        8 * rows * tokens,
+    )(back, scaled, hits)
+    return value_grad, row_grad.T, col_grad.T, core_grad
+
+
 def solution(mesh):
-    return jax.shard_map(
-        local,
-        mesh=mesh,
-        in_specs=(
-            P(("group", "mem"), None),
-            P("mem", "col"),
-            P(None, "col", "mem"),
-            P(("group", "mem"), None),
-            P(("group", "mem"), None),
-            P(),
-            P(None, ("group", "mem")),
-            P(("group", "mem")),
-        ),
-        out_specs=(
-            P(("group", "mem"), "col"),
-            P(("group", "mem"), None),
-            P(("group", "mem"), None),
-            P("group", None),
-        ),
-        check_vma=False,
-    )
+    ngroup, nmem, ncol = (mesh.shape[a] for a in ("group", "mem", "col"))
+
+    def run(*args):
+        rows = args[6].shape[1] // (ngroup * nmem)
+        depth = args[0].shape[1]
+        fits = nmem % 2 == 0 and ncol == 2 and rows == 16 * nmem == 128
+        fits = fits and depth % (128 * nmem) == 0
+        if fits and nmem * rows <= E * depth:
+            used = Mesh(
+                mesh.devices.reshape(ngroup, nmem // 2, 2, ncol), ("group", "far", "near", "col")
+            )
+            mem, body = ("far", "near"), local_pairs
+        else:
+            used, mem, body = mesh, ("mem",), local_weights
+        both = ("group",) + mem
+        return jax.shard_map(
+            body,
+            mesh=used,
+            in_specs=(
+                P(both, None),
+                P(mem, "col"),
+                P(None, "col", mem),
+                P(both, None),
+                P(both, None),
+                P(),
+                P(None, both),
+                P(both),
+            ),
+            out_specs=(
+                P(both, "col"),
+                P(both, None),
+                P(both, None),
+                P("group", None),
+            ),
+            check_vma=False,
+        )(*args)
+
+    return run

time: 137 us -> 51.2 us (0.37)
  waiting for transfers between devices: 51.3 us -> 25.1 us
  blocking collectives: 24.8 us -> 0 us
  between operations: 14.2 us -> 0.69 us
  other arithmetic: 10.6 us -> 0 us
  local copies, waits for them, and re-layouts: 13.6 us -> 3.37 us
  Pallas kernels: 0 us -> 6.42 us
  matrix products: 5.08 us -> 0 us
  starting transfers between devices: 16.6 us -> 15.1 us
    all_gather x1 -> x0, waiting for transfers between devices: 50.6 us -> none  [local(): lax.all_gather(expand_weight, 'mem', axis=2, tiled=True)]
    psum x2 -> x0, blocking collectives: 24.8 us -> none  [the longest x1 22.3 us: local(): core_grad = lax.psum(core_part, 'mem')]
    all_to_all x3, waiting for transfers between devices: 0.01 us -> 23.1 us  [the longest x1 9.27 us: local_pairs(): lax.all_to_all(parts, ('far', 'col'), split_axis=0, concat_axis=0, tiled=...]
    pallas_call x0 -> x6, Pallas kernels: none -> 6.42 us  [the longest x1 1.96 us: local_pairs(): call(functools.partial(prepare_kernel, far), 'prepare', (shape((nmem, par...]
    gather x7 -> x0, local copies, waits for them, and re-layouts: 6.27 us -> none  [the longest x2 1.69 us: local(): live = within < counts[owner]]
    dot_general x5 -> x0, matrix products: 5.08 us -> none  [the longest x1 3.46 us: local(): jnp.einsum('tn,evn->tev', grads, lax.all_gather(expand_weight, 'mem', axi...]
    lt x1 -> x0, other arithmetic: 4.99 us -> none  [local(): live = within < counts[owner]]
    all_to_all x3, starting transfers between devices: 16.6 us -> 12.1 us  [the longest x1 5.01 us: local_pairs(): lax.all_to_all(send, ('far', 'near'), split_axis=0, concat_axis=0, tiled=...]
  transfers between devices with their start and end apart: 4 -> 6, of which waited for: 1 -> 4; matrix products, arithmetic and copies ran while one was open for 19% -> 0% of each run, Pallas kernels for 0% -> 7%
where the time goes in v1:
time: 51.2 us; the launch traced here: 50.7 us
  waiting for transfers between devices  25.1 us (49%)
  starting transfers between devices  15.1 us (29%)
  Pallas kernels  6.42 us (13%)
  local copies, waits for them, and re-layouts  3.37 us (7%)
  between operations  0.69 us (1%)
    all_to_all x1, waiting for transfers between devices, local_pairs(): lax.all_to_all(parts, ('far', 'col'), split_axis=0, concat_axis=0, tiled=...  9.27 us
    all_to_all x1, waiting for transfers between devices, local_pairs(): lax.all_to_all(send, ('far', 'near'), split_axis=0, concat_axis=0, tiled=...  7.95 us
    all_to_all x1, waiting for transfers between devices, local_pairs(): lax.all_to_all(back, ('far', 'near', 'col'), split_axis=0, concat_axis=0,...  5.84 us
    all_to_all x1, starting transfers between devices, local_pairs(): lax.all_to_all(send, ('far', 'near'), split_axis=0, concat_axis=0, tiled=...  5.01 us
    all_to_all x1, starting transfers between devices, local_pairs(): lax.all_to_all(parts, ('far', 'col'), split_axis=0, concat_axis=0, tiled=...  3.54 us
    all_to_all x1, starting transfers between devices, local_pairs(): lax.all_to_all(back, ('far', 'near', 'col'), split_axis=0, concat_axis=0,...  3.49 us
    unnamed x16, local copies, waits for them, and re-layouts  3.36 us
    ppermute x1, starting transfers between devices, local_pairs(): own_near = lax.ppermute(expand_weight, 'near', swap)  3 us
  transfers between devices with their start and end apart: 6, of which 4 were waited for; matrix products, arithmetic and copies ran while one was open for 0% of the time, Pallas kernels for 7%

profile of v1, /device:TPU:0, one launch (start us, length us, event | category | flops | bytes accessed | tf_op | source)
XLA Modules:
  0.0 50.7 jit_solution(4923591941193660477)
XLA Ops:
  0.6 3.0 %collective-permute-start.1 = (bf16[4,256,256]{2,1,0:T(8,128)(2,1)}, bf16[4,256,256]{2,1,0:T(8,128)(2,1)S(1)}, u32[]{:S(2)}, u32[]{:S(2)}) collective-permute-start(bf16[4,256,256]{2,1,0:T(8,128)(2,1)} %own.1), channel_id=1, source_target_pairs={{0,2},{2,0},{1,3},{3,1},{4,6},{6,4},{5,7},{7,5},{8,10},{10,8},{9,1... | collective-permute-start | bytes 1572872 | tf_op jit(solution)/shard_map/ppermute | solution.py:290
  3.6 0.0 copy-start.6
  3.6 0.0 copy-start.5
  3.6 0.0 copy-start.7
  3.6 0.7 %copy-done.6 = f32[2,2]{1,0:T(2,128)S(1)} copy-done((f32[2,2]{1,0:T(2,128)S(1)}, f32[2,2]{1,0:T(2,128)}, u32[]{:S(2)}) %copy-start.6) | copy-done | bytes 40
  4.3 0.0 copy-done.5
  4.3 0.0 copy-done.7
  4.3 0.0 copy-start
  4.3 1.2 %copy-done = bf16[256,2048]{1,0:T(8,128)(2,1)S(1)} copy-done((bf16[256,2048]{1,0:T(8,128)(2,1)S(1)}, bf16[256,2048]{1,0:T(8,128)(2,1)}, u32[]{:S(2)}) %copy-start) | copy-done | bytes 1048600
  5.6 0.0 copy-start.3
  5.6 0.7 %copy-done.3 = f32[256,16]{0,1:T(8,128)S(1)} copy-done((f32[256,16]{0,1:T(8,128)S(1)}, f32[256,16]{0,1:T(8,128)}, u32[]{:S(2)}) %copy-start.3) | copy-done | bytes 16408
  6.3 0.0 copy-start.4
  6.3 0.7 %copy-done.4 = f32[256,16]{0,1:T(8,128)S(1)} copy-done((f32[256,16]{0,1:T(8,128)S(1)}, f32[256,16]{0,1:T(8,128)}, u32[]{:S(2)}) %copy-start.4) | copy-done | bytes 16408
  7.0 2.0 %prepare.1 = (bf16[8,32,640]{2,1,0:T(8,128)(2,1)}, f32[32,128]{1,0:T(8,128)S(1)}, bf16[256,128]{1,0:T(8,128)(2,1)S(1)}) custom-call(s32[2,128]{1,0:T(2,128)S(1)} %copy-done.5, s32[8]{0:T(128)S(1)} %copy-done.7, f32[2,2]{1,0:T(2,128)S(1)} %copy-done.6, f32[16,256]{1,0:T(8,128)S(1)} %bitcast.4, f32[16,256]{1,0:T(8,128)S(1)} %bitcast.5, ...), custom_call_target="tpu_custom_call" | custom-call | flops 67108864 | bytes 1048576 | tf_op jit(solution)/shard_map/prepare/pallas_call | solution.py:295
  9.0 0.0 copy-start.1
  9.0 5.0 %all-to-all-start = ((bf16[8,32,640]{2,1,0:T(8,128)(2,1)}), bf16[8,32,640]{2,1,0:T(8,128)(2,1)S(1)}, u32[]{:S(2)}, u32[]{:S(2)}) async-start(bf16[8,32,640]{2,1,0:T(8,128)(2,1)} %get-tuple-element.15), calls=%async_computation | async-start | bytes 655360 | tf_op jit(solution)/shard_map/all_to_all | solution.py:307
  14.0 0.0 copy-done.1
  14.0 0.1 collective-permute-start
  14.1 2.0 %collective-permute-done.1.own_near = bf16[4,256,256]{2,1,0:T(8,128)(2,1)S(1)} collective-permute-done((bf16[4,256,256]{2,1,0:T(8,128)(2,1)}, bf16[4,256,256]{2,1,0:T(8,128)(2,1)S(1)}, u32[]{:S(2)}, u32[]{:S(2)}) %collective-permute-start.1) | collective-permute-done | bytes 524320 | tf_op jit(solution)/shard_map/ppermute | solution.py:290
  16.0 0.0 collective-permute-start.2
  16.0 0.0 collective-permute-done.own_col
  16.1 8.0 %all-to-all-done.got = bf16[8,32,640]{2,1,0:T(8,128)(2,1)S(1)} async-done(((bf16[8,32,640]{2,1,0:T(8,128)(2,1)}), bf16[8,32,640]{2,1,0:T(8,128)(2,1)S(1)}, u32[]{:S(2)}, u32[]{:S(2)}) %all-to-all-start) | async-done | bytes 327712 | tf_op jit(solution)/shard_map/all_to_all | solution.py:307
  24.0 0.0 collective-permute-done.2.own_both
  24.0 1.4 %project.1 = bf16[8,64,256]{2,1,0:T(8,128)(2,1)} custom-call(bf16[8,32,640]{2,1,0:T(8,128)(2,1)S(1)} %all-to-all-done.got, bf16[4,256,256]{2,1,0:T(8,128)(2,1)S(1)} %copy-done.1, bf16[4,256,256]{2,1,0:T(8,128)(2,1)S(1)} %collective-permute-done.own_col, bf16[4,256,256]{2,1,0:T(8,128)(2,1)S(1)} %collective-permute-done.1.own_near, ...), custom_call_target="tpu_custom_call" | custom-call | flops 536870912 | bytes 2097152 | tf_op jit(solution)/shard_map/project/pallas_call | solution.py:308
  25.5 0.0 copy-start.2
  25.5 3.5 %all-to-all-start.1 = ((bf16[8,64,256]{2,1,0:T(8,128)(2,1)}), bf16[8,64,256]{2,1,0:T(8,128)(2,1)S(1)}, u32[]{:S(2)}, u32[]{:S(2)}) async-start(bf16[8,64,256]{2,1,0:T(8,128)(2,1)} %project.1), calls=%async_computation.1 | async-start | bytes 524288 | tf_op jit(solution)/shard_map/all_to_all | solution.py:316
  29.0 0.0 copy-done.2
  29.0 0.4 lookup.1
  29.4 9.3 %all-to-all-done.1.parts = bf16[8,64,256]{2,1,0:T(8,128)(2,1)S(1)} async-done(((bf16[8,64,256]{2,1,0:T(8,128)(2,1)}), bf16[8,64,256]{2,1,0:T(8,128)(2,1)S(1)}, u32[]{:S(2)}, u32[]{:S(2)}) %all-to-all-start.1) | async-done | bytes 262176 | tf_op jit(solution)/shard_map/all_to_all | solution.py:316
  38.7 0.8 %reduce.1 = (bf16[128,256]{1,0:T(8,128)(2,1)S(1)}, f32[16,8,128]{2,1,0:T(8,128)}) custom-call(bf16[8,64,256]{2,1,0:T(8,128)(2,1)S(1)} %all-to-all-done.1.parts, bf16[128,256]{1,0:T(8,128)(2,1)S(1)} %get-tuple-element.17.fetched, f32[128,128]{1,0:T(8,128)S(1)} %get-tuple-element.18.records), custom_call_target="tpu_custom_call" | custom-call | flops 262144 | bytes 327680 | tf_op jit(solution)/shard_map/reduce/pallas_call | solution.py:329
  39.4 3.5 %all-to-all-start.2 = ((f32[16,8,128]{2,1,0:T(8,128)}), f32[16,8,128]{2,1,0:T(8,128)S(1)}, u32[]{:S(2)}, u32[]{:S(2)}) async-start(f32[16,8,128]{2,1,0:T(8,128)} %get-tuple-element.20), calls=%async_computation.2 | async-start | bytes 131072 | tf_op jit(solution)/shard_map/all_to_all | solution.py:337
  42.9 1.0 %value_rows.1 = f32[512,256]{1,0:T(8,128)} custom-call(bf16[128,512]{1,0:T(8,128)(2,1)S(1)} %get-tuple-element.16.onehot, bf16[128,256]{1,0:T(8,128)(2,1)S(1)} %get-tuple-element.19.contrib), custom_call_target="tpu_custom_call" | custom-call | flops 33554432 | bytes 524288 | tf_op jit(solution)/shard_map/value_rows/pallas_call | solution.py:338
  44.0 5.8 %all-to-all-done.2.back = f32[16,8,128]{2,1,0:T(8,128)S(1)} async-done(((f32[16,8,128]{2,1,0:T(8,128)}), f32[16,8,128]{2,1,0:T(8,128)S(1)}, u32[]{:S(2)}, u32[]{:S(2)}) %all-to-all-start.2) | async-done | bytes 65568 | tf_op jit(solution)/shard_map/all_to_all | solution.py:337
  49.8 0.8 %finish.1 = (f32[16,256]{1,0:T(8,128)}, f32[16,256]{1,0:T(8,128)}, f32[2,2]{1,0:T(2,128)}) custom-call(f32[16,8,128]{2,1,0:T(8,128)S(1)} %all-to-all-done.2.back, f32[32,128]{1,0:T(8,128)S(1)} %get-tuple-element.21.scaled, bf16[256,128]{1,0:T(8,128)(2,1)S(1)} %get-tuple-element.22.hits), custom_call_target="tpu_custom_call" | custom-call | flops 4194304 | bytes 262144 | tf_op jit(solution)/shard_map/finish/pallas_call | solution.py:346
  (1 shorter events, 0.0 us)
Async XLA Ops:
  0.6 15.4 %collective-permute-start.1 = (bf16[4,256,256]{2,1,0:T(8,128)(2,1)}, bf16[4,256,256]{2,1,0:T(8,128)(2,1)S(1)}, u32[]{:S(2)}, u32[]{:S(2)}) collective-permute-start(bf16[4,256,256]{2,1,0:T(8,128)(2,1)} %own.1), channel_id=1, source_target_pairs={{0,2},{2,0},{1,3},{3,1},{4,6},{6,4},{5,7},{7,5},{8,10},{10,8},{9,1... | collective-permute-start | bytes 1572872 | tf_op jit(solution)/shard_map/ppermute | solution.py:290
  3.6 0.7 %copy-start.6 = (f32[2,2]{1,0:T(2,128)S(1)}, f32[2,2]{1,0:T(2,128)}, u32[]{:S(2)}) copy-start(f32[2,2]{1,0:T(2,128)} %core.1) | copy-start | bytes 52
  3.6 0.7 %copy-start.5 = (s32[2,128]{1,0:T(2,128)S(1)}, s32[2,128]{1,0:T(2,128)}, u32[]{:S(2)}) copy-start(s32[2,128]{1,0:T(2,128)} %pair.1) | copy-start | bytes 3076
  3.6 0.7 %copy-start.7 = (s32[8]{0:T(128)S(1)}, s32[8]{0:T(128)}, u32[]{:S(2)}) copy-start(s32[8]{0:T(128)} %counts.1) | copy-start | bytes 100
  4.3 1.2 %copy-start = (bf16[256,2048]{1,0:T(8,128)(2,1)S(1)}, bf16[256,2048]{1,0:T(8,128)(2,1)}, u32[]{:S(2)}) copy-start(bf16[256,2048]{1,0:T(8,128)(2,1)} %grads.1) | copy-start | bytes 3145732
  5.6 0.7 %copy-start.3 = (f32[256,16]{0,1:T(8,128)S(1)}, f32[256,16]{0,1:T(8,128)}, u32[]{:S(2)}) copy-start(f32[256,16]{0,1:T(8,128)} %param.11) | copy-start | bytes 49156
  6.3 0.7 %copy-start.4 = (f32[256,16]{0,1:T(8,128)S(1)}, f32[256,16]{0,1:T(8,128)}, u32[]{:S(2)}) copy-start(f32[256,16]{0,1:T(8,128)} %param.12) | copy-start | bytes 49156
  9.0 5.0 %copy-start.1 = (bf16[4,256,256]{2,1,0:T(8,128)(2,1)S(1)}, bf16[4,256,256]{2,1,0:T(8,128)(2,1)}, u32[]{:S(2)}) copy-start(bf16[4,256,256]{2,1,0:T(8,128)(2,1)} %own.1) | copy-start | bytes 1572868
  9.0 15.0 %all-to-all-start = ((bf16[8,32,640]{2,1,0:T(8,128)(2,1)}), bf16[8,32,640]{2,1,0:T(8,128)(2,1)S(1)}, u32[]{:S(2)}, u32[]{:S(2)}) async-start(bf16[8,32,640]{2,1,0:T(8,128)(2,1)} %get-tuple-element.15), calls=%async_computation | async-start | bytes 655360 | tf_op jit(solution)/shard_map/all_to_all | solution.py:307
  14.0 2.1 %collective-permute-start = (bf16[4,256,256]{2,1,0:T(8,128)(2,1)S(1)}, bf16[4,256,256]{2,1,0:T(8,128)(2,1)S(1)}, u32[]{:S(2)}, u32[]{:S(2)}) collective-permute-start(bf16[4,256,256]{2,1,0:T(8,128)(2,1)S(1)} %copy-done.1), channel_id=1, source_target_pairs={{0,1},{1,0},{2,3},{3,2},{4,5},{5,4},{6,7},{7,6},{8,9},{9,8},{10,11... | collective-permute-start | bytes 1572872 | tf_op jit(solution)/shard_map/ppermute | solution.py:291
  16.0 8.0 %collective-permute-start.2 = (bf16[4,256,256]{2,1,0:T(8,128)(2,1)S(1)}, bf16[4,256,256]{2,1,0:T(8,128)(2,1)S(1)}, u32[]{:S(2)}, u32[]{:S(2)}) collective-permute-start(bf16[4,256,256]{2,1,0:T(8,128)(2,1)S(1)} %collective-permute-done.1.own_near), channel_id=1, source_target_pairs={{0,1},{1,0},{2,3},{3,2},{4,5},{5,4},{6,7},{7,6},{8,9},{9,8},{10,11... | collective-permute-start | bytes 1572872 | tf_op jit(solution)/shard_map/ppermute | solution.py:292
  25.5 3.6 %copy-start.2 = (bf16[512,256]{1,0:T(8,128)(2,1)S(1)}, bf16[512,256]{1,0:T(8,128)(2,1)}, u32[]{:S(2)}) copy-start(bf16[512,256]{1,0:T(8,128)(2,1)} %values.1) | copy-start | bytes 786436
  25.5 13.2 %all-to-all-start.1 = ((bf16[8,64,256]{2,1,0:T(8,128)(2,1)}), bf16[8,64,256]{2,1,0:T(8,128)(2,1)S(1)}, u32[]{:S(2)}, u32[]{:S(2)}) async-start(bf16[8,64,256]{2,1,0:T(8,128)(2,1)} %project.1), calls=%async_computation.1 | async-start | bytes 524288 | tf_op jit(solution)/shard_map/all_to_all | solution.py:316
  39.4 10.4 %all-to-all-start.2 = ((f32[16,8,128]{2,1,0:T(8,128)}), f32[16,8,128]{2,1,0:T(8,128)S(1)}, u32[]{:S(2)}, u32[]{:S(2)}) async-start(f32[16,8,128]{2,1,0:T(8,128)} %get-tuple-element.20), calls=%async_computation.2 | async-start | bytes 131072 | tf_op jit(solution)/shard_map/all_to_all | solution.py:337

commit v2 on v1

v2 whole, which is shorter than its diff:
```python
import functools
import math

import jax
import jax.numpy as jnp
from jax import lax
from jax.experimental import pallas as pl
from jax.experimental.pallas import tpu as pltpu
from jax.sharding import Mesh
from jax.sharding import PartitionSpec as P

E = 4
RANK = 2
NR = 8
NC = 8
KC = 64
F32 = jnp.float32
BF16 = jnp.bfloat16

SCORE, ROW_HIGH, ROW_LOW, OUTER, OUTER_REST = 0, 1, 2, 4, 12
RECORD = 16
FULL = 32000.0


def local_weights(grads, values, expand_weight, row_factors, col_factors, core, pair_index, counts):
    nmem = lax.axis_size("mem")
    tokens = grads.shape[0]
    width = values.shape[1]
    vrows = values.shape[0]
    rows = pair_index.shape[1]
    cap = rows // nmem
    high = lax.Precision.HIGHEST
    expanded = jnp.einsum(
        "tn,evn->tev",
        grads,
        lax.all_gather(expand_weight, "mem", axis=2, tiled=True),
        preferred_element_type=jnp.float32,
    ).astype(jnp.bfloat16)
    code = pair_index[0]
    local_row = pair_index[1]
    within = jnp.tile(jnp.arange(cap, dtype=jnp.int32), nmem)
    owner = jnp.repeat(jnp.arange(nmem, dtype=jnp.int32), cap)
    live = within < counts[owner]
    token = code // (NR * NC)
    row_cand = code // NC % NR
    col_cand = code % NC
    a_p = row_factors.reshape(tokens, NR, RANK)[token, row_cand]
    b_p = col_factors.reshape(tokens, NC, RANK)[token, col_cand]
    core_b = jnp.dot(b_p, core.T, precision=high)
    core_a = jnp.dot(a_p, core, precision=high)
    score = jnp.where(live, jnp.sum(a_p * core_b, -1), 0.0).astype(jnp.bfloat16)
    proj = local_row % KC % E
    pair_grad = jnp.where(live[:, None], expanded[token, proj], jnp.zeros((), jnp.bfloat16))
    got_row = lax.all_to_all(
        local_row.reshape(nmem, cap), "mem", split_axis=0, concat_axis=0, tiled=True
    ).reshape(rows)
    fetched = lax.all_to_all(
        values[got_row].reshape(nmem, cap, width), "mem", split_axis=0, concat_axis=0, tiled=True
    ).reshape(rows, width)
    own_contrib = (score.astype(jnp.float32)[:, None] * pair_grad.astype(jnp.float32)).astype(
        jnp.bfloat16
    )
    contrib = lax.all_to_all(
        own_contrib.reshape(nmem, cap, width), "mem", split_axis=0, concat_axis=0, tiled=True
    ).reshape(rows, width)
    dscore = jnp.einsum("pv,pv->p", pair_grad, fetched, preferred_element_type=jnp.float32)
    block = min(2048, rows)

    def add_block(step, total):
        onehot = (jnp.arange(vrows, dtype=jnp.int32)[:, None] == got_row[None, :]).astype(
            jnp.bfloat16
        )
        return total + jnp.dot(onehot, contrib, preferred_element_type=jnp.float32)

    value_grad = lax.fori_loop(0, rows // block, add_block, jnp.zeros((vrows, width), jnp.float32))
    dscore = lax.psum(dscore, "col")
    row_grad = jax.ops.segment_sum(
        dscore[:, None] * core_b, token * NR + row_cand, num_segments=tokens * NR
    )
    col_grad = jax.ops.segment_sum(
        dscore[:, None] * core_a, token * NC + col_cand, num_segments=tokens * NC
    )
    row_grad = row_grad.reshape(tokens, NR * RANK)
    col_grad = col_grad.reshape(tokens, NC * RANK)
    core_part = jnp.dot((dscore[:, None] * a_p).T, b_p, precision=high)
    core_grad = lax.psum(core_part, "mem")
    return (value_grad, row_grad, col_grad, core_grad)


def iota(shape, dim):
    return lax.broadcasted_iota(jnp.int32, shape, dim)


def dot_nn(x, y):
    return jnp.dot(x, y, preferred_element_type=F32)


def dot_nt(x, y):
    return lax.dot_general(x, y, (((1,), (1,)), ((), ())), preferred_element_type=F32)


def thirds(x):
    first = x.astype(BF16)
    rest = x - first.astype(F32)
    second = rest.astype(BF16)
    third = (rest - second.astype(F32)).astype(BF16)
    return jnp.concatenate([first, second, third], axis=0)


def add_thirds(y):
    n = y.shape[0] // 3
    return (y[2 * n :] + y[n : 2 * n]) + y[:n]


def place():
    return lax.axis_index("far"), lax.axis_index("near"), lax.axis_index("col")


def prepare_kernel(
    far, pair_hbm, counts_hbm, core_hbm, row_hbm, col_hbm, grads_hbm, *refs
):
    sends, (scaled, hits), (pair, counts, core, row_fac, col_fac, grads, sems) = (
        refs[:far],
        refs[far : far + 2],
        refs[far + 2 :],
    )
    sources = (pair_hbm, counts_hbm, core_hbm, row_hbm, col_hbm, grads_hbm)
    targets = (pair, counts, core, row_fac, col_fac, grads)
    copies = [
        pltpu.make_async_copy(source, target, sems.at[k])
        for k, (source, target) in enumerate(zip(sources, targets))
    ]
    for copy in copies:
        copy.start()
    for copy in copies[:-1]:
        copy.wait()
    z, x, c = place()
    nmem = 2 * far
    rows = pair.shape[1]
    cap = rows // nmem
    half = cap // 2
    tokens, depth = grads.shape
    shard = depth // nmem
    code = pair[0:1, :]
    local_row = pair[1:2, :]
    lane = iota((1, rows), 1)
    owner = lane // cap
    limit = jnp.zeros((1, rows), jnp.int32)
    for o in range(nmem):
        limit = jnp.where(owner == o, counts[0:1, o : o + 1], limit)
    live = lane % cap < limit
    token = code // (NR * NC)
    row_cand = code // NC % NR
    col_cand = code % NC
    hit = iota((tokens, rows), 0) == token
    hot = jnp.where(hit, 1.0, 0.0).astype(BF16)
    hits[...] = hot
    factors = jnp.concatenate([row_fac[...], col_fac[...]], axis=0)
    found = add_thirds(dot_nn(thirds(factors), hot))
    at = iota(found.shape, 0)
    split = NR * RANK

    def pick(row):
        return jnp.sum(jnp.where(at == row, found, 0.0), axis=0, keepdims=True)

    a0, a1 = pick(row_cand * RANK), pick(row_cand * RANK + 1)
    b0, b1 = pick(split + col_cand * RANK), pick(split + col_cand * RANK + 1)
    c00, c01, c10, c11 = core[0:1, 0:1], core[0:1, 1:2], core[1:2, 0:1], core[1:2, 1:2]
    core_b0, core_b1 = c00 * b0 + c01 * b1, c10 * b0 + c11 * b1
    core_a0, core_a1 = c00 * a0 + c10 * a1, c01 * a0 + c11 * a1
    score = jnp.where(live, a0 * core_b0 + a1 * core_b1, 0.0)
    even = at % RANK == 0
    of_row = jnp.where(at // RANK == row_cand, jnp.where(even, core_b0, core_b1), 0.0)
    of_col = jnp.where((at - split) // RANK == col_cand, jnp.where(even, core_a0, core_a1), 0.0)
    scaled[...] = jnp.where(at < split, of_row, of_col)

    field = iota((RECORD, rows), 0)
    record = jnp.where(field == SCORE, score, 0.0)
    record = jnp.where(field == ROW_HIGH, (local_row // KC).astype(F32), record)
    record = jnp.where(field == ROW_LOW, (local_row % KC).astype(F32), record)
    for k, outer in enumerate((a0 * b0, a0 * b1, a1 * b0, a1 * b1)):
        top = outer.astype(BF16).astype(F32)
        record = jnp.where(field == OUTER + k, top, record)
        record = jnp.where(field == OUTER_REST + k, outer - top, record)

    to = iota((rows, rows), 1)
    to_m, to_y = to // (2 * cap), to // cap % 2
    to_pair = ((to_m ^ z) * 2 + (to_y ^ x)) * cap + (to // half % 2 ^ c) * half + to % half
    order = jnp.where(iota((rows, rows), 0) == to_pair, 1.0, 0.0).astype(BF16)
    records = dot_nn(record.astype(BF16), order).astype(BF16)

    mine = rows // 2
    q = iota((mine, rows), 0)
    q_pair = ((q // cap ^ z) * 2 + (q // half % 2 ^ x)) * cap + c * half + q % half
    take = jnp.where(iota((mine, rows), 1) == q_pair, 1.0, 0.0).astype(BF16)
    live_hits = jnp.where(jnp.logical_and(hit, live), 1.0, 0.0).astype(BF16)
    chosen = dot_nt(take, live_hits).astype(BF16)
    copies[-1].wait()
    for k in range(far):
        blocks = []
        for y in range(2):
            start = pl.multiple_of(((z ^ k) * 2 + (x ^ y)) * shard, shard)
            taken = dot_nn(chosen, grads[:, pl.ds(start, shard)]).astype(BF16)
            blocks += [taken[:, :128], taken[:, 128:]]
        sends[k][...] = jnp.concatenate(blocks + [records], axis=0)


def project_kernel(far, *refs):
    ours, theirs = refs[:far], refs[far : 2 * far]
    own, near = refs[2 * far : 2 * far + 2]
    whole, coded = refs[2 * far + 2], refs[2 * far + 3 :]
    mine = (ours[0].shape[0] - RECORD) // 4
    cap = mine // far // 2 * 2
    half = cap // 2
    rows = 2 * mine
    lane, line = iota((rows, rows), 1), iota((rows, rows), 0)
    mask = line % mine // half * cap + line // mine * half + line % half == lane
    firsts, seconds, projs = [], [], []
    for k in range(far):
        for block in (ours[k], theirs[k]):
            firsts.append(jnp.concatenate([block[0:mine], block[mine : 2 * mine]], axis=1))
            seconds.append(
                jnp.concatenate([block[2 * mine : 3 * mine], block[3 * mine : 4 * mine]], axis=1)
            )
        record = ours[k][4 * mine : 4 * mine + RECORD].astype(F32)
        low = jnp.where(mask, record[ROW_LOW : ROW_LOW + 1], 0.0)
        projs.append(jnp.sum(low, axis=1, keepdims=True))
    first, second = jnp.concatenate(firsts, axis=0), jnp.concatenate(seconds, axis=0)
    proj = jnp.concatenate(projs, axis=0).astype(jnp.int32) % E
    total = None
    for e in range(E):
        here = dot_nt(first, own[e]) + dot_nt(second, near[e])
        total = here if total is None else jnp.where(proj == e, here, total)

    def rows_for(j):
        pieces = []
        for y in range(2):
            for n in range(far):
                for g in range(2):
                    start = (j ^ n) * rows + g * mine + n * cap + y * half
                    pieces.append(total[start : start + half])
        return jnp.concatenate(pieces, axis=0)

    whole[...] = rows_for(0)
    diagonal = line == lane
    for j in range(1, far):
        part = rows_for(j)
        top = jnp.max(jnp.abs(part), axis=1, keepdims=True)
        power = jnp.floor(jnp.log(jnp.maximum(top, 2.0**-100)) * (1 / math.log(2))) + 1.0
        level = jnp.abs(part) * jnp.exp2(-power)
        root = level * lax.rsqrt(jnp.maximum(level, 1e-30)) * FULL
        code = jnp.floor(jnp.where(part < 0, -root, root) + 0.5)
        powers = jnp.sum(jnp.where(diagonal, power, 0.0), axis=0, keepdims=True)
        powers = jnp.broadcast_to(powers, (RECORD, rows))
        block = jnp.concatenate([code[:, :128], code[:, 128:], powers], axis=0)
        coded[j - 1][...] = block.astype(jnp.int32).astype(jnp.int16)


def lookup_kernel(far, *refs):
    blocks, (values, near_values), (fetched, records, value_rows) = (
        refs[:far],
        refs[far : far + 2],
        refs[far + 2 :],
    )
    rows = records.shape[0]
    group = rows // far
    lane, line = iota((rows, rows), 1), iota((rows, rows), 0)
    total = jnp.zeros((RECORD, rows), F32)
    for n in range(far):
        tile = blocks[n][2 * rows : 2 * rows + RECORD]
        source = n * group + lane // (rows // 2) * (group // 2) + lane % (group // 2)
        inside = lane // (group // 2) % far == n
        move = jnp.where(jnp.logical_and(line == source, inside), 1.0, 0.0).astype(BF16)
        total = total + dot_nn(tile, move)
    value_row = KC * total[ROW_HIGH : ROW_HIGH + 1] + total[ROW_LOW : ROW_LOW + 1]
    value_rows[...] = jnp.broadcast_to(value_row, value_rows.shape)
    padded = jnp.concatenate([total, jnp.zeros((rows - RECORD, rows), F32)], axis=0).astype(BF16)
    column = dot_nt(jnp.where(line == lane, 1.0, 0.0).astype(BF16), padded)
    records[...] = column
    row = KC * column[:, ROW_HIGH : ROW_HIGH + 1] + column[:, ROW_LOW : ROW_LOW + 1]
    hot = iota((rows, values.shape[0]), 1) == row.astype(jnp.int32)
    hot = jnp.where(hot, 1.0, 0.0).astype(BF16)
    fetched[: rows // 2] = dot_nn(hot[: rows // 2], values[...])
    fetched[rows // 2 :] = dot_nn(hot[rows // 2 :], near_values[...])


def reduce_kernel(far, *refs):
    (whole, fetched, records, value_rows), coded, (contrib, pass_on, back) = (
        refs[:4],
        refs[4 : 3 + far],
        refs[3 + far :],
    )
    z, x, c = place()
    rows, width = whole.shape
    half = rows // far // 4
    line, lane = iota((rows, rows), 0), iota((rows, rows), 1)
    diagonal = line == lane
    total = whole[...]
    for block in coded:
        code = block[...].astype(jnp.int32).astype(F32)
        power = jnp.where(diagonal, code[2 * rows : 2 * rows + 1], 0.0)
        scale = jnp.exp2(jnp.sum(power, axis=1, keepdims=True)) * (1 / FULL**2)
        value = jnp.concatenate([code[:rows], code[rows : 2 * rows]], axis=1)
        total = total + value * jnp.abs(value) * scale
    pair_grad = total.astype(BF16).astype(F32)
    record = records[...]
    share = record[:, SCORE : SCORE + 1] * pair_grad
    contrib[...] = share[: rows // 2].astype(BF16)
    send = value_rows[0:1]
    send_high = jnp.floor(send * (1 / KC))
    tile = iota((RECORD, width), 0)
    spare = jnp.zeros((1, width - rows), F32)
    high_row = jnp.concatenate([send_high, spare], axis=1)
    low_row = jnp.concatenate([send - KC * send_high, spare], axis=1)
    tail = jnp.where(tile == 0, high_row, jnp.where(tile == 1, low_row, 0.0))
    pass_on[...] = jnp.concatenate([share[rows // 2 :], tail], axis=0).astype(BF16)
    dscore = jnp.sum(pair_grad * fetched[...], axis=1, keepdims=True)
    owner = z * 2 + (line // (rows // 2) ^ x)
    target = owner * (2 * half) + (line // half % 2 ^ c) * half + line % half
    spread = jnp.where(lane == target, dscore, 0.0).reshape(2, far, 2 * half, rows)
    spread = jnp.sum(spread[0] + spread[1], axis=1)
    outer = jnp.sum(dscore * record, axis=0, keepdims=True)
    empty = jnp.zeros((7 - far, rows), F32)
    block = jnp.concatenate([spread, outer, empty], axis=0)
    for k in range(back.shape[0]):
        back[k] = block


def value_kernel(contrib, passed, value_rows, out):
    half = contrib.shape[0]
    rows = 2 * half
    tail = passed[half : half + RECORD].astype(F32)
    lane = iota((1, rows), 1)
    other = (KC * tail[0:1] + tail[1:2])[:, :rows]
    row = jnp.where(lane < half, value_rows[0:1], other).astype(jnp.int32)
    hot = jnp.where(iota((out.shape[0], rows), 0) == row, 1.0, 0.0).astype(BF16)
    out[...] = dot_nn(hot, jnp.concatenate([contrib[...], passed[:half]], axis=0))


def finish_kernel(far, back, scaled, hits, row_out, col_out, core_out):
    z, x, _ = place()
    line = iota(back.shape[1:], 0)
    total = jnp.zeros(back.shape[1:], F32)
    for k in range(back.shape[0]):
        mine = jnp.logical_and(line == (k // 4 ^ z), k // 2 % 2 == x)
        total = total + jnp.where(jnp.logical_or(mine, line == far), back[k], 0.0)
    dscore = jnp.sum(total[:far], axis=0, keepdims=True)
    outer = total[far : far + 1]
    grads = add_thirds(dot_nt(thirds(scaled[...] * dscore), hits[...]))
    split = row_out.shape[0]
    row_out[...] = grads[:split]
    col_out[...] = grads[split:]
    lane = iota(outer.shape, 1)
    r, s = iota((RANK, RANK), 0), iota((RANK, RANK), 1)
    result = jnp.zeros((RANK, RANK), F32)
    for k in range(RANK * RANK):
        mask = jnp.logical_or(lane == OUTER + k, lane == OUTER_REST + k)
        value = jnp.sum(jnp.where(mask, outer, 0.0), axis=1, keepdims=True)
        result = jnp.where(r * RANK + s == k, value, result)
    core_out[...] = result


VMEM = pl.BlockSpec(memory_space=pltpu.VMEM)
HBM = pl.BlockSpec(memory_space=pl.ANY)


def call(kernel, name, outs, ins, flops, moved, scratch=(), limit=24):
    return pl.pallas_call(
        kernel,
        name=name,
        out_shape=outs,
        in_specs=ins,
        out_specs=jax.tree.map(lambda _: VMEM, outs),
        scratch_shapes=scratch,
        cost_estimate=pl.CostEstimate(flops=flops, bytes_accessed=moved, transcendentals=0),
        compiler_params=pltpu.CompilerParams(vmem_limit_bytes=limit << 20),
    )


def shape(dims, kind):
    return jax.ShapeDtypeStruct(dims, kind)


def local_pairs(grads, values, expand_weight, row_factors, col_factors, core, pair_index, counts):
    far = lax.axis_size("far")
    nmem = 2 * far
    tokens, depth = grads.shape
    vrows, width = values.shape
    rows = pair_index.shape[1]
    factors = NR * RANK + NC * RANK
    swap = [(0, 1), (1, 0)]

    def along_far(block, k):
        return lax.ppermute(block, "far", [(i, i ^ k) for i in range(far)])

    near_weight = lax.ppermute(expand_weight, "near", swap)
    block = shape((2 * rows + RECORD, 128), BF16)
    *sends, scaled, hits = call(
        functools.partial(prepare_kernel, far),
        "prepare",
        (block,) * far + (shape((factors, rows), F32), shape((tokens, rows), BF16)),
        [HBM] * 6,
        rows * tokens * depth,
        2 * tokens * depth,
        (
            pltpu.VMEM((2, rows), jnp.int32),
            pltpu.VMEM((1, nmem), jnp.int32),
            pltpu.VMEM((RANK, RANK), F32),
            pltpu.VMEM((NR * RANK, tokens), F32),
            pltpu.VMEM((NC * RANK, tokens), F32),
            pltpu.VMEM((tokens, depth), BF16),
            pltpu.SemaphoreType.DMA((6,)),
        ),
    )(pair_index, counts.reshape(1, nmem), core, row_factors.T, col_factors.T, grads)
    ours = [sends[0]] + [along_far(sends[k], k) for k in range(1, far)]
    theirs = [lax.ppermute(got, "col", swap) for got in ours]
    near_values = lax.ppermute(values, "near", swap)
    code = shape((2 * rows + RECORD, 128), jnp.int16)
    whole, *coded = call(
        functools.partial(project_kernel, far),
        "project",
        (shape((rows, width), F32),) + (code,) * (far - 1),
        [VMEM] * (2 * far + 2),
        4 * E * far * rows * depth // far * width,
        8 * E * width * depth // nmem,
    )(*ours, *theirs, expand_weight, near_weight)
    coded = [along_far(coded[j - 1], j) for j in range(1, far)]
    fetched, records, value_rows = call(
        functools.partial(lookup_kernel, far),
        "lookup",
        (shape((rows, width), F32), shape((rows, rows), F32), shape((8, rows), F32)),
        [VMEM] * (far + 2),
        2 * rows * vrows * width,
        4 * vrows * width,
    )(*ours, values, near_values)
    contrib, pass_on, back = call(
        functools.partial(reduce_kernel, far),
        "reduce",
        (
            shape((rows // 2, width), BF16),
            shape((rows // 2 + RECORD, width), BF16),
            shape((2 * nmem, 8, rows), F32),
        ),
        [VMEM] * (3 + far),
        8 * rows * width,
        10 * rows * width,
    )(whole, fetched, records, value_rows, *coded)
    back = lax.all_to_all(back, ("far", "near", "col"), split_axis=0, concat_axis=0, tiled=True)
    passed = lax.ppermute(pass_on, "near", swap)
    value_grad = call(
        value_kernel,
        "value_rows",
        shape((vrows, width), F32),
        [VMEM] * 3,
        2 * rows * vrows * width,
        4 * vrows * width,
    )(contrib, passed, value_rows)
    row_grad, col_grad, core_grad = call(
        functools.partial(finish_kernel, far),
        "finish",
        (
            shape((NR * RANK, tokens), F32),
            shape((NC * RANK, tokens), F32),
            shape((RANK, RANK), F32),
        ),
        [VMEM] * 3,
        2 * rows * tokens * 96,
        4 * rows * tokens,
    )(back, scaled, hits)
    return value_grad, row_grad.T, col_grad.T, core_grad


def solution(mesh):
    ngroup, nmem, ncol = (mesh.shape[a] for a in ("group", "mem", "col"))

    def run(*args):
        rows = args[6].shape[1] // (ngroup * nmem)
        depth = args[0].shape[1]
        fits = nmem % 2 == 0 and ncol == 2 and rows == 16 * nmem == 128
        fits = fits and depth == 256 * nmem and args[1].shape[1] == 256 * ncol
        if fits and nmem * rows <= E * depth:
            used = Mesh(
                mesh.devices.reshape(ngroup, nmem // 2, 2, ncol), ("group", "far", "near", "col")
            )
            mem, body = ("far", "near"), local_pairs
        else:
            used, mem, body = mesh, ("mem",), local_weights
        both = ("group",) + mem
        return jax.shard_map(
            body,
            mesh=used,
            in_specs=(
                P(both, None),
                P(mem, "col"),
                P(None, "col", mem),
                P(both, None),
                P(both, None),
                P(),
                P(None, both),
                P(both),
            ),
            out_specs=(
                P(both, "col"),
                P(both, None),
                P(both, None),
                P("group", None),
            ),
            check_vma=False,
        )(*args)

    return run
```

time: 51.2 us -> 42.5 us (0.83)
  waiting for transfers between devices: 25.1 us -> 15.3 us
  starting transfers between devices: 15.1 us -> 17.5 us
  Pallas kernels: 6.42 us -> 5.19 us
    all_to_all x2 -> x0, waiting for transfers between devices: 17.2 us -> none  [the longest x1 9.27 us: local_pairs(): lax.all_to_all(parts, ('far', 'col'), split_axis=0, concat_axis=0, tiled=...]
    ppermute x3 -> x13, waiting for transfers between devices: 2 us -> 13.7 us  [the longest x6 10.4 us: along_far(): return lax.ppermute(block, 'far', [(i, i ^ k) for i in range(far)])]
    ppermute x3 -> x13, starting transfers between devices: 3.08 us -> 13.8 us  [the longest x6 8.01 us: along_far(): return lax.ppermute(block, 'far', [(i, i ^ k) for i in range(far)])]
    all_to_all x2 -> x0, starting transfers between devices: 8.56 us -> none  [the longest x1 5.01 us: local_pairs(): lax.all_to_all(send, ('far', 'near'), split_axis=0, concat_axis=0, tiled=...]
    all_to_all x1, waiting for transfers between devices: 5.84 us -> 1.61 us  [local_pairs(): lax.all_to_all(back, ('far', 'near', 'col'), split_axis=0, concat_axis=0,...]
    pallas_call x6, Pallas kernels: 6.42 us -> 5.19 us  [the longest x1 1.06 us: local_pairs(): call(functools.partial(project_kernel, far), 'project', (shape((rows, wid...]
  transfers between devices with their start and end apart: 6 -> 14, of which waited for: 4 -> 9; matrix products, arithmetic and copies ran while one was open for 0% -> 0% of each run, Pallas kernels for 7% -> 8%
where the time goes in v2:
time: 42.5 us; the launch traced here: 42 us
  starting transfers between devices  17.5 us (41%)
  waiting for transfers between devices  15.3 us (36%)
  Pallas kernels  5.19 us (12%)
  local copies, waits for them, and re-layouts  3.36 us (8%)
  between operations  0.68 us (2%)
    ppermute x6, waiting for transfers between devices, along_far(): return lax.ppermute(block, 'far', [(i, i ^ k) for i in range(far)])  10.4 us
    ppermute x6, starting transfers between devices, along_far(): return lax.ppermute(block, 'far', [(i, i ^ k) for i in range(far)])  8.01 us
    all_to_all x1, starting transfers between devices, local_pairs(): lax.all_to_all(back, ('far', 'near', 'col'), split_axis=0, concat_axis=0,...  3.7 us
    unnamed x16, local copies, waits for them, and re-layouts  3.36 us
    ppermute x1, starting transfers between devices, local_pairs(): near_weight = lax.ppermute(expand_weight, 'near', swap)  3 us
    ppermute x1, waiting for transfers between devices, local_pairs(): passed = lax.ppermute(pass_on, 'near', swap)  2.36 us
    ppermute x1, starting transfers between devices, local_pairs(): passed = lax.ppermute(pass_on, 'near', swap)  1.93 us
    all_to_all x1, waiting for transfers between devices, local_pairs(): lax.all_to_all(back, ('far', 'near', 'col'), split_axis=0, concat_axis=0,...  1.61 us
  transfers between devices with their start and end apart: 14, of which 9 were waited for; matrix products, arithmetic and copies ran while one was open for 0% of the time, Pallas kernels for 8%

profile of v2, /device:TPU:0, one launch (start us, length us, event | category | flops | bytes accessed | tf_op | source)
XLA Modules:
  0.0 42.0 jit_solution(9444217191063741164)
XLA Ops:
  0.6 3.0 %collective-permute-start.7 = (bf16[4,256,256]{2,1,0:T(8,128)(2,1)}, bf16[4,256,256]{2,1,0:T(8,128)(2,1)S(1)}, u32[]{:S(2)}, u32[]{:S(2)}) collective-permute-start(bf16[4,256,256]{2,1,0:T(8,128)(2,1)} %refs_8_.1), channel_id=1, source_target_pairs={{0,2},{2,0},{1,3},{3,1},{4,6},{6,4},{5,7},{7,5},{8,10},{10,8},{9,1... | collective-permute-start | bytes 1572872 | tf_op jit(solution)/shard_map/ppermute | solution.py:396
  3.6 0.0 copy-start.5
  3.6 0.0 copy-start.4
  3.6 0.0 copy-start.6
  3.6 0.7 %copy-done.5 = f32[2,2]{1,0:T(2,128)S(1)} copy-done((f32[2,2]{1,0:T(2,128)S(1)}, f32[2,2]{1,0:T(2,128)}, u32[]{:S(2)}) %copy-start.5) | copy-done | bytes 40
  4.3 0.0 copy-done.4
  4.3 0.0 copy-done.6
  4.3 0.0 copy-start
  4.3 1.2 %copy-done = bf16[256,2048]{1,0:T(8,128)(2,1)S(1)} copy-done((bf16[256,2048]{1,0:T(8,128)(2,1)S(1)}, bf16[256,2048]{1,0:T(8,128)(2,1)}, u32[]{:S(2)}) %copy-start) | copy-done | bytes 1048600
  5.6 0.0 copy-start.2
  5.6 0.7 %copy-done.2 = f32[256,16]{0,1:T(8,128)S(1)} copy-done((f32[256,16]{0,1:T(8,128)S(1)}, f32[256,16]{0,1:T(8,128)}, u32[]{:S(2)}) %copy-start.2) | copy-done | bytes 16408
  6.3 0.0 copy-start.3
  6.3 0.7 %copy-done.3 = f32[256,16]{0,1:T(8,128)S(1)} copy-done((f32[256,16]{0,1:T(8,128)S(1)}, f32[256,16]{0,1:T(8,128)}, u32[]{:S(2)}) %copy-start.3) | copy-done | bytes 16408
  7.0 0.0 copy-start.1
  7.0 0.0 copy-start.7
  7.0 0.8 %prepare.1 = (bf16[272,128]{1,0:T(8,128)(2,1)S(1)}, bf16[272,128]{1,0:T(8,128)(2,1)S(1)}, bf16[272,128]{1,0:T(8,128)(2,1)S(1)}, bf16[272,128]{1,0:T(8,128)(2,1)S...) custom-call(s32[2,128]{1,0:T(2,128)S(1)} %copy-done.4, s32[1,8]{1,0:T(1,128)S(1)} %bitcast.7, ...), custom_call_target="tpu_custom_call" | custom-call | flops 67108864 | bytes 1048576 | tf_op jit(solution)/shard_map/prepare/pallas_call | solution.py:398
  7.8 1.6 %collective-permute-start = (bf16[272,128]{1,0:T(8,128)(2,1)S(1)}, bf16[272,128]{1,0:T(8,128)(2,1)S(1)}, u32[]{:S(2)}, u32[]{:S(2)}) collective-permute-start(bf16[272,128]{1,0:T(8,128)(2,1)S(1)} %get-tuple-element.24), channel_id=1, source_target_pairs={{0,4},{4,0},{8,12},{12,8},{1,5},{5,1},{9,13},{13,9},{2,6},{6,2},{1... | collective-permute-start | bytes 208904 | tf_op jit(solution)/shard_map/ppermute | solution.py:394
  9.4 2.6 %collective-permute-start.1 = (bf16[272,128]{1,0:T(8,128)(2,1)S(1)}, bf16[272,128]{1,0:T(8,128)(2,1)S(1)}, u32[]{:S(2)}, u32[]{:S(2)}) collective-permute-start(bf16[272,128]{1,0:T(8,128)(2,1)S(1)} %get-tuple-element.25), channel_id=1, source_target_pairs={{0,8},{4,12},{8,0},{12,4},{1,9},{5,13},{9,1},{13,5},{2,10},{6,14},... | collective-permute-start | bytes 208904 | tf_op jit(solution)/shard_map/ppermute | solution.py:394
  12.0 0.2 collective-permute-start.2
  12.2 0.0 collective-permute-start.3
  12.2 0.0 collective-permute-done.refs_1_
  12.3 0.0 copy-done.1
  12.3 0.4 collective-permute-start.8
  12.6 4.0 %collective-permute-done.1.refs_2_ = bf16[272,128]{1,0:T(8,128)(2,1)S(1)} collective-permute-done((bf16[272,128]{1,0:T(8,128)(2,1)S(1)}, bf16[272,128]{1,0:T(8,128)(2,1)S(1)}, u32[]{:S(2)}, u32[]{:S(2)}) %collective-permute-start.1) | collective-permute-done | bytes 69664 | tf_op jit(solution)/shard_map/ppermute | solution.py:394
  16.7 0.0 collective-permute-start.4
  16.7 1.5 %collective-permute-done.2.refs_3_ = bf16[272,128]{1,0:T(8,128)(2,1)S(1)} collective-permute-done((bf16[272,128]{1,0:T(8,128)(2,1)S(1)}, bf16[272,128]{1,0:T(8,128)(2,1)S(1)}, u32[]{:S(2)}, u32[]{:S(2)}) %collective-permute-start.2) | collective-permute-done | bytes 69664 | tf_op jit(solution)/shard_map/ppermute | solution.py:394
  18.2 0.0 collective-permute-start.5
  18.2 0.0 collective-permute-done.3.refs_4_
  18.2 0.5 %collective-permute-start.6 = (bf16[272,128]{1,0:T(8,128)(2,1)S(1)}, bf16[272,128]{1,0:T(8,128)(2,1)S(1)}, u32[]{:S(2)}, u32[]{:S(2)}) collective-permute-start(bf16[272,128]{1,0:T(8,128)(2,1)S(1)} %collective-permute-done.2.refs_3_), channel_id=1, source_target_pairs={{0,1},{1,0},{2,3},{3,2},{4,5},{5,4},{6,7},{7,6},{8,9},{9,8},{10,11... | collective-permute-start | bytes 208904 | tf_op jit(solution)/shard_map/ppermute | solution.py:416
  18.7 0.0 collective-permute-done.4.refs_5_
  18.7 0.7 %collective-permute-done.5.refs_6_ = bf16[272,128]{1,0:T(8,128)(2,1)S(1)} collective-permute-done((bf16[272,128]{1,0:T(8,128)(2,1)S(1)}, bf16[272,128]{1,0:T(8,128)(2,1)S(1)}, u32[]{:S(2)}, u32[]{:S(2)}) %collective-permute-start.5) | collective-permute-done | bytes 69664 | tf_op jit(solution)/shard_map/ppermute | solution.py:416
  19.4 0.2 collective-permute-done.6.refs_7_
  19.6 0.0 collective-permute-done.7.refs_9_
  19.6 0.0 copy-done.7
  19.6 1.1 %project.1 = (f32[128,256]{1,0:T(8,128)S(1)}, s16[272,128]{1,0:T(8,128)(2,1)S(1)}, s16[272,128]{1,0:T(8,128)(2,1)S(1)}, s16[272,128]{1,0:T(8,128)(2,1)S(1)}) custom-call(bf16[272,128]{1,0:T(8,128)(2,1)S(1)} %get-tuple-element.23.refs_0_, bf16[272,128]{1,0:T(8,128)(2,1)S(1)} %collective-permute-done.refs_1_, ...), custom_call_target="tpu_custom_call" | custom-call | flops 1073741824 | bytes 2097152 | tf_op jit(solution)/shard_map/project/pallas_call | solution.py:419
  20.7 1.6 %collective-permute-start.10 = (s16[272,128]{1,0:T(8,128)(2,1)S(1)}, s16[272,128]{1,0:T(8,128)(2,1)S(1)}, u32[]{:S(2)}, u32[]{:S(2)}) collective-permute-start(s16[272,128]{1,0:T(8,128)(2,1)S(1)} %get-tuple-element.32), channel_id=1, source_target_pairs={{0,8},{4,12},{8,0},{12,4},{1,9},{5,13},{9,1},{13,5},{2,10},{6,14},... | collective-permute-start | bytes 208904 | tf_op jit(solution)/shard_map/ppermute | solution.py:394
  22.3 0.6 %collective-permute-start.11 = (s16[272,128]{1,0:T(8,128)(2,1)S(1)}, s16[272,128]{1,0:T(8,128)(2,1)S(1)}, u32[]{:S(2)}, u32[]{:S(2)}) collective-permute-start(s16[272,128]{1,0:T(8,128)(2,1)S(1)} %get-tuple-element.33), channel_id=1, source_target_pairs={{0,12},{4,8},{8,4},{12,0},{1,13},{5,9},{9,5},{13,1},{2,14},{6,10},... | collective-permute-start | bytes 208904 | tf_op jit(solution)/shard_map/ppermute | solution.py:394
  22.9 1.3 %collective-permute-start.9 = (s16[272,128]{1,0:T(8,128)(2,1)S(1)}, s16[272,128]{1,0:T(8,128)(2,1)S(1)}, u32[]{:S(2)}, u32[]{:S(2)}) collective-permute-start(s16[272,128]{1,0:T(8,128)(2,1)S(1)} %get-tuple-element.31), channel_id=1, source_target_pairs={{0,4},{4,0},{8,12},{12,8},{1,5},{5,1},{9,13},{13,9},{2,6},{6,2},{1... | collective-permute-start | bytes 208904 | tf_op jit(solution)/shard_map/ppermute | solution.py:394
  24.2 0.0 collective-permute-done.8.refs_5_
  24.2 0.7 %lookup.1 = (f32[128,256]{1,0:T(8,128)S(1)}, f32[128,128]{1,0:T(8,128)S(1)}, f32[8,128]{1,0:T(8,128)S(1)}) custom-call(bf16[272,128]{1,0:T(8,128)(2,1)S(1)} %get-tuple-element.23.refs_0_, bf16[272,128]{1,0:T(8,128)(2,1)S(1)} %collective-permute-done.refs_1_, bf16[272,128]{1,0:T(8,128)(2,1)S(1)} %collective-permute-done.1.refs_2_, ...), custom_call_target="tpu_custom_call" | custom-call | flops 33554432 | bytes 524288 | tf_op jit(solution)/shard_map/lookup/pallas_call | solution.py:428
  24.9 2.8 %collective-permute-done.10.refs_5_ = s16[272,128]{1,0:T(8,128)(2,1)S(1)} collective-permute-done((s16[272,128]{1,0:T(8,128)(2,1)S(1)}, s16[272,128]{1,0:T(8,128)(2,1)S(1)}, u32[]{:S(2)}, u32[]{:S(2)}) %collective-permute-start.10) | collective-permute-done | bytes 69664 | tf_op jit(solution)/shard_map/ppermute | solution.py:394
  27.7 1.3 %collective-permute-done.11.refs_6_ = s16[272,128]{1,0:T(8,128)(2,1)S(1)} collective-permute-done((s16[272,128]{1,0:T(8,128)(2,1)S(1)}, s16[272,128]{1,0:T(8,128)(2,1)S(1)}, u32[]{:S(2)}, u32[]{:S(2)}) %collective-permute-start.11) | collective-permute-done | bytes 69664 | tf_op jit(solution)/shard_map/ppermute | solution.py:394
  29.0 0.7 %collective-permute-done.9.refs_4_ = s16[272,128]{1,0:T(8,128)(2,1)S(1)} collective-permute-done((s16[272,128]{1,0:T(8,128)(2,1)S(1)}, s16[272,128]{1,0:T(8,128)(2,1)S(1)}, u32[]{:S(2)}, u32[]{:S(2)}) %collective-permute-start.9) | collective-permute-done | bytes 69664 | tf_op jit(solution)/shard_map/ppermute | solution.py:394
  29.8 0.9 %reduce.1 = (bf16[64,256]{1,0:T(8,128)(2,1)S(1)}, bf16[80,256]{1,0:T(8,128)(2,1)S(1)}, f32[16,8,128]{2,1,0:T(8,128)}) custom-call(f32[128,256]{1,0:T(8,128)S(1)} %get-tuple-element.27.refs_0_, f32[128,256]{1,0:T(8,128)S(1)} %get-tuple-element.28.refs_1_, f32[128,128]{1,0:T(8,128)S(1)} %get-tuple-element.29.refs_2_, ...), custom_call_target="tpu_custom_call" | custom-call | flops 262144 | bytes 327680 | tf_op jit(solution)/shard_map/reduce/pallas_call | solution.py:436
  30.7 3.7 %all-to-all-start = ((f32[16,8,128]{2,1,0:T(8,128)}), f32[16,8,128]{2,1,0:T(8,128)S(1)}, u32[]{:S(2)}, u32[]{:S(2)}) async-start(f32[16,8,128]{2,1,0:T(8,128)} %get-tuple-element.36), calls=%async_computation | async-start | bytes 131072 | tf_op jit(solution)/shard_map/all_to_all | solution.py:448
  34.4 1.9 %collective-permute-start.12 = (bf16[80,256]{1,0:T(8,128)(2,1)S(1)}, bf16[80,256]{1,0:T(8,128)(2,1)S(1)}, u32[]{:S(2)}, u32[]{:S(2)}) collective-permute-start(bf16[80,256]{1,0:T(8,128)(2,1)S(1)} %get-tuple-element.35), channel_id=1, source_target_pairs={{0,2},{2,0},{1,3},{3,1},{4,6},{6,4},{5,7},{7,5},{8,10},{10,8},{9,1... | collective-permute-start | bytes 122888 | tf_op jit(solution)/shard_map/ppermute | solution.py:449
  36.3 2.4 %collective-permute-done.12.passed = bf16[80,256]{1,0:T(8,128)(2,1)S(1)} collective-permute-done((bf16[80,256]{1,0:T(8,128)(2,1)S(1)}, bf16[80,256]{1,0:T(8,128)(2,1)S(1)}, u32[]{:S(2)}, u32[]{:S(2)}) %collective-permute-start.12) | collective-permute-done | bytes 40992 | tf_op jit(solution)/shard_map/ppermute | solution.py:449
  38.6 1.0 %value_rows.1 = f32[512,256]{1,0:T(8,128)} custom-call(bf16[64,256]{1,0:T(8,128)(2,1)S(1)} %get-tuple-element.34.contrib, bf16[80,256]{1,0:T(8,128)(2,1)S(1)} %collective-permute-done.12.passed, f32[8,128]{1,0:T(8,128)S(1)} %get-tuple-element.30.refs_3_.value_rows), custom_call_target="tpu_custom_call" | custom-call | flops 33554432 | bytes 524288 | tf_op jit(solution)/shard_map/value_rows/pallas_call | solution.py:450
  39.6 1.6 %all-to-all-done.back = f32[16,8,128]{2,1,0:T(8,128)S(1)} async-done(((f32[16,8,128]{2,1,0:T(8,128)}), f32[16,8,128]{2,1,0:T(8,128)S(1)}, u32[]{:S(2)}, u32[]{:S(2)}) %all-to-all-start) | async-done | bytes 65568 | tf_op jit(solution)/shard_map/all_to_all | solution.py:448
  41.3 0.8 %finish.1 = (f32[16,256]{1,0:T(8,128)}, f32[16,256]{1,0:T(8,128)}, f32[2,2]{1,0:T(2,128)}) custom-call(f32[16,8,128]{2,1,0:T(8,128)S(1)} %all-to-all-done.back, f32[32,128]{1,0:T(8,128)S(1)} %get-tuple-element.37.scaled, bf16[256,128]{1,0:T(8,128)(2,1)S(1)} %get-tuple-element.38.hits), custom_call_target="tpu_custom_call" | custom-call | flops 6291456 | bytes 131072 | tf_op jit(solution)/shard_map/finish/pallas_call | solution.py:458
Async XLA Ops:
  0.6 19.0 %collective-permute-start.7 = (bf16[4,256,256]{2,1,0:T(8,128)(2,1)}, bf16[4,256,256]{2,1,0:T(8,128)(2,1)S(1)}, u32[]{:S(2)}, u32[]{:S(2)}) collective-permute-start(bf16[4,256,256]{2,1,0:T(8,128)(2,1)} %refs_8_.1), channel_id=1, source_target_pairs={{0,2},{2,0},{1,3},{3,1},{4,6},{6,4},{5,7},{7,5},{8,10},{10,8},{9,1... | collective-permute-start | bytes 1572872 | tf_op jit(solution)/shard_map/ppermute | solution.py:396
  3.6 0.7 %copy-start.5 = (f32[2,2]{1,0:T(2,128)S(1)}, f32[2,2]{1,0:T(2,128)}, u32[]{:S(2)}) copy-start(f32[2,2]{1,0:T(2,128)} %core_hbm.1) | copy-start | bytes 52
  3.6 0.7 %copy-start.4 = (s32[2,128]{1,0:T(2,128)S(1)}, s32[2,128]{1,0:T(2,128)}, u32[]{:S(2)}) copy-start(s32[2,128]{1,0:T(2,128)} %pair_hbm.1) | copy-start | bytes 3076
  3.6 0.7 %copy-start.6 = (s32[8]{0:T(128)S(1)}, s32[8]{0:T(128)}, u32[]{:S(2)}) copy-start(s32[8]{0:T(128)} %param.15) | copy-start | bytes 100
  4.3 1.2 %copy-start = (bf16[256,2048]{1,0:T(8,128)(2,1)S(1)}, bf16[256,2048]{1,0:T(8,128)(2,1)}, u32[]{:S(2)}) copy-start(bf16[256,2048]{1,0:T(8,128)(2,1)} %grads_hbm.1) | copy-start | bytes 3145732
  5.6 0.7 %copy-start.2 = (f32[256,16]{0,1:T(8,128)S(1)}, f32[256,16]{0,1:T(8,128)}, u32[]{:S(2)}) copy-start(f32[256,16]{0,1:T(8,128)} %param.11) | copy-start | bytes 49156
  6.3 0.7 %copy-start.3 = (f32[256,16]{0,1:T(8,128)S(1)}, f32[256,16]{0,1:T(8,128)}, u32[]{:S(2)}) copy-start(f32[256,16]{0,1:T(8,128)} %param.12) | copy-start | bytes 49156
  7.0 5.3 %copy-start.1 = (bf16[512,256]{1,0:T(8,128)(2,1)S(1)}, bf16[512,256]{1,0:T(8,128)(2,1)}, u32[]{:S(2)}) copy-start(bf16[512,256]{1,0:T(8,128)(2,1)} %refs_4_.1) | copy-start | bytes 786436
  7.0 12.6 %copy-start.7 = (bf16[4,256,256]{2,1,0:T(8,128)(2,1)S(1)}, bf16[4,256,256]{2,1,0:T(8,128)(2,1)}, u32[]{:S(2)}) copy-start(bf16[4,256,256]{2,1,0:T(8,128)(2,1)} %refs_8_.1) | copy-start | bytes 1572868
  7.8 4.5 %collective-permute-start = (bf16[272,128]{1,0:T(8,128)(2,1)S(1)}, bf16[272,128]{1,0:T(8,128)(2,1)S(1)}, u32[]{:S(2)}, u32[]{:S(2)}) collective-permute-start(bf16[272,128]{1,0:T(8,128)(2,1)S(1)} %get-tuple-element.24), channel_id=1, source_target_pairs={{0,4},{4,0},{8,12},{12,8},{1,5},{5,1},{9,13},{13,9},{2,6},{6,2},{1... | collective-permute-start | bytes 208904 | tf_op jit(solution)/shard_map/ppermute | solution.py:394
  9.4 7.2 %collective-permute-start.1 = (bf16[272,128]{1,0:T(8,128)(2,1)S(1)}, bf16[272,128]{1,0:T(8,128)(2,1)S(1)}, u32[]{:S(2)}, u32[]{:S(2)}) collective-permute-start(bf16[272,128]{1,0:T(8,128)(2,1)S(1)} %get-tuple-element.25), channel_id=1, source_target_pairs={{0,8},{4,12},{8,0},{12,4},{1,9},{5,13},{9,1},{13,5},{2,10},{6,14},... | collective-permute-start | bytes 208904 | tf_op jit(solution)/shard_map/ppermute | solution.py:394
  12.0 6.1 %collective-permute-start.2 = (bf16[272,128]{1,0:T(8,128)(2,1)S(1)}, bf16[272,128]{1,0:T(8,128)(2,1)S(1)}, u32[]{:S(2)}, u32[]{:S(2)}) collective-permute-start(bf16[272,128]{1,0:T(8,128)(2,1)S(1)} %get-tuple-element.26), channel_id=1, source_target_pairs={{0,12},{4,8},{8,4},{12,0},{1,13},{5,9},{9,5},{13,1},{2,14},{6,10},... | collective-permute-start | bytes 208904 | tf_op jit(solution)/shard_map/ppermute | solution.py:394
  12.2 5.9 %collective-permute-start.3 = (bf16[272,128]{1,0:T(8,128)(2,1)S(1)}, bf16[272,128]{1,0:T(8,128)(2,1)S(1)}, u32[]{:S(2)}, u32[]{:S(2)}) collective-permute-start(bf16[272,128]{1,0:T(8,128)(2,1)S(1)} %get-tuple-element.23.refs_0_), channel_id=1, source_target_pairs={{0,1},{1,0},{2,3},{3,2},{4,5},{5,4},{6,7},{7,6},{8,9},{9,8},{10,11... | collective-permute-start | bytes 208904 | tf_op jit(solution)/shard_map/ppermute | solution.py:416
  12.3 12.0 %collective-permute-start.8 = (bf16[512,256]{1,0:T(8,128)(2,1)S(1)}, bf16[512,256]{1,0:T(8,128)(2,1)S(1)}, u32[]{:S(2)}, u32[]{:S(2)}) collective-permute-start(bf16[512,256]{1,0:T(8,128)(2,1)S(1)} %copy-done.1), channel_id=1, source_target_pairs={{0,2},{2,0},{1,3},{3,1},{4,6},{6,4},{5,7},{7,5},{8,10},{10,8},{9,1... | collective-permute-start | bytes 786440 | tf_op jit(solution)/shard_map/ppermute | solution.py:417
  16.7 2.0 %collective-permute-start.4 = (bf16[272,128]{1,0:T(8,128)(2,1)S(1)}, bf16[272,128]{1,0:T(8,128)(2,1)S(1)}, u32[]{:S(2)}, u32[]{:S(2)}) collective-permute-start(bf16[272,128]{1,0:T(8,128)(2,1)S(1)} %collective-permute-done.refs_1_), channel_id=1, source_target_pairs={{0,1},{1,0},{2,3},{3,2},{4,5},{5,4},{6,7},{7,6},{8,9},{9,8},{10,11... | collective-permute-start | bytes 208904 | tf_op jit(solution)/shard_map/ppermute | solution.py:416
  18.2 1.3 %collective-permute-start.5 = (bf16[272,128]{1,0:T(8,128)(2,1)S(1)}, bf16[272,128]{1,0:T(8,128)(2,1)S(1)}, u32[]{:S(2)}, u32[]{:S(2)}) collective-permute-start(bf16[272,128]{1,0:T(8,128)(2,1)S(1)} %collective-permute-done.1.refs_2_), channel_id=1, source_target_pairs={{0,1},{1,0},{2,3},{3,2},{4,5},{5,4},{6,7},{7,6},{8,9},{9,8},{10,11... | collective-permute-start | bytes 208904 | tf_op jit(solution)/shard_map/ppermute | solution.py:416
  18.2 1.4 %collective-permute-start.6 = (bf16[272,128]{1,0:T(8,128)(2,1)S(1)}, bf16[272,128]{1,0:T(8,128)(2,1)S(1)}, u32[]{:S(2)}, u32[]{:S(2)}) collective-permute-start(bf16[272,128]{1,0:T(8,128)(2,1)S(1)} %collective-permute-done.2.refs_3_), channel_id=1, source_target_pairs={{0,1},{1,0},{2,3},{3,2},{4,5},{5,4},{6,7},{7,6},{8,9},{9,8},{10,11... | collective-permute-start | bytes 208904 | tf_op jit(solution)/shard_map/ppermute | solution.py:416
  20.7 7.0 %collective-permute-start.10 = (s16[272,128]{1,0:T(8,128)(2,1)S(1)}, s16[272,128]{1,0:T(8,128)(2,1)S(1)}, u32[]{:S(2)}, u32[]{:S(2)}) collective-permute-start(s16[272,128]{1,0:T(8,128)(2,1)S(1)} %get-tuple-element.32), channel_id=1, source_target_pairs={{0,8},{4,12},{8,0},{12,4},{1,9},{5,13},{9,1},{13,5},{2,10},{6,14},... | collective-permute-start | bytes 208904 | tf_op jit(solution)/shard_map/ppermute | solution.py:394
  22.3 6.7 %collective-permute-start.11 = (s16[272,128]{1,0:T(8,128)(2,1)S(1)}, s16[272,128]{1,0:T(8,128)(2,1)S(1)}, u32[]{:S(2)}, u32[]{:S(2)}) collective-permute-start(s16[272,128]{1,0:T(8,128)(2,1)S(1)} %get-tuple-element.33), channel_id=1, source_target_pairs={{0,12},{4,8},{8,4},{12,0},{1,13},{5,9},{9,5},{13,1},{2,14},{6,10},... | collective-permute-start | bytes 208904 | tf_op jit(solution)/shard_map/ppermute | solution.py:394
  22.9 6.8 %collective-permute-start.9 = (s16[272,128]{1,0:T(8,128)(2,1)S(1)}, s16[272,128]{1,0:T(8,128)(2,1)S(1)}, u32[]{:S(2)}, u32[]{:S(2)}) collective-permute-start(s16[272,128]{1,0:T(8,128)(2,1)S(1)} %get-tuple-element.31), channel_id=1, source_target_pairs={{0,4},{4,0},{8,12},{12,8},{1,5},{5,1},{9,13},{13,9},{2,6},{6,2},{1... | collective-permute-start | bytes 208904 | tf_op jit(solution)/shard_map/ppermute | solution.py:394
  30.7 10.6 %all-to-all-start = ((f32[16,8,128]{2,1,0:T(8,128)}), f32[16,8,128]{2,1,0:T(8,128)S(1)}, u32[]{:S(2)}, u32[]{:S(2)}) async-start(f32[16,8,128]{2,1,0:T(8,128)} %get-tuple-element.36), calls=%async_computation | async-start | bytes 131072 | tf_op jit(solution)/shard_map/all_to_all | solution.py:448
  34.4 4.3 %collective-permute-start.12 = (bf16[80,256]{1,0:T(8,128)(2,1)S(1)}, bf16[80,256]{1,0:T(8,128)(2,1)S(1)}, u32[]{:S(2)}, u32[]{:S(2)}) collective-permute-start(bf16[80,256]{1,0:T(8,128)(2,1)S(1)} %get-tuple-element.35), channel_id=1, source_target_pairs={{0,2},{2,0},{1,3},{3,1},{4,6},{6,4},{5,7},{7,5},{8,10},{10,8},{9,1... | collective-permute-start | bytes 122888 | tf_op jit(solution)/shard_map/ppermute | solution.py:449

commit v3 on v2

--- a/solution.py
+++ b/solution.py
@@ -20,6 +20,7 @@
 SCORE, ROW_HIGH, ROW_LOW, OUTER, OUTER_REST = 0, 1, 2, 4, 12
 RECORD = 16
 FULL = 32000.0
+WHOLE = 2
 
 
 def local_weights(grads, values, expand_weight, row_factors, col_factors, core, pair_index, counts):
@@ -116,16 +117,13 @@
     return lax.axis_index("far"), lax.axis_index("near"), lax.axis_index("col")
 
 
-def prepare_kernel(
-    far, pair_hbm, counts_hbm, core_hbm, row_hbm, col_hbm, grads_hbm, *refs
-):
-    sends, (scaled, hits), (pair, counts, core, row_fac, col_fac, grads, sems) = (
-        refs[:far],
-        refs[far : far + 2],
-        refs[far + 2 :],
-    )
-    sources = (pair_hbm, counts_hbm, core_hbm, row_hbm, col_hbm, grads_hbm)
-    targets = (pair, counts, core, row_fac, col_fac, grads)
+def prepare_kernel(far, first, last, extra, *refs):
+    sources, refs = refs[:6], refs[6:]
+    sends, refs = refs[: last - first], refs[last - first :]
+    if extra:
+        (scaled, hits), refs = refs[:2], refs[2:]
+    targets, sems = refs[:6], refs[6]
+    pair, counts, core, row_fac, col_fac, grads = targets
     copies = [
         pltpu.make_async_copy(source, target, sems.at[k])
         for k, (source, target) in enumerate(zip(sources, targets))
@@ -154,7 +152,6 @@
     col_cand = code % NC
     hit = iota((tokens, rows), 0) == token
     hot = jnp.where(hit, 1.0, 0.0).astype(BF16)
-    hits[...] = hot
     factors = jnp.concatenate([row_fac[...], col_fac[...]], axis=0)
     found = add_thirds(dot_nn(thirds(factors), hot))
     at = iota(found.shape, 0)
@@ -167,12 +164,14 @@
     b0, b1 = pick(split + col_cand * RANK), pick(split + col_cand * RANK + 1)
     c00, c01, c10, c11 = core[0:1, 0:1], core[0:1, 1:2], core[1:2, 0:1], core[1:2, 1:2]
     core_b0, core_b1 = c00 * b0 + c01 * b1, c10 * b0 + c11 * b1
-    core_a0, core_a1 = c00 * a0 + c10 * a1, c01 * a0 + c11 * a1
     score = jnp.where(live, a0 * core_b0 + a1 * core_b1, 0.0)
-    even = at % RANK == 0
-    of_row = jnp.where(at // RANK == row_cand, jnp.where(even, core_b0, core_b1), 0.0)
-    of_col = jnp.where((at - split) // RANK == col_cand, jnp.where(even, core_a0, core_a1), 0.0)
-    scaled[...] = jnp.where(at < split, of_row, of_col)
+    if extra:
+        hits[...] = hot
+        core_a0, core_a1 = c00 * a0 + c10 * a1, c01 * a0 + c11 * a1
+        even = at % RANK == 0
+        of_row = jnp.where(at // RANK == row_cand, jnp.where(even, core_b0, core_b1), 0.0)
+        of_col = jnp.where((at - split) // RANK == col_cand, jnp.where(even, core_a0, core_a1), 0.0)
+        scaled[...] = jnp.where(at < split, of_row, of_col)
 
     field = iota((RECORD, rows), 0)
     record = jnp.where(field == SCORE, score, 0.0)
@@ -189,27 +188,32 @@
     order = jnp.where(iota((rows, rows), 0) == to_pair, 1.0, 0.0).astype(BF16)
     records = dot_nn(record.astype(BF16), order).astype(BF16)
 
+    q = iota((rows, rows), 0)
     mine = rows // 2
-    q = iota((mine, rows), 0)
-    q_pair = ((q // cap ^ z) * 2 + (q // half % 2 ^ x)) * cap + c * half + q % half
-    take = jnp.where(iota((mine, rows), 1) == q_pair, 1.0, 0.0).astype(BF16)
+    q_pair = ((q % mine // cap ^ z) * 2 + (q // half % 2 ^ x)) * cap
+    q_pair = q_pair + (q // mine ^ c) * half + q % half
+    take = jnp.where(iota((rows, rows), 1) == q_pair, 1.0, 0.0).astype(BF16)
     live_hits = jnp.where(jnp.logical_and(hit, live), 1.0, 0.0).astype(BF16)
     chosen = dot_nt(take, live_hits).astype(BF16)
     copies[-1].wait()
-    for k in range(far):
-        blocks = []
+    for k in range(first, last):
+        taken = []
         for y in range(2):
             start = pl.multiple_of(((z ^ k) * 2 + (x ^ y)) * shard, shard)
-            taken = dot_nn(chosen, grads[:, pl.ds(start, shard)]).astype(BF16)
-            blocks += [taken[:, :128], taken[:, 128:]]
-        sends[k][...] = jnp.concatenate(blocks + [records], axis=0)
+            part = grads[:, pl.ds(start, shard)]
+            taken.append(dot_nn(chosen if k < WHOLE else chosen[:mine], part).astype(BF16))
+        blocks = []
+        for g in range(2 if k < WHOLE else 1):
+            for part in taken:
+                part = part[g * mine : (g + 1) * mine]
+                blocks += [part[:, :128], part[:, 128:]]
+        sends[k - first][...] = jnp.concatenate(blocks + [records], axis=0)
 
 
 def project_kernel(far, *refs):
-    ours, theirs = refs[:far], refs[far : 2 * far]
-    own, near = refs[2 * far : 2 * far + 2]
-    whole, coded = refs[2 * far + 2], refs[2 * far + 3 :]
-    mine = (ours[0].shape[0] - RECORD) // 4
+    ours, theirs = refs[:far], refs[far : 2 * far - WHOLE]
+    own, near, whole, *coded = refs[2 * far - WHOLE :]
+    mine = (ours[far - 1].shape[0] - RECORD) // 4
     cap = mine // far // 2 * 2
     half = cap // 2
     rows = 2 * mine
@@ -217,12 +221,13 @@
     mask = line % mine // half * cap + line // mine * half + line % half == lane
     firsts, seconds, projs = [], [], []
     for k in range(far):
-        for block in (ours[k], theirs[k]):
-            firsts.append(jnp.concatenate([block[0:mine], block[mine : 2 * mine]], axis=1))
-            seconds.append(
-                jnp.concatenate([block[2 * mine : 3 * mine], block[3 * mine : 4 * mine]], axis=1)
-            )
-        record = ours[k][4 * mine : 4 * mine + RECORD].astype(F32)
+        for g in range(2):
+            block, at = (ours[k], 4 * mine * g) if k < WHOLE or g == 0 else (theirs[k - WHOLE], 0)
+            quarters = [block[at + i * mine : at + (i + 1) * mine] for i in range(4)]
+            firsts.append(jnp.concatenate(quarters[:2], axis=1))
+            seconds.append(jnp.concatenate(quarters[2:], axis=1))
+        at = ours[k].shape[0] - RECORD
+        record = ours[k][at : at + RECORD].astype(F32)
         low = jnp.where(mask, record[ROW_LOW : ROW_LOW + 1], 0.0)
         projs.append(jnp.sum(low, axis=1, keepdims=True))
     first, second = jnp.concatenate(firsts, axis=0), jnp.concatenate(seconds, axis=0)
@@ -267,7 +272,8 @@
     lane, line = iota((rows, rows), 1), iota((rows, rows), 0)
     total = jnp.zeros((RECORD, rows), F32)
     for n in range(far):
-        tile = blocks[n][2 * rows : 2 * rows + RECORD]
+        at = blocks[n].shape[0] - RECORD
+        tile = blocks[n][at : at + RECORD]
         source = n * group + lane // (rows // 2) * (group // 2) + lane % (group // 2)
         inside = lane // (group // 2) % far == n
         move = jnp.where(jnp.logical_and(line == source, inside), 1.0, 0.0).astype(BF16)
@@ -326,7 +332,8 @@
         back[k] = block
 
 
-def value_kernel(contrib, passed, value_rows, out):
+def output_kernel(far, contrib, passed, value_rows, back, scaled, hits, *outs):
+    out, row_out, col_out, core_out = outs
     half = contrib.shape[0]
     rows = 2 * half
     tail = passed[half : half + RECORD].astype(F32)
@@ -335,9 +342,6 @@
     row = jnp.where(lane < half, value_rows[0:1], other).astype(jnp.int32)
     hot = jnp.where(iota((out.shape[0], rows), 0) == row, 1.0, 0.0).astype(BF16)
     out[...] = dot_nn(hot, jnp.concatenate([contrib[...], passed[:half]], axis=0))
-
-
-def finish_kernel(far, back, scaled, hits, row_out, col_out, core_out):
     z, x, _ = place()
     line = iota(back.shape[1:], 0)
     total = jnp.zeros(back.shape[1:], F32)
@@ -350,7 +354,6 @@
     split = row_out.shape[0]
     row_out[...] = grads[:split]
     col_out[...] = grads[split:]
-    lane = iota(outer.shape, 1)
     r, s = iota((RANK, RANK), 0), iota((RANK, RANK), 1)
     result = jnp.zeros((RANK, RANK), F32)
     for k in range(RANK * RANK):
@@ -361,7 +364,7 @@
 
 
 VMEM = pl.BlockSpec(memory_space=pltpu.VMEM)
-HBM = pl.BlockSpec(memory_space=pl.ANY)
+HBM = pl.BlockSpec(memory_space=pltpu.HBM)
 
 
 def call(kernel, name, outs, ins, flops, moved, scratch=(), limit=24):
@@ -394,37 +397,45 @@
         return lax.ppermute(block, "far", [(i, i ^ k) for i in range(far)])
 
     near_weight = lax.ppermute(expand_weight, "near", swap)
-    block = shape((2 * rows + RECORD, 128), BF16)
-    *sends, scaled, hits = call(
-        functools.partial(prepare_kernel, far),
-        "prepare",
-        (block,) * far + (shape((factors, rows), F32), shape((tokens, rows), BF16)),
-        [HBM] * 6,
-        rows * tokens * depth,
-        2 * tokens * depth,
-        (
-            pltpu.VMEM((2, rows), jnp.int32),
-            pltpu.VMEM((1, nmem), jnp.int32),
-            pltpu.VMEM((RANK, RANK), F32),
-            pltpu.VMEM((NR * RANK, tokens), F32),
-            pltpu.VMEM((NC * RANK, tokens), F32),
-            pltpu.VMEM((tokens, depth), BF16),
-            pltpu.SemaphoreType.DMA((6,)),
-        ),
-    )(pair_index, counts.reshape(1, nmem), core, row_factors.T, col_factors.T, grads)
-    ours = [sends[0]] + [along_far(sends[k], k) for k in range(1, far)]
-    theirs = [lax.ppermute(got, "col", swap) for got in ours]
+    blocks = [shape(((4 if k < WHOLE else 2) * rows + RECORD, 128), BF16) for k in range(far)]
+
+    def prepare(name, first, last, extra, limit):
+        extras = (shape((factors, rows), F32), shape((tokens, rows), BF16)) if extra else ()
+        return call(
+            functools.partial(prepare_kernel, far, first, last, extra),
+            name,
+            tuple(blocks[first:last]) + extras,
+            [HBM] * 6,
+            rows * tokens * depth,
+            2 * tokens * depth,
+            (
+                pltpu.VMEM((2, rows), jnp.int32),
+                pltpu.VMEM((1, nmem), jnp.int32),
+                pltpu.VMEM((RANK, RANK), F32),
+                pltpu.VMEM((NR * RANK, tokens), F32),
+                pltpu.VMEM((NC * RANK, tokens), F32),
+                pltpu.VMEM((tokens, depth), BF16),
+                pltpu.SemaphoreType.DMA((6,)),
+            ),
+            limit,
+        )(pair_index, counts.reshape(1, nmem), core, row_factors.T, col_factors.T, grads)
+
+    sends = (None,) + tuple(prepare("prepare", 1, far, False, 60))
+    own_block, scaled, hits = prepare("prepare_own", 0, 1, True, 24)
+    got = {k: along_far(sends[k], k) for k in reversed(range(1, far))}
+    ours = [own_block] + [got[k] for k in range(1, far)]
+    theirs = [lax.ppermute(block, "col", swap) for block in ours[WHOLE:]]
     near_values = lax.ppermute(values, "near", swap)
     code = shape((2 * rows + RECORD, 128), jnp.int16)
     whole, *coded = call(
         functools.partial(project_kernel, far),
         "project",
         (shape((rows, width), F32),) + (code,) * (far - 1),
-        [VMEM] * (2 * far + 2),
+        [VMEM] * (2 * far - WHOLE + 2),
         4 * E * far * rows * depth // far * width,
         8 * E * width * depth // nmem,
     )(*ours, *theirs, expand_weight, near_weight)
-    coded = [along_far(coded[j - 1], j) for j in range(1, far)]
+    coded = [along_far(coded[j - 1], j) for j in reversed(range(1, far))]
     fetched, records, value_rows = call(
         functools.partial(lookup_kernel, far),
         "lookup",
@@ -447,26 +458,19 @@
     )(whole, fetched, records, value_rows, *coded)
     back = lax.all_to_all(back, ("far", "near", "col"), split_axis=0, concat_axis=0, tiled=True)
     passed = lax.ppermute(pass_on, "near", swap)
-    value_grad = call(
-        value_kernel,
-        "value_rows",
-        shape((vrows, width), F32),
-        [VMEM] * 3,
-        2 * rows * vrows * width,
-        4 * vrows * width,
-    )(contrib, passed, value_rows)
-    row_grad, col_grad, core_grad = call(
-        functools.partial(finish_kernel, far),
-        "finish",
+    value_grad, row_grad, col_grad, core_grad = call(
+        functools.partial(output_kernel, far),
+        "outputs",
         (
+            shape((vrows, width), F32),
             shape((NR * RANK, tokens), F32),
             shape((NC * RANK, tokens), F32),
             shape((RANK, RANK), F32),
         ),
-        [VMEM] * 3,
-        2 * rows * tokens * 96,
-        4 * rows * tokens,
-    )(back, scaled, hits)
+        [VMEM] * 6,
+        2 * rows * vrows * width,
+        4 * vrows * width,
+    )(contrib, passed, value_rows, back, scaled, hits)
     return value_grad, row_grad.T, col_grad.T, core_grad
 
 

time: 42.5 us -> 40.7 us (0.958)
  local copies, waits for them, and re-layouts: 3.36 us -> 0.03 us
  Pallas kernels: 5.19 us -> 6.66 us
  starting transfers between devices: 17.5 us -> 18.4 us
  waiting for transfers between devices: 15.3 us -> 14.7 us
    unnamed x16, local copies, waits for them, and re-layouts: 3.36 us -> 0.03 us
    pallas_call x3, Pallas kernels: 2.57 us -> 4.02 us  [the longest x2 2.99 us: prepare(): call(functools.partial(prepare_kernel, far, first, last, extra), name, tu...]
    ppermute x6, waiting for transfers between devices: 10.4 us -> 9.26 us  [along_far(): return lax.ppermute(block, 'far', [(i, i ^ k) for i in range(far)])]
    all_to_all x1, waiting for transfers between devices: 1.61 us -> 2.61 us  [local_pairs(): lax.all_to_all(back, ('far', 'near', 'col'), split_axis=0, concat_axis=0,...]
    ppermute x6, starting transfers between devices: 8.01 us -> 8.96 us  [along_far(): return lax.ppermute(block, 'far', [(i, i ^ k) for i in range(far)])]
    ppermute x4 -> x2, starting transfers between devices: 0.52 us -> 0.01 us  [local_pairs(): theirs = [lax.ppermute(block, 'col', swap) for block in ours[WHOLE:]]]
    ppermute x4 -> x2, waiting for transfers between devices: 0.91 us -> 0.49 us  [local_pairs(): theirs = [lax.ppermute(block, 'col', swap) for block in ours[WHOLE:]]]
  transfers between devices with their start and end apart: 14 -> 12, of which waited for: 9 -> 7; matrix products, arithmetic and copies ran while one was open for 0% -> 0% of each run, Pallas kernels for 8% -> 12%
where the time goes in v3:
time: 40.7 us; the launch traced here: 40.5 us
  starting transfers between devices  18.4 us (45%)
  waiting for transfers between devices  14.7 us (36%)
  Pallas kernels  6.66 us (16%)
  between operations  0.75 us (2%)
    ppermute x6, waiting for transfers between devices, along_far(): return lax.ppermute(block, 'far', [(i, i ^ k) for i in range(far)])  9.26 us
    ppermute x6, starting transfers between devices, along_far(): return lax.ppermute(block, 'far', [(i, i ^ k) for i in range(far)])  8.96 us
    all_to_all x1, starting transfers between devices, local_pairs(): lax.all_to_all(back, ('far', 'near', 'col'), split_axis=0, concat_axis=0,...  3.92 us
    ppermute x1, starting transfers between devices, local_pairs(): near_weight = lax.ppermute(expand_weight, 'near', swap)  3 us
    pallas_call x2, Pallas kernels, prepare(): call(functools.partial(prepare_kernel, far, first, last, extra), name, tu...  2.99 us
    all_to_all x1, waiting for transfers between devices, local_pairs(): lax.all_to_all(back, ('far', 'near', 'col'), split_axis=0, concat_axis=0,...  2.61 us
    ppermute x1, waiting for transfers between devices, local_pairs(): passed = lax.ppermute(pass_on, 'near', swap)  2.36 us
    ppermute x1, starting transfers between devices, local_pairs(): passed = lax.ppermute(pass_on, 'near', swap)  1.93 us
  transfers between devices with their start and end apart: 12, of which 7 were waited for; matrix products, arithmetic and copies ran while one was open for 0% of the time, Pallas kernels for 12%

profile of v3, /device:TPU:0, one launch (start us, length us, event | category | flops | bytes accessed | tf_op | source)
XLA Modules:
  0.0 40.5 jit_solution(3525927651899556659)
XLA Ops:
  0.6 0.0 copy-start
  0.6 3.0 %collective-permute-start.5 = (bf16[4,256,256]{2,1,0:T(8,128)(2,1)}, bf16[4,256,256]{2,1,0:T(8,128)(2,1)S(1)}, u32[]{:S(2)}, u32[]{:S(2)}) collective-permute-start(bf16[4,256,256]{2,1,0:T(8,128)(2,1)} %refs_6_.1), channel_id=1, source_target_pairs={{0,2},{2,0},{1,3},{3,1},{4,6},{6,4},{5,7},{7,5},{8,10},{10,8},{9,1... | collective-permute-start | bytes 1572872 | tf_op jit(solution)/shard_map/ppermute | solution.py:399
  3.6 0.0 copy-start.2
  3.6 0.0 copy-start.3
  3.6 2.3 %prepare.1 = (bf16[528,128]{1,0:T(8,128)(2,1)}, bf16[272,128]{1,0:T(8,128)(2,1)}, bf16[272,128]{1,0:T(8,128)(2,1)}) custom-call(s32[2,128]{1,0:T(2,128)} %refs_0_.3, s32[1,8]{1,0:T(1,128)} %bitcast.9, f32[2,2]{1,0:T(2,128)} %refs_2_.3, f32[16,256]{1,0:T(8,128)} %bitcast.5, f32[16,256]{1,0:T(8,128)} %bitcast.7, bf16[256,2048]{1,0:T(8,128)(2,1)} %refs_5_.3), custom_call_target="tpu_custom_call" | custom-call | flops 67108864 | bytes 1048576 | tf_op jit(solution)/shard_map/prepare/pallas_call | solution.py:404
  5.9 2.7 %collective-permute-start.1 = (bf16[272,128]{1,0:T(8,128)(2,1)}, bf16[272,128]{1,0:T(8,128)(2,1)S(1)}, u32[]{:S(2)}, u32[]{:S(2)}) collective-permute-start(bf16[272,128]{1,0:T(8,128)(2,1)} %get-tuple-element.26), channel_id=1, source_target_pairs={{0,8},{4,12},{8,0},{12,4},{1,9},{5,13},{9,1},{13,5},{2,10},{6,14},... | collective-permute-start | bytes 208904 | tf_op jit(solution)/shard_map/ppermute | solution.py:397
  8.6 0.0 copy-start.5
  8.6 0.0 copy-start.4
  8.6 0.0 copy-start.6
  8.6 1.3 %collective-permute-start.2 = (bf16[272,128]{1,0:T(8,128)(2,1)}, bf16[272,128]{1,0:T(8,128)(2,1)S(1)}, u32[]{:S(2)}, u32[]{:S(2)}) collective-permute-start(bf16[272,128]{1,0:T(8,128)(2,1)} %get-tuple-element.27), channel_id=1, source_target_pairs={{0,12},{4,8},{8,4},{12,0},{1,13},{5,9},{9,5},{13,1},{2,14},{6,10},... | collective-permute-start | bytes 208904 | tf_op jit(solution)/shard_map/ppermute | solution.py:397
  10.0 0.0 copy-start.7
  10.0 0.3 collective-permute-start
  10.3 0.5 %collective-permute-start.6 = (bf16[512,256]{1,0:T(8,128)(2,1)}, bf16[512,256]{1,0:T(8,128)(2,1)S(1)}, u32[]{:S(2)}, u32[]{:S(2)}) collective-permute-start(bf16[512,256]{1,0:T(8,128)(2,1)} %refs_4_.1), channel_id=1, source_target_pairs={{0,2},{2,0},{1,3},{3,1},{4,6},{6,4},{5,7},{7,5},{8,10},{10,8},{9,1... | collective-permute-start | bytes 786440 | tf_op jit(solution)/shard_map/ppermute | solution.py:428
  10.8 2.6 %collective-permute-done.1.refs_2_ = bf16[272,128]{1,0:T(8,128)(2,1)S(1)} collective-permute-done((bf16[272,128]{1,0:T(8,128)(2,1)}, bf16[272,128]{1,0:T(8,128)(2,1)S(1)}, u32[]{:S(2)}, u32[]{:S(2)}) %collective-permute-start.1) | collective-permute-done | bytes 69664 | tf_op jit(solution)/shard_map/ppermute | solution.py:397
  13.4 0.0 collective-permute-start.3
  13.4 2.1 %collective-permute-done.2.refs_3_ = bf16[272,128]{1,0:T(8,128)(2,1)S(1)} collective-permute-done((bf16[272,128]{1,0:T(8,128)(2,1)}, bf16[272,128]{1,0:T(8,128)(2,1)S(1)}, u32[]{:S(2)}, u32[]{:S(2)}) %collective-permute-start.2) | collective-permute-done | bytes 69664 | tf_op jit(solution)/shard_map/ppermute | solution.py:397
  15.6 0.0 collective-permute-start.4
  15.6 0.0 copy-done
  15.6 0.0 copy-done.2
  15.6 0.0 copy-done.3
  15.6 0.0 copy-done.5
  15.6 0.0 copy-done.4
  15.6 0.0 copy-done.6
  15.6 0.7 %prepare_own.1 = (bf16[528,128]{1,0:T(8,128)(2,1)S(1)}, f32[32,128]{1,0:T(8,128)S(1)}, bf16[256,128]{1,0:T(8,128)(2,1)S(1)}) custom-call(s32[2,128]{1,0:T(2,128)S(1)} %copy-done.4, s32[1,8]{1,0:T(1,128)S(1)} %bitcast.10, f32[2,2]{1,0:T(2,128)S(1)} %copy-done.5, f32[16,256]{1,0:T(8,128)S(1)} %bitcast.6, f32[16,256]{1,0:T(8,128)S(1)} %bitcast.8, ...), custom_call_target="tpu_custom_call" | custom-call | flops 67108864 | bytes 1048576 | tf_op jit(solution)/shard_map/prepare_own/pallas_call | solution.py:404
  16.3 0.0 collective-permute-done.refs_1_
  16.3 0.0 collective-permute-done.3.refs_4_
  16.3 0.5 %collective-permute-done.4.refs_5_ = bf16[272,128]{1,0:T(8,128)(2,1)S(1)} collective-permute-done((bf16[272,128]{1,0:T(8,128)(2,1)S(1)}, bf16[272,128]{1,0:T(8,128)(2,1)S(1)}, u32[]{:S(2)}, u32[]{:S(2)}) %collective-permute-start.4) | collective-permute-done | bytes 69664 | tf_op jit(solution)/shard_map/ppermute | solution.py:427
  16.8 0.0 collective-permute-done.5.refs_7_
  16.8 0.0 copy-done.7
  16.8 0.0 copy-start.1
  16.8 1.1 %project.1 = (f32[128,256]{1,0:T(8,128)S(1)}, s16[272,128]{1,0:T(8,128)(2,1)S(1)}, s16[272,128]{1,0:T(8,128)(2,1)S(1)}, s16[272,128]{1,0:T(8,128)(2,1)S(1)}) custom-call(bf16[528,128]{1,0:T(8,128)(2,1)S(1)} %get-tuple-element.24.refs_0_, bf16[528,128]{1,0:T(8,128)(2,1)S(1)} %collective-permute-done.refs_1_, ...), custom_call_target="tpu_custom_call" | custom-call | flops 1073741824 | bytes 2097152 | tf_op jit(solution)/shard_map/project/pallas_call | solution.py:430
  17.9 4.0 %collective-permute-start.7 = (s16[272,128]{1,0:T(8,128)(2,1)S(1)}, s16[272,128]{1,0:T(8,128)(2,1)S(1)}, u32[]{:S(2)}, u32[]{:S(2)}) collective-permute-start(s16[272,128]{1,0:T(8,128)(2,1)S(1)} %get-tuple-element.32), channel_id=1, source_target_pairs={{0,12},{4,8},{8,4},{12,0},{1,13},{5,9},{9,5},{13,1},{2,14},{6,10},... | collective-permute-start | bytes 208904 | tf_op jit(solution)/shard_map/ppermute | solution.py:397
  21.9 0.0 collective-permute-start.8
  21.9 0.6 %collective-permute-start.9 = (s16[272,128]{1,0:T(8,128)(2,1)S(1)}, s16[272,128]{1,0:T(8,128)(2,1)S(1)}, u32[]{:S(2)}, u32[]{:S(2)}) collective-permute-start(s16[272,128]{1,0:T(8,128)(2,1)S(1)} %get-tuple-element.34), channel_id=1, source_target_pairs={{0,4},{4,0},{8,12},{12,8},{1,5},{5,1},{9,13},{13,9},{2,6},{6,2},{1... | collective-permute-start | bytes 208904 | tf_op jit(solution)/shard_map/ppermute | solution.py:397
  22.6 0.0 collective-permute-done.6.refs_5_
  22.6 0.0 copy-done.1
  22.6 0.7 %lookup.1 = (f32[128,256]{1,0:T(8,128)S(1)}, f32[128,128]{1,0:T(8,128)S(1)}, f32[8,128]{1,0:T(8,128)S(1)}) custom-call(bf16[528,128]{1,0:T(8,128)(2,1)S(1)} %get-tuple-element.24.refs_0_, bf16[528,128]{1,0:T(8,128)(2,1)S(1)} %collective-permute-done.refs_1_, bf16[272,128]{1,0:T(8,128)(2,1)S(1)} %collective-permute-done.1.refs_2_, ...), custom_call_target="tpu_custom_call" | custom-call | flops 33554432 | bytes 524288 | tf_op jit(solution)/shard_map/lookup/pallas_call | solution.py:439
  23.2 1.6 %collective-permute-done.7.refs_4_ = s16[272,128]{1,0:T(8,128)(2,1)S(1)} collective-permute-done((s16[272,128]{1,0:T(8,128)(2,1)S(1)}, s16[272,128]{1,0:T(8,128)(2,1)S(1)}, u32[]{:S(2)}, u32[]{:S(2)}) %collective-permute-start.7) | collective-permute-done | bytes 69664 | tf_op jit(solution)/shard_map/ppermute | solution.py:397
  24.8 2.9 %collective-permute-done.8.refs_5_ = s16[272,128]{1,0:T(8,128)(2,1)S(1)} collective-permute-done((s16[272,128]{1,0:T(8,128)(2,1)S(1)}, s16[272,128]{1,0:T(8,128)(2,1)S(1)}, u32[]{:S(2)}, u32[]{:S(2)}) %collective-permute-start.8) | collective-permute-done | bytes 69664 | tf_op jit(solution)/shard_map/ppermute | solution.py:397
  27.7 0.0 collective-permute-done.9.refs_6_
  27.7 0.9 %reduce.1 = (bf16[64,256]{1,0:T(8,128)(2,1)S(1)}, bf16[80,256]{1,0:T(8,128)(2,1)S(1)}, f32[16,8,128]{2,1,0:T(8,128)}) custom-call(f32[128,256]{1,0:T(8,128)S(1)} %get-tuple-element.28.refs_0_, f32[128,256]{1,0:T(8,128)S(1)} %get-tuple-element.29.refs_1_, f32[128,128]{1,0:T(8,128)S(1)} %get-tuple-element.30.refs_2_, ...), custom_call_target="tpu_custom_call" | custom-call | flops 262144 | bytes 327680 | tf_op jit(solution)/shard_map/reduce/pallas_call | solution.py:447
  28.6 3.9 %all-to-all-start = ((f32[16,8,128]{2,1,0:T(8,128)}), f32[16,8,128]{2,1,0:T(8,128)S(1)}, u32[]{:S(2)}, u32[]{:S(2)}) async-start(f32[16,8,128]{2,1,0:T(8,128)} %get-tuple-element.37), calls=%async_computation | async-start | bytes 131072 | tf_op jit(solution)/shard_map/all_to_all | solution.py:459
  32.6 1.9 %collective-permute-start.10 = (bf16[80,256]{1,0:T(8,128)(2,1)S(1)}, bf16[80,256]{1,0:T(8,128)(2,1)S(1)}, u32[]{:S(2)}, u32[]{:S(2)}) collective-permute-start(bf16[80,256]{1,0:T(8,128)(2,1)S(1)} %get-tuple-element.36), channel_id=1, source_target_pairs={{0,2},{2,0},{1,3},{3,1},{4,6},{6,4},{5,7},{7,5},{8,10},{10,8},{9,1... | collective-permute-start | bytes 122888 | tf_op jit(solution)/shard_map/ppermute | solution.py:460
  34.5 2.4 %collective-permute-done.10.passed = bf16[80,256]{1,0:T(8,128)(2,1)S(1)} collective-permute-done((bf16[80,256]{1,0:T(8,128)(2,1)S(1)}, bf16[80,256]{1,0:T(8,128)(2,1)S(1)}, u32[]{:S(2)}, u32[]{:S(2)}) %collective-permute-start.10) | collective-permute-done | bytes 40992 | tf_op jit(solution)/shard_map/ppermute | solution.py:460
  36.9 2.6 %all-to-all-done.back = f32[16,8,128]{2,1,0:T(8,128)S(1)} async-done(((f32[16,8,128]{2,1,0:T(8,128)}), f32[16,8,128]{2,1,0:T(8,128)S(1)}, u32[]{:S(2)}, u32[]{:S(2)}) %all-to-all-start) | async-done | bytes 65568 | tf_op jit(solution)/shard_map/all_to_all | solution.py:459
  39.5 1.0 %outputs.1 = (f32[512,256]{1,0:T(8,128)}, f32[16,256]{1,0:T(8,128)}, f32[16,256]{1,0:T(8,128)}, f32[2,2]{1,0:T(2,128)}) custom-call(bf16[64,256]{1,0:T(8,128)(2,1)S(1)} %get-tuple-element.35.contrib, bf16[80,256]{1,0:T(8,128)(2,1)S(1)} %collective-permute-done.10.passed, f32[8,128]{1,0:T(8,128)S(1)} %get-tuple-element.31.refs_3_.value_rows, ...), custom_call_target="tpu_custom_call" | custom-call | flops 33554432 | bytes 524288 | tf_op jit(solution)/shard_map/outputs/pallas_call | solution.py:461
Async XLA Ops:
  0.6 14.9 %copy-start = (bf16[256,2048]{1,0:T(8,128)(2,1)S(1)}, bf16[256,2048]{1,0:T(8,128)(2,1)}, u32[]{:S(2)}) copy-start(bf16[256,2048]{1,0:T(8,128)(2,1)} %refs_5_.3) | copy-start | bytes 3145732
  0.6 16.2 %collective-permute-start.5 = (bf16[4,256,256]{2,1,0:T(8,128)(2,1)}, bf16[4,256,256]{2,1,0:T(8,128)(2,1)S(1)}, u32[]{:S(2)}, u32[]{:S(2)}) collective-permute-start(bf16[4,256,256]{2,1,0:T(8,128)(2,1)} %refs_6_.1), channel_id=1, source_target_pairs={{0,2},{2,0},{1,3},{3,1},{4,6},{6,4},{5,7},{7,5},{8,10},{10,8},{9,1... | collective-permute-start | bytes 1572872 | tf_op jit(solution)/shard_map/ppermute | solution.py:399
  3.6 11.9 %copy-start.2 = (f32[256,16]{0,1:T(8,128)S(1)}, f32[256,16]{0,1:T(8,128)}, u32[]{:S(2)}) copy-start(f32[256,16]{0,1:T(8,128)} %param.11) | copy-start | bytes 49156
  3.6 11.9 %copy-start.3 = (f32[256,16]{0,1:T(8,128)S(1)}, f32[256,16]{0,1:T(8,128)}, u32[]{:S(2)}) copy-start(f32[256,16]{0,1:T(8,128)} %param.12) | copy-start | bytes 49156
  5.9 7.5 %collective-permute-start.1 = (bf16[272,128]{1,0:T(8,128)(2,1)}, bf16[272,128]{1,0:T(8,128)(2,1)S(1)}, u32[]{:S(2)}, u32[]{:S(2)}) collective-permute-start(bf16[272,128]{1,0:T(8,128)(2,1)} %get-tuple-element.26), channel_id=1, source_target_pairs={{0,8},{4,12},{8,0},{12,4},{1,9},{5,13},{9,1},{13,5},{2,10},{6,14},... | collective-permute-start | bytes 208904 | tf_op jit(solution)/shard_map/ppermute | solution.py:397
  8.6 7.0 %copy-start.5 = (f32[2,2]{1,0:T(2,128)S(1)}, f32[2,2]{1,0:T(2,128)}, u32[]{:S(2)}) copy-start(f32[2,2]{1,0:T(2,128)} %refs_2_.3) | copy-start | bytes 52
  8.6 7.0 %copy-start.4 = (s32[2,128]{1,0:T(2,128)S(1)}, s32[2,128]{1,0:T(2,128)}, u32[]{:S(2)}) copy-start(s32[2,128]{1,0:T(2,128)} %refs_0_.3) | copy-start | bytes 3076
  8.6 7.0 %copy-start.6 = (s32[8]{0:T(128)S(1)}, s32[8]{0:T(128)}, u32[]{:S(2)}) copy-start(s32[8]{0:T(128)} %param.15) | copy-start | bytes 100
  8.6 6.9 %collective-permute-start.2 = (bf16[272,128]{1,0:T(8,128)(2,1)}, bf16[272,128]{1,0:T(8,128)(2,1)S(1)}, u32[]{:S(2)}, u32[]{:S(2)}) collective-permute-start(bf16[272,128]{1,0:T(8,128)(2,1)} %get-tuple-element.27), channel_id=1, source_target_pairs={{0,12},{4,8},{8,4},{12,0},{1,13},{5,9},{9,5},{13,1},{2,14},{6,10},... | collective-permute-start | bytes 208904 | tf_op jit(solution)/shard_map/ppermute | solution.py:397
  10.0 6.9 %copy-start.7 = (bf16[4,256,256]{2,1,0:T(8,128)(2,1)S(1)}, bf16[4,256,256]{2,1,0:T(8,128)(2,1)}, u32[]{:S(2)}) copy-start(bf16[4,256,256]{2,1,0:T(8,128)(2,1)} %refs_6_.1) | copy-start | bytes 1572868
  10.0 6.4 %collective-permute-start = (bf16[528,128]{1,0:T(8,128)(2,1)}, bf16[528,128]{1,0:T(8,128)(2,1)S(1)}, u32[]{:S(2)}, u32[]{:S(2)}) collective-permute-start(bf16[528,128]{1,0:T(8,128)(2,1)} %get-tuple-element.25), channel_id=1, source_target_pairs={{0,4},{4,0},{8,12},{12,8},{1,5},{5,1},{9,13},{13,9},{2,6},{6,2},{1... | collective-permute-start | bytes 405512 | tf_op jit(solution)/shard_map/ppermute | solution.py:397
  10.3 12.3 %collective-permute-start.6 = (bf16[512,256]{1,0:T(8,128)(2,1)}, bf16[512,256]{1,0:T(8,128)(2,1)S(1)}, u32[]{:S(2)}, u32[]{:S(2)}) collective-permute-start(bf16[512,256]{1,0:T(8,128)(2,1)} %refs_4_.1), channel_id=1, source_target_pairs={{0,2},{2,0},{1,3},{3,1},{4,6},{6,4},{5,7},{7,5},{8,10},{10,8},{9,1... | collective-permute-start | bytes 786440 | tf_op jit(solution)/shard_map/ppermute | solution.py:428
  13.4 2.9 %collective-permute-start.3 = (bf16[272,128]{1,0:T(8,128)(2,1)S(1)}, bf16[272,128]{1,0:T(8,128)(2,1)S(1)}, u32[]{:S(2)}, u32[]{:S(2)}) collective-permute-start(bf16[272,128]{1,0:T(8,128)(2,1)S(1)} %collective-permute-done.1.refs_2_), channel_id=1, source_target_pairs={{0,1},{1,0},{2,3},{3,2},{4,5},{5,4},{6,7},{7,6},{8,9},{9,8},{10,11... | collective-permute-start | bytes 208904 | tf_op jit(solution)/shard_map/ppermute | solution.py:427
  15.6 1.3 %collective-permute-start.4 = (bf16[272,128]{1,0:T(8,128)(2,1)S(1)}, bf16[272,128]{1,0:T(8,128)(2,1)S(1)}, u32[]{:S(2)}, u32[]{:S(2)}) collective-permute-start(bf16[272,128]{1,0:T(8,128)(2,1)S(1)} %collective-permute-done.2.refs_3_), channel_id=1, source_target_pairs={{0,1},{1,0},{2,3},{3,2},{4,5},{5,4},{6,7},{7,6},{8,9},{9,8},{10,11... | collective-permute-start | bytes 208904 | tf_op jit(solution)/shard_map/ppermute | solution.py:427
  16.8 5.7 %copy-start.1 = (bf16[512,256]{1,0:T(8,128)(2,1)S(1)}, bf16[512,256]{1,0:T(8,128)(2,1)}, u32[]{:S(2)}) copy-start(bf16[512,256]{1,0:T(8,128)(2,1)} %refs_4_.1) | copy-start | bytes 786436
  17.9 6.9 %collective-permute-start.7 = (s16[272,128]{1,0:T(8,128)(2,1)S(1)}, s16[272,128]{1,0:T(8,128)(2,1)S(1)}, u32[]{:S(2)}, u32[]{:S(2)}) collective-permute-start(s16[272,128]{1,0:T(8,128)(2,1)S(1)} %get-tuple-element.32), channel_id=1, source_target_pairs={{0,12},{4,8},{8,4},{12,0},{1,13},{5,9},{9,5},{13,1},{2,14},{6,10},... | collective-permute-start | bytes 208904 | tf_op jit(solution)/shard_map/ppermute | solution.py:397
  21.9 5.8 %collective-permute-start.8 = (s16[272,128]{1,0:T(8,128)(2,1)S(1)}, s16[272,128]{1,0:T(8,128)(2,1)S(1)}, u32[]{:S(2)}, u32[]{:S(2)}) collective-permute-start(s16[272,128]{1,0:T(8,128)(2,1)S(1)} %get-tuple-element.33), channel_id=1, source_target_pairs={{0,8},{4,12},{8,0},{12,4},{1,9},{5,13},{9,1},{13,5},{2,10},{6,14},... | collective-permute-start | bytes 208904 | tf_op jit(solution)/shard_map/ppermute | solution.py:397
  21.9 5.8 %collective-permute-start.9 = (s16[272,128]{1,0:T(8,128)(2,1)S(1)}, s16[272,128]{1,0:T(8,128)(2,1)S(1)}, u32[]{:S(2)}, u32[]{:S(2)}) collective-permute-start(s16[272,128]{1,0:T(8,128)(2,1)S(1)} %get-tuple-element.34), channel_id=1, source_target_pairs={{0,4},{4,0},{8,12},{12,8},{1,5},{5,1},{9,13},{13,9},{2,6},{6,2},{1... | collective-permute-start | bytes 208904 | tf_op jit(solution)/shard_map/ppermute | solution.py:397
  28.6 10.8 %all-to-all-start = ((f32[16,8,128]{2,1,0:T(8,128)}), f32[16,8,128]{2,1,0:T(8,128)S(1)}, u32[]{:S(2)}, u32[]{:S(2)}) async-start(f32[16,8,128]{2,1,0:T(8,128)} %get-tuple-element.37), calls=%async_computation | async-start | bytes 131072 | tf_op jit(solution)/shard_map/all_to_all | solution.py:459
  32.6 4.3 %collective-permute-start.10 = (bf16[80,256]{1,0:T(8,128)(2,1)S(1)}, bf16[80,256]{1,0:T(8,128)(2,1)S(1)}, u32[]{:S(2)}, u32[]{:S(2)}) collective-permute-start(bf16[80,256]{1,0:T(8,128)(2,1)S(1)} %get-tuple-element.36), channel_id=1, source_target_pairs={{0,2},{2,0},{1,3},{3,1},{4,6},{6,4},{5,7},{7,5},{8,10},{10,8},{9,1... | collective-permute-start | bytes 122888 | tf_op jit(solution)/shard_map/ppermute | solution.py:460

commit v4 on v3

--- a/solution.py
+++ b/solution.py
@@ -332,7 +332,7 @@
         back[k] = block
 
 
-def output_kernel(far, contrib, passed, value_rows, back, scaled, hits, *outs):
+def output_kernel(far, order, contrib, passed, value_rows, back, scaled, hits, *outs):
     out, row_out, col_out, core_out = outs
     half = contrib.shape[0]
     rows = 2 * half
@@ -346,7 +346,8 @@
     line = iota(back.shape[1:], 0)
     total = jnp.zeros(back.shape[1:], F32)
     for k in range(back.shape[0]):
-        mine = jnp.logical_and(line == (k // 4 ^ z), k // 2 % 2 == x)
+        sender = order[k]
+        mine = jnp.logical_and(line == (sender // 4 ^ z), sender // 2 % 2 == x)
         total = total + jnp.where(jnp.logical_or(mine, line == far), back[k], 0.0)
     dscore = jnp.sum(total[:far], axis=0, keepdims=True)
     outer = total[far : far + 1]
@@ -398,6 +399,8 @@
 
     near_weight = lax.ppermute(expand_weight, "near", swap)
     blocks = [shape(((4 if k < WHOLE else 2) * rows + RECORD, 128), BF16) for k in range(far)]
+
+    operands = (pair_index, counts.reshape(1, nmem), core, row_factors.T, col_factors.T, grads)
 
     def prepare(name, first, last, extra, limit):
         extras = (shape((factors, rows), F32), shape((tokens, rows), BF16)) if extra else ()
@@ -418,10 +421,10 @@
                 pltpu.SemaphoreType.DMA((6,)),
             ),
             limit,
-        )(pair_index, counts.reshape(1, nmem), core, row_factors.T, col_factors.T, grads)
-
-    sends = (None,) + tuple(prepare("prepare", 1, far, False, 60))
-    own_block, scaled, hits = prepare("prepare_own", 0, 1, True, 24)
+        )(*(pltpu.with_memory_space_constraint(a, pltpu.HBM) for a in operands))
+
+    own_block, *sends, scaled, hits = prepare("prepare", 0, far, True, 24)
+    sends = [None] + sends
     got = {k: along_far(sends[k], k) for k in reversed(range(1, far))}
     ours = [own_block] + [got[k] for k in range(1, far)]
     theirs = [lax.ppermute(block, "col", swap) for block in ours[WHOLE:]]
@@ -456,10 +459,19 @@
         8 * rows * width,
         10 * rows * width,
     )(whole, fetched, records, value_rows, *coded)
-    back = lax.all_to_all(back, ("far", "near", "col"), split_axis=0, concat_axis=0, tiled=True)
+    fars = [*range(far // 2 - 1, far), *range(far // 2 - 1)]
+    order = [4 * z + k for z in fars for k in (3, 2, 1, 0)]
+    back = lax.all_to_all(
+        back,
+        ("far", "near", "col"),
+        split_axis=0,
+        concat_axis=0,
+        axis_index_groups=[order],
+        tiled=True,
+    )
     passed = lax.ppermute(pass_on, "near", swap)
     value_grad, row_grad, col_grad, core_grad = call(
-        functools.partial(output_kernel, far),
+        functools.partial(output_kernel, far, order),
         "outputs",
         (
             shape((vrows, width), F32),

time: 40.7 us -> 38.2 us (0.939)
  Pallas kernels: 6.66 us -> 5.39 us
  waiting for transfers between devices: 14.7 us -> 14.1 us
  starting transfers between devices: 18.4 us -> 17.8 us
    all_to_all x1, waiting for transfers between devices: 2.61 us -> 0.1 us  [local_pairs(): lax.all_to_all(back, ('far', 'near', 'col'), split_axis=0, concat_axis=0,...]
    ppermute x1, starting transfers between devices: 1.93 us -> 0.56 us  [local_pairs(): passed = lax.ppermute(pass_on, 'near', swap)]
    pallas_call x2 -> x1, Pallas kernels: 2.99 us -> 1.73 us  [prepare(): call(functools.partial(prepare_kernel, far, first, last, extra), name, tu...]
    ppermute x1, waiting for transfers between devices: 2.36 us -> 3.53 us  [local_pairs(): passed = lax.ppermute(pass_on, 'near', swap)]
    all_to_all x1, starting transfers between devices: 3.92 us -> 4.61 us  [local_pairs(): lax.all_to_all(back, ('far', 'near', 'col'), split_axis=0, concat_axis=0,...]
    ppermute x1, waiting for transfers between devices: 0.01 us -> 0.55 us  [local_pairs(): near_weight = lax.ppermute(expand_weight, 'near', swap)]
  transfers between devices with their start and end apart: 12 -> 12, of which waited for: 7 -> 9; matrix products, arithmetic and copies ran while one was open for 0% -> 0% of each run, Pallas kernels for 12% -> 9%
where the time goes in v4:
time: 38.2 us; the launch traced here: 38 us
  starting transfers between devices  17.8 us (47%)
  waiting for transfers between devices  14.1 us (37%)
  Pallas kernels  5.39 us (14%)
  between operations  0.67 us (2%)
    ppermute x6, waiting for transfers between devices, along_far(): return lax.ppermute(block, 'far', [(i, i ^ k) for i in range(far)])  9.34 us
    ppermute x6, starting transfers between devices, along_far(): return lax.ppermute(block, 'far', [(i, i ^ k) for i in range(far)])  9.12 us
    all_to_all x1, starting transfers between devices, local_pairs(): lax.all_to_all(back, ('far', 'near', 'col'), split_axis=0, concat_axis=0,...  4.61 us
    ppermute x1, waiting for transfers between devices, local_pairs(): passed = lax.ppermute(pass_on, 'near', swap)  3.53 us
    ppermute x1, starting transfers between devices, local_pairs(): near_weight = lax.ppermute(expand_weight, 'near', swap)  3 us
    pallas_call x1, Pallas kernels, prepare(): call(functools.partial(prepare_kernel, far, first, last, extra), name, tu...  1.73 us
    pallas_call x1, Pallas kernels, local_pairs(): call(functools.partial(project_kernel, far), 'project', (shape((rows, wid...  1.06 us
    pallas_call x1, Pallas kernels, local_pairs(): call(functools.partial(output_kernel, far, order), 'outputs', (shape((vro...  1.03 us
  transfers between devices with their start and end apart: 12, of which 9 were waited for; matrix products, arithmetic and copies ran while one was open for 0% of the time, Pallas kernels for 9%

profile of v4, /device:TPU:0, one launch (start us, length us, event | category | flops | bytes accessed | tf_op | source)
XLA Modules:
  0.0 38.0 jit_solution(16952464145287429335)
XLA Ops:
  0.6 3.0 %collective-permute-start.5 = (bf16[4,256,256]{2,1,0:T(8,128)(2,1)}, bf16[4,256,256]{2,1,0:T(8,128)(2,1)S(1)}, u32[]{:S(2)}, u32[]{:S(2)}) collective-permute-start(bf16[4,256,256]{2,1,0:T(8,128)(2,1)} %refs_6_.1), channel_id=1, source_target_pairs={{0,2},{2,0},{1,3},{3,1},{4,6},{6,4},{5,7},{7,5},{8,10},{10,8},{9,1... | collective-permute-start | bytes 1572872 | tf_op jit(solution)/shard_map/ppermute | solution.py:400
  3.6 0.0 copy-start
  3.6 0.0 copy-start.1
  3.6 1.7 %prepare.1 = (bf16[528,128]{1,0:T(8,128)(2,1)S(1)}, bf16[528,128]{1,0:T(8,128)(2,1)S(1)}, bf16[272,128]{1,0:T(8,128)(2,1)S(1)}, bf16[272,128]{1,0:T(8,128)(2,1)S...) custom-call(s32[2,128]{1,0:T(2,128)} %refs_0_.1, s32[1,8]{1,0:T(1,128)} %bitcast.7, f32[2,2]{1,0:T(2,128)} %refs_2_.1, ...), custom_call_target="tpu_custom_call" | custom-call | flops 67108864 | bytes 1048576 | tf_op jit(solution)/shard_map/prepare/pallas_call | solution.py:407
  5.4 2.7 %collective-permute-start.1 = (bf16[272,128]{1,0:T(8,128)(2,1)S(1)}, bf16[272,128]{1,0:T(8,128)(2,1)S(1)}, u32[]{:S(2)}, u32[]{:S(2)}) collective-permute-start(bf16[272,128]{1,0:T(8,128)(2,1)S(1)} %get-tuple-element.26), channel_id=1, source_target_pairs={{0,8},{4,12},{8,0},{12,4},{1,9},{5,13},{9,1},{13,5},{2,10},{6,14},... | collective-permute-start | bytes 208904 | tf_op jit(solution)/shard_map/ppermute | solution.py:398
  8.0 1.3 %collective-permute-start.2 = (bf16[272,128]{1,0:T(8,128)(2,1)S(1)}, bf16[272,128]{1,0:T(8,128)(2,1)S(1)}, u32[]{:S(2)}, u32[]{:S(2)}) collective-permute-start(bf16[272,128]{1,0:T(8,128)(2,1)S(1)} %get-tuple-element.27), channel_id=1, source_target_pairs={{0,12},{4,8},{8,4},{12,0},{1,13},{5,9},{9,5},{13,1},{2,14},{6,10},... | collective-permute-start | bytes 208904 | tf_op jit(solution)/shard_map/ppermute | solution.py:398
  9.4 0.2 collective-permute-start
  9.6 0.0 copy-done
  9.6 0.5 %collective-permute-start.6 = (bf16[512,256]{1,0:T(8,128)(2,1)S(1)}, bf16[512,256]{1,0:T(8,128)(2,1)S(1)}, u32[]{:S(2)}, u32[]{:S(2)}) collective-permute-start(bf16[512,256]{1,0:T(8,128)(2,1)S(1)} %copy-done), channel_id=1, source_target_pairs={{0,2},{2,0},{1,3},{3,1},{4,6},{6,4},{5,7},{7,5},{8,10},{10,8},{9,1... | collective-permute-start | bytes 786440 | tf_op jit(solution)/shard_map/ppermute | solution.py:431
  10.1 2.5 %collective-permute-done.1.refs_2_ = bf16[272,128]{1,0:T(8,128)(2,1)S(1)} collective-permute-done((bf16[272,128]{1,0:T(8,128)(2,1)S(1)}, bf16[272,128]{1,0:T(8,128)(2,1)S(1)}, u32[]{:S(2)}, u32[]{:S(2)}) %collective-permute-start.1) | collective-permute-done | bytes 69664 | tf_op jit(solution)/shard_map/ppermute | solution.py:398
  12.6 0.0 collective-permute-start.3
  12.6 2.1 %collective-permute-done.2.refs_3_ = bf16[272,128]{1,0:T(8,128)(2,1)S(1)} collective-permute-done((bf16[272,128]{1,0:T(8,128)(2,1)S(1)}, bf16[272,128]{1,0:T(8,128)(2,1)S(1)}, u32[]{:S(2)}, u32[]{:S(2)}) %collective-permute-start.2) | collective-permute-done | bytes 69664 | tf_op jit(solution)/shard_map/ppermute | solution.py:398
  14.8 0.0 collective-permute-start.4
  14.8 0.6 %collective-permute-done.refs_1_ = bf16[528,128]{1,0:T(8,128)(2,1)S(1)} collective-permute-done((bf16[528,128]{1,0:T(8,128)(2,1)S(1)}, bf16[528,128]{1,0:T(8,128)(2,1)S(1)}, u32[]{:S(2)}, u32[]{:S(2)}) %collective-permute-start) | collective-permute-done | bytes 135200 | tf_op jit(solution)/shard_map/ppermute | solution.py:398
  15.4 0.0 collective-permute-done.3.refs_4_
  15.4 0.6 %collective-permute-done.4.refs_5_ = bf16[272,128]{1,0:T(8,128)(2,1)S(1)} collective-permute-done((bf16[272,128]{1,0:T(8,128)(2,1)S(1)}, bf16[272,128]{1,0:T(8,128)(2,1)S(1)}, u32[]{:S(2)}, u32[]{:S(2)}) %collective-permute-start.4) | collective-permute-done | bytes 69664 | tf_op jit(solution)/shard_map/ppermute | solution.py:430
  16.0 0.6 %collective-permute-done.5.refs_7_ = bf16[4,256,256]{2,1,0:T(8,128)(2,1)S(1)} collective-permute-done((bf16[4,256,256]{2,1,0:T(8,128)(2,1)}, bf16[4,256,256]{2,1,0:T(8,128)(2,1)S(1)}, u32[]{:S(2)}, u32[]{:S(2)}) %collective-permute-start.5) | collective-permute-done | bytes 524320 | tf_op jit(solution)/shard_map/ppermute | solution.py:400
  16.6 0.0 copy-done.1
  16.6 1.1 %project.1 = (f32[128,256]{1,0:T(8,128)S(1)}, s16[272,128]{1,0:T(8,128)(2,1)S(1)}, s16[272,128]{1,0:T(8,128)(2,1)S(1)}, s16[272,128]{1,0:T(8,128)(2,1)S(1)}) custom-call(bf16[528,128]{1,0:T(8,128)(2,1)S(1)} %get-tuple-element.24.refs_0_, bf16[528,128]{1,0:T(8,128)(2,1)S(1)} %collective-permute-done.refs_1_, ...), custom_call_target="tpu_custom_call" | custom-call | flops 1073741824 | bytes 2097152 | tf_op jit(solution)/shard_map/project/pallas_call | solution.py:433
  17.7 4.2 %collective-permute-start.7 = (s16[272,128]{1,0:T(8,128)(2,1)S(1)}, s16[272,128]{1,0:T(8,128)(2,1)S(1)}, u32[]{:S(2)}, u32[]{:S(2)}) collective-permute-start(s16[272,128]{1,0:T(8,128)(2,1)S(1)} %get-tuple-element.32), channel_id=1, source_target_pairs={{0,12},{4,8},{8,4},{12,0},{1,13},{5,9},{9,5},{13,1},{2,14},{6,10},... | collective-permute-start | bytes 208904 | tf_op jit(solution)/shard_map/ppermute | solution.py:398
  21.9 0.0 collective-permute-start.8
  21.9 0.6 %collective-permute-start.9 = (s16[272,128]{1,0:T(8,128)(2,1)S(1)}, s16[272,128]{1,0:T(8,128)(2,1)S(1)}, u32[]{:S(2)}, u32[]{:S(2)}) collective-permute-start(s16[272,128]{1,0:T(8,128)(2,1)S(1)} %get-tuple-element.34), channel_id=1, source_target_pairs={{0,4},{4,0},{8,12},{12,8},{1,5},{5,1},{9,13},{13,9},{2,6},{6,2},{1... | collective-permute-start | bytes 208904 | tf_op jit(solution)/shard_map/ppermute | solution.py:398
  22.5 0.0 collective-permute-done.6.refs_5_
  22.6 0.7 %lookup.1 = (f32[128,256]{1,0:T(8,128)S(1)}, f32[128,128]{1,0:T(8,128)S(1)}, f32[8,128]{1,0:T(8,128)S(1)}) custom-call(bf16[528,128]{1,0:T(8,128)(2,1)S(1)} %get-tuple-element.24.refs_0_, bf16[528,128]{1,0:T(8,128)(2,1)S(1)} %collective-permute-done.refs_1_, bf16[272,128]{1,0:T(8,128)(2,1)S(1)} %collective-permute-done.1.refs_2_, ...), custom_call_target="tpu_custom_call" | custom-call | flops 33554432 | bytes 524288 | tf_op jit(solution)/shard_map/lookup/pallas_call | solution.py:442
  23.2 1.3 %collective-permute-done.7.refs_4_ = s16[272,128]{1,0:T(8,128)(2,1)S(1)} collective-permute-done((s16[272,128]{1,0:T(8,128)(2,1)S(1)}, s16[272,128]{1,0:T(8,128)(2,1)S(1)}, u32[]{:S(2)}, u32[]{:S(2)}) %collective-permute-start.7) | collective-permute-done | bytes 69664 | tf_op jit(solution)/shard_map/ppermute | solution.py:398
  24.5 2.8 %collective-permute-done.8.refs_5_ = s16[272,128]{1,0:T(8,128)(2,1)S(1)} collective-permute-done((s16[272,128]{1,0:T(8,128)(2,1)S(1)}, s16[272,128]{1,0:T(8,128)(2,1)S(1)}, u32[]{:S(2)}, u32[]{:S(2)}) %collective-permute-start.8) | collective-permute-done | bytes 69664 | tf_op jit(solution)/shard_map/ppermute | solution.py:398
  27.3 0.0 collective-permute-done.9.refs_6_
  27.3 0.9 %reduce.1 = (bf16[64,256]{1,0:T(8,128)(2,1)S(1)}, bf16[80,256]{1,0:T(8,128)(2,1)S(1)}, f32[16,8,128]{2,1,0:T(8,128)}) custom-call(f32[128,256]{1,0:T(8,128)S(1)} %get-tuple-element.28.refs_0_, f32[128,256]{1,0:T(8,128)S(1)} %get-tuple-element.29.refs_1_, f32[128,128]{1,0:T(8,128)S(1)} %get-tuple-element.30.refs_2_, ...), custom_call_target="tpu_custom_call" | custom-call | flops 262144 | bytes 327680 | tf_op jit(solution)/shard_map/reduce/pallas_call | solution.py:450
  28.2 4.6 %all-to-all-start = ((f32[16,8,128]{2,1,0:T(8,128)}), f32[16,8,128]{2,1,0:T(8,128)S(1)}, u32[]{:S(2)}, u32[]{:S(2)}) async-start(f32[16,8,128]{2,1,0:T(8,128)} %get-tuple-element.37), calls=%async_computation | async-start | bytes 131072 | tf_op jit(solution)/shard_map/all_to_all | solution.py:464
  32.8 0.6 %collective-permute-start.10 = (bf16[80,256]{1,0:T(8,128)(2,1)S(1)}, bf16[80,256]{1,0:T(8,128)(2,1)S(1)}, u32[]{:S(2)}, u32[]{:S(2)}) collective-permute-start(bf16[80,256]{1,0:T(8,128)(2,1)S(1)} %get-tuple-element.36), channel_id=1, source_target_pairs={{0,2},{2,0},{1,3},{3,1},{4,6},{6,4},{5,7},{7,5},{8,10},{10,8},{9,1... | collective-permute-start | bytes 122888 | tf_op jit(solution)/shard_map/ppermute | solution.py:472
  33.4 3.5 %collective-permute-done.10.passed = bf16[80,256]{1,0:T(8,128)(2,1)S(1)} collective-permute-done((bf16[80,256]{1,0:T(8,128)(2,1)S(1)}, bf16[80,256]{1,0:T(8,128)(2,1)S(1)}, u32[]{:S(2)}, u32[]{:S(2)}) %collective-permute-start.10) | collective-permute-done | bytes 40992 | tf_op jit(solution)/shard_map/ppermute | solution.py:472
  36.9 0.1 all-to-all-done.back
  37.0 1.0 %outputs.1 = (f32[512,256]{1,0:T(8,128)}, f32[16,256]{1,0:T(8,128)}, f32[16,256]{1,0:T(8,128)}, f32[2,2]{1,0:T(2,128)}) custom-call(bf16[64,256]{1,0:T(8,128)(2,1)S(1)} %get-tuple-element.35.contrib, bf16[80,256]{1,0:T(8,128)(2,1)S(1)} %collective-permute-done.10.passed, f32[8,128]{1,0:T(8,128)S(1)} %get-tuple-element.31.refs_3_.value_rows, ...), custom_call_target="tpu_custom_call" | custom-call | flops 33554432 | bytes 524288 | tf_op jit(solution)/shard_map/outputs/pallas_call | solution.py:473
Async XLA Ops:
  0.6 16.0 %collective-permute-start.5 = (bf16[4,256,256]{2,1,0:T(8,128)(2,1)}, bf16[4,256,256]{2,1,0:T(8,128)(2,1)S(1)}, u32[]{:S(2)}, u32[]{:S(2)}) collective-permute-start(bf16[4,256,256]{2,1,0:T(8,128)(2,1)} %refs_6_.1), channel_id=1, source_target_pairs={{0,2},{2,0},{1,3},{3,1},{4,6},{6,4},{5,7},{7,5},{8,10},{10,8},{9,1... | collective-permute-start | bytes 1572872 | tf_op jit(solution)/shard_map/ppermute | solution.py:400
  3.6 6.0 %copy-start = (bf16[512,256]{1,0:T(8,128)(2,1)S(1)}, bf16[512,256]{1,0:T(8,128)(2,1)}, u32[]{:S(2)}) copy-start(bf16[512,256]{1,0:T(8,128)(2,1)} %refs_4_.1) | copy-start | bytes 786436
  3.6 13.0 %copy-start.1 = (bf16[4,256,256]{2,1,0:T(8,128)(2,1)S(1)}, bf16[4,256,256]{2,1,0:T(8,128)(2,1)}, u32[]{:S(2)}) copy-start(bf16[4,256,256]{2,1,0:T(8,128)(2,1)} %refs_6_.1) | copy-start | bytes 1572868
  5.4 7.3 %collective-permute-start.1 = (bf16[272,128]{1,0:T(8,128)(2,1)S(1)}, bf16[272,128]{1,0:T(8,128)(2,1)S(1)}, u32[]{:S(2)}, u32[]{:S(2)}) collective-permute-start(bf16[272,128]{1,0:T(8,128)(2,1)S(1)} %get-tuple-element.26), channel_id=1, source_target_pairs={{0,8},{4,12},{8,0},{12,4},{1,9},{5,13},{9,1},{13,5},{2,10},{6,14},... | collective-permute-start | bytes 208904 | tf_op jit(solution)/shard_map/ppermute | solution.py:398
  8.0 6.7 %collective-permute-start.2 = (bf16[272,128]{1,0:T(8,128)(2,1)S(1)}, bf16[272,128]{1,0:T(8,128)(2,1)S(1)}, u32[]{:S(2)}, u32[]{:S(2)}) collective-permute-start(bf16[272,128]{1,0:T(8,128)(2,1)S(1)} %get-tuple-element.27), channel_id=1, source_target_pairs={{0,12},{4,8},{8,4},{12,0},{1,13},{5,9},{9,5},{13,1},{2,14},{6,10},... | collective-permute-start | bytes 208904 | tf_op jit(solution)/shard_map/ppermute | solution.py:398
  9.4 6.0 %collective-permute-start = (bf16[528,128]{1,0:T(8,128)(2,1)S(1)}, bf16[528,128]{1,0:T(8,128)(2,1)S(1)}, u32[]{:S(2)}, u32[]{:S(2)}) collective-permute-start(bf16[528,128]{1,0:T(8,128)(2,1)S(1)} %get-tuple-element.25), channel_id=1, source_target_pairs={{0,4},{4,0},{8,12},{12,8},{1,5},{5,1},{9,13},{13,9},{2,6},{6,2},{1... | collective-permute-start | bytes 405512 | tf_op jit(solution)/shard_map/ppermute | solution.py:398
  9.6 12.9 %collective-permute-start.6 = (bf16[512,256]{1,0:T(8,128)(2,1)S(1)}, bf16[512,256]{1,0:T(8,128)(2,1)S(1)}, u32[]{:S(2)}, u32[]{:S(2)}) collective-permute-start(bf16[512,256]{1,0:T(8,128)(2,1)S(1)} %copy-done), channel_id=1, source_target_pairs={{0,2},{2,0},{1,3},{3,1},{4,6},{6,4},{5,7},{7,5},{8,10},{10,8},{9,1... | collective-permute-start | bytes 786440 | tf_op jit(solution)/shard_map/ppermute | solution.py:431
  12.6 2.8 %collective-permute-start.3 = (bf16[272,128]{1,0:T(8,128)(2,1)S(1)}, bf16[272,128]{1,0:T(8,128)(2,1)S(1)}, u32[]{:S(2)}, u32[]{:S(2)}) collective-permute-start(bf16[272,128]{1,0:T(8,128)(2,1)S(1)} %collective-permute-done.1.refs_2_), channel_id=1, source_target_pairs={{0,1},{1,0},{2,3},{3,2},{4,5},{5,4},{6,7},{7,6},{8,9},{9,8},{10,11... | collective-permute-start | bytes 208904 | tf_op jit(solution)/shard_map/ppermute | solution.py:430
  14.8 1.3 %collective-permute-start.4 = (bf16[272,128]{1,0:T(8,128)(2,1)S(1)}, bf16[272,128]{1,0:T(8,128)(2,1)S(1)}, u32[]{:S(2)}, u32[]{:S(2)}) collective-permute-start(bf16[272,128]{1,0:T(8,128)(2,1)S(1)} %collective-permute-done.2.refs_3_), channel_id=1, source_target_pairs={{0,1},{1,0},{2,3},{3,2},{4,5},{5,4},{6,7},{7,6},{8,9},{9,8},{10,11... | collective-permute-start | bytes 208904 | tf_op jit(solution)/shard_map/ppermute | solution.py:430
  17.7 6.8 %collective-permute-start.7 = (s16[272,128]{1,0:T(8,128)(2,1)S(1)}, s16[272,128]{1,0:T(8,128)(2,1)S(1)}, u32[]{:S(2)}, u32[]{:S(2)}) collective-permute-start(s16[272,128]{1,0:T(8,128)(2,1)S(1)} %get-tuple-element.32), channel_id=1, source_target_pairs={{0,12},{4,8},{8,4},{12,0},{1,13},{5,9},{9,5},{13,1},{2,14},{6,10},... | collective-permute-start | bytes 208904 | tf_op jit(solution)/shard_map/ppermute | solution.py:398
  21.9 5.4 %collective-permute-start.8 = (s16[272,128]{1,0:T(8,128)(2,1)S(1)}, s16[272,128]{1,0:T(8,128)(2,1)S(1)}, u32[]{:S(2)}, u32[]{:S(2)}) collective-permute-start(s16[272,128]{1,0:T(8,128)(2,1)S(1)} %get-tuple-element.33), channel_id=1, source_target_pairs={{0,8},{4,12},{8,0},{12,4},{1,9},{5,13},{9,1},{13,5},{2,10},{6,14},... | collective-permute-start | bytes 208904 | tf_op jit(solution)/shard_map/ppermute | solution.py:398
  21.9 5.4 %collective-permute-start.9 = (s16[272,128]{1,0:T(8,128)(2,1)S(1)}, s16[272,128]{1,0:T(8,128)(2,1)S(1)}, u32[]{:S(2)}, u32[]{:S(2)}) collective-permute-start(s16[272,128]{1,0:T(8,128)(2,1)S(1)} %get-tuple-element.34), channel_id=1, source_target_pairs={{0,4},{4,0},{8,12},{12,8},{1,5},{5,1},{9,13},{13,9},{2,6},{6,2},{1... | collective-permute-start | bytes 208904 | tf_op jit(solution)/shard_map/ppermute | solution.py:398
  28.2 8.8 %all-to-all-start = ((f32[16,8,128]{2,1,0:T(8,128)}), f32[16,8,128]{2,1,0:T(8,128)S(1)}, u32[]{:S(2)}, u32[]{:S(2)}) async-start(f32[16,8,128]{2,1,0:T(8,128)} %get-tuple-element.37), calls=%async_computation | async-start | bytes 131072 | tf_op jit(solution)/shard_map/all_to_all | solution.py:464
  32.8 4.1 %collective-permute-start.10 = (bf16[80,256]{1,0:T(8,128)(2,1)S(1)}, bf16[80,256]{1,0:T(8,128)(2,1)S(1)}, u32[]{:S(2)}, u32[]{:S(2)}) collective-permute-start(bf16[80,256]{1,0:T(8,128)(2,1)S(1)} %get-tuple-element.36), channel_id=1, source_target_pairs={{0,2},{2,0},{1,3},{3,1},{4,6},{6,4},{5,7},{7,5},{8,10},{10,8},{9,1... | collective-permute-start | bytes 122888 | tf_op jit(solution)/shard_map/ppermute | solution.py:472

commit v5 on v4

--- a/solution.py
+++ b/solution.py
@@ -117,12 +117,8 @@
     return lax.axis_index("far"), lax.axis_index("near"), lax.axis_index("col")
 
 
-def prepare_kernel(far, first, last, extra, *refs):
-    sources, refs = refs[:6], refs[6:]
-    sends, refs = refs[: last - first], refs[last - first :]
-    if extra:
-        (scaled, hits), refs = refs[:2], refs[2:]
-    targets, sems = refs[:6], refs[6]
+def prepare_kernel(far, *refs):
+    sources, sends, (scaled, hits, *targets, sems) = refs[:6], refs[6 : 6 + far], refs[6 + far :]
     pair, counts, core, row_fac, col_fac, grads = targets
     copies = [
         pltpu.make_async_copy(source, target, sems.at[k])
@@ -165,13 +161,12 @@
     c00, c01, c10, c11 = core[0:1, 0:1], core[0:1, 1:2], core[1:2, 0:1], core[1:2, 1:2]
     core_b0, core_b1 = c00 * b0 + c01 * b1, c10 * b0 + c11 * b1
     score = jnp.where(live, a0 * core_b0 + a1 * core_b1, 0.0)
-    if extra:
-        hits[...] = hot
-        core_a0, core_a1 = c00 * a0 + c10 * a1, c01 * a0 + c11 * a1
-        even = at % RANK == 0
-        of_row = jnp.where(at // RANK == row_cand, jnp.where(even, core_b0, core_b1), 0.0)
-        of_col = jnp.where((at - split) // RANK == col_cand, jnp.where(even, core_a0, core_a1), 0.0)
-        scaled[...] = jnp.where(at < split, of_row, of_col)
+    hits[...] = hot
+    core_a0, core_a1 = c00 * a0 + c10 * a1, c01 * a0 + c11 * a1
+    even = at % RANK == 0
+    of_row = jnp.where(at // RANK == row_cand, jnp.where(even, core_b0, core_b1), 0.0)
+    of_col = jnp.where((at - split) // RANK == col_cand, jnp.where(even, core_a0, core_a1), 0.0)
+    scaled[...] = jnp.where(at < split, of_row, of_col)
 
     field = iota((RECORD, rows), 0)
     record = jnp.where(field == SCORE, score, 0.0)
@@ -196,7 +191,7 @@
     live_hits = jnp.where(jnp.logical_and(hit, live), 1.0, 0.0).astype(BF16)
     chosen = dot_nt(take, live_hits).astype(BF16)
     copies[-1].wait()
-    for k in range(first, last):
+    for k in range(far):
         taken = []
         for y in range(2):
             start = pl.multiple_of(((z ^ k) * 2 + (x ^ y)) * shard, shard)
@@ -207,7 +202,7 @@
             for part in taken:
                 part = part[g * mine : (g + 1) * mine]
                 blocks += [part[:, :128], part[:, 128:]]
-        sends[k - first][...] = jnp.concatenate(blocks + [records], axis=0)
+        sends[k][...] = jnp.concatenate(blocks + [records], axis=0)
 
 
 def project_kernel(far, *refs):
@@ -251,7 +246,7 @@
     for j in range(1, far):
         part = rows_for(j)
         top = jnp.max(jnp.abs(part), axis=1, keepdims=True)
-        power = jnp.floor(jnp.log(jnp.maximum(top, 2.0**-100)) * (1 / math.log(2))) + 1.0
+        power = jnp.floor(jnp.log(jnp.maximum(top, 2.0**-126)) * (1 / math.log(2))) + 1.0
         level = jnp.abs(part) * jnp.exp2(-power)
         root = level * lax.rsqrt(jnp.maximum(level, 1e-30)) * FULL
         code = jnp.floor(jnp.where(part < 0, -root, root) + 0.5)
@@ -290,7 +285,7 @@
     fetched[rows // 2 :] = dot_nn(hot[rows // 2 :], near_values[...])
 
 
-def reduce_kernel(far, *refs):
+def reduce_kernel(far, fars, *refs):
     (whole, fetched, records, value_rows), coded, (contrib, pass_on, back) = (
         refs[:4],
         refs[4 : 3 + far],
@@ -305,8 +300,8 @@
     for block in coded:
         code = block[...].astype(jnp.int32).astype(F32)
         power = jnp.where(diagonal, code[2 * rows : 2 * rows + 1], 0.0)
-        scale = jnp.exp2(jnp.sum(power, axis=1, keepdims=True)) * (1 / FULL**2)
-        value = jnp.concatenate([code[:rows], code[rows : 2 * rows]], axis=1)
+        scale = jnp.exp2(jnp.sum(power, axis=1, keepdims=True))
+        value = jnp.concatenate([code[:rows], code[rows : 2 * rows]], axis=1) * (1 / FULL)
         total = total + value * jnp.abs(value) * scale
     pair_grad = total.astype(BF16).astype(F32)
     record = records[...]
@@ -326,10 +321,15 @@
     spread = jnp.where(lane == target, dscore, 0.0).reshape(2, far, 2 * half, rows)
     spread = jnp.sum(spread[0] + spread[1], axis=1)
     outer = jnp.sum(dscore * record, axis=0, keepdims=True)
-    empty = jnp.zeros((7 - far, rows), F32)
-    block = jnp.concatenate([spread, outer, empty], axis=0)
-    for k in range(back.shape[0]):
-        back[k] = block
+    low = z < far // 2
+    core_row = jnp.where(low, pltpu.roll(outer, rows // 2, 1), outer)
+    core_lane = iota((1, rows), 1) - jnp.where(low, rows // 2, 0)
+    core_row = jnp.where(jnp.logical_and(core_lane >= 0, core_lane < RECORD), core_row, 0.0)
+    for n in range(far):
+        for k in range(4):
+            row = jnp.where(x == k // 2, spread[n : n + 1], 0.0) + core_row
+            rank = sum(jnp.where(z ^ n == far_at, at, 0) for at, far_at in enumerate(fars))
+            back[rank * 4 + 3 - k] = row
 
 
 def output_kernel(far, order, contrib, passed, value_rows, back, scaled, hits, *outs):
@@ -342,15 +342,13 @@
     row = jnp.where(lane < half, value_rows[0:1], other).astype(jnp.int32)
     hot = jnp.where(iota((out.shape[0], rows), 0) == row, 1.0, 0.0).astype(BF16)
     out[...] = dot_nn(hot, jnp.concatenate([contrib[...], passed[:half]], axis=0))
-    z, x, _ = place()
-    line = iota(back.shape[1:], 0)
-    total = jnp.zeros(back.shape[1:], F32)
-    for k in range(back.shape[0]):
-        sender = order[k]
-        mine = jnp.logical_and(line == (sender // 4 ^ z), sender // 2 % 2 == x)
-        total = total + jnp.where(jnp.logical_or(mine, line == far), back[k], 0.0)
-    dscore = jnp.sum(total[:far], axis=0, keepdims=True)
-    outer = total[far : far + 1]
+    sums = [jnp.zeros(back.shape[1:], F32) for _ in range(2)]
+    for k, sender in enumerate(order):
+        upper = sender // 4 >= far // 2
+        sums[upper] = sums[upper] + back[k]
+    left = lane < rows // 2
+    dscore = jnp.where(left, sums[0], sums[1])
+    outer = jnp.where(left, sums[1], sums[0])
     grads = add_thirds(dot_nt(thirds(scaled[...] * dscore), hits[...]))
     split = row_out.shape[0]
     row_out[...] = grads[:split]
@@ -358,7 +356,8 @@
     r, s = iota((RANK, RANK), 0), iota((RANK, RANK), 1)
     result = jnp.zeros((RANK, RANK), F32)
     for k in range(RANK * RANK):
-        mask = jnp.logical_or(lane == OUTER + k, lane == OUTER_REST + k)
+        place_in = lane % (rows // 2)
+        mask = jnp.logical_or(place_in == OUTER + k, place_in == OUTER_REST + k)
         value = jnp.sum(jnp.where(mask, outer, 0.0), axis=1, keepdims=True)
         result = jnp.where(r * RANK + s == k, value, result)
     core_out[...] = result
@@ -399,34 +398,18 @@
 
     near_weight = lax.ppermute(expand_weight, "near", swap)
     blocks = [shape(((4 if k < WHOLE else 2) * rows + RECORD, 128), BF16) for k in range(far)]
-
     operands = (pair_index, counts.reshape(1, nmem), core, row_factors.T, col_factors.T, grads)
-
-    def prepare(name, first, last, extra, limit):
-        extras = (shape((factors, rows), F32), shape((tokens, rows), BF16)) if extra else ()
-        return call(
-            functools.partial(prepare_kernel, far, first, last, extra),
-            name,
-            tuple(blocks[first:last]) + extras,
-            [HBM] * 6,
-            rows * tokens * depth,
-            2 * tokens * depth,
-            (
-                pltpu.VMEM((2, rows), jnp.int32),
-                pltpu.VMEM((1, nmem), jnp.int32),
-                pltpu.VMEM((RANK, RANK), F32),
-                pltpu.VMEM((NR * RANK, tokens), F32),
-                pltpu.VMEM((NC * RANK, tokens), F32),
-                pltpu.VMEM((tokens, depth), BF16),
-                pltpu.SemaphoreType.DMA((6,)),
-            ),
-            limit,
-        )(*(pltpu.with_memory_space_constraint(a, pltpu.HBM) for a in operands))
-
-    own_block, *sends, scaled, hits = prepare("prepare", 0, far, True, 24)
-    sends = [None] + sends
+    *sends, scaled, hits = call(
+        functools.partial(prepare_kernel, far),
+        "prepare",
+        (*blocks, shape((factors, rows), F32), shape((tokens, rows), BF16)),
+        [HBM] * 6,
+        rows * tokens * depth,
+        2 * tokens * depth,
+        [pltpu.VMEM(a.shape, a.dtype) for a in operands] + [pltpu.SemaphoreType.DMA((6,))],
+    )(*(pltpu.with_memory_space_constraint(a, pltpu.HBM) for a in operands))
     got = {k: along_far(sends[k], k) for k in reversed(range(1, far))}
-    ours = [own_block] + [got[k] for k in range(1, far)]
+    ours = [sends[0]] + [got[k] for k in range(1, far)]
     theirs = [lax.ppermute(block, "col", swap) for block in ours[WHOLE:]]
     near_values = lax.ppermute(values, "near", swap)
     code = shape((2 * rows + RECORD, 128), jnp.int16)
@@ -447,19 +430,19 @@
         2 * rows * vrows * width,
         4 * vrows * width,
     )(*ours, values, near_values)
+    fars = sorted(range(far), key=lambda z: abs(2 * z - far))
     contrib, pass_on, back = call(
-        functools.partial(reduce_kernel, far),
+        functools.partial(reduce_kernel, far, fars),
         "reduce",
         (
             shape((rows // 2, width), BF16),
             shape((rows // 2 + RECORD, width), BF16),
-            shape((2 * nmem, 8, rows), F32),
+            shape((2 * nmem, 1, rows), F32),
         ),
         [VMEM] * (3 + far),
         8 * rows * width,
         10 * rows * width,
     )(whole, fetched, records, value_rows, *coded)
-    fars = [*range(far // 2 - 1, far), *range(far // 2 - 1)]
     order = [4 * z + k for z in fars for k in (3, 2, 1, 0)]
     back = lax.all_to_all(
         back,

time: 38.2 us -> 38 us (level)
  blocking collectives: 0 us -> 7.83 us
  starting transfers between devices: 17.8 us -> 14 us
  waiting for transfers between devices: 14.1 us -> 10.5 us
  Pallas kernels: 5.39 us -> 4.78 us
    all_to_all x0 -> x1, blocking collectives: none -> 7.83 us  [local_pairs(): lax.all_to_all(back, ('far', 'near', 'col'), split_axis=0, concat_axis=0,...]
    all_to_all x1 -> x0, starting transfers between devices: 4.61 us -> none  [local_pairs(): lax.all_to_all(back, ('far', 'near', 'col'), split_axis=0, concat_axis=0,...]
    ppermute x1, waiting for transfers between devices: 3.53 us -> 0.01 us  [local_pairs(): passed = lax.ppermute(pass_on, 'near', swap)]
    ppermute x1, starting transfers between devices: 0.56 us -> 1.35 us  [local_pairs(): passed = lax.ppermute(pass_on, 'near', swap)]
    pallas_call x2, Pallas kernels: 2.63 us -> 2.03 us  [the longest x1 1.73 us: local_pairs(): call(functools.partial(prepare_kernel, far), 'prepare', (*blocks, shape((...]
  transfers between devices with their start and end apart: 12 -> 11, of which waited for: 9 -> 7; matrix products, arithmetic and copies ran while one was open for 0% -> 0% of each run, Pallas kernels for 9% -> 9%
where the time goes in v5:
time: 38 us; the launch traced here: 37.8 us
  starting transfers between devices  14 us (37%)
  waiting for transfers between devices  10.5 us (28%)
  blocking collectives  7.83 us (21%)
  Pallas kernels  4.78 us (13%)
  between operations  0.67 us (2%)
    ppermute x6, waiting for transfers between devices, along_far(): return lax.ppermute(block, 'far', [(i, i ^ k) for i in range(far)])  9.34 us
    ppermute x6, starting transfers between devices, along_far(): return lax.ppermute(block, 'far', [(i, i ^ k) for i in range(far)])  9.12 us
    all_to_all x1, blocking collectives, local_pairs(): lax.all_to_all(back, ('far', 'near', 'col'), split_axis=0, concat_axis=0,...  7.83 us
    ppermute x1, starting transfers between devices, local_pairs(): near_weight = lax.ppermute(expand_weight, 'near', swap)  3 us
    pallas_call x1, Pallas kernels, local_pairs(): call(functools.partial(prepare_kernel, far), 'prepare', (*blocks, shape((...  1.73 us
    ppermute x1, starting transfers between devices, local_pairs(): passed = lax.ppermute(pass_on, 'near', swap)  1.35 us
    pallas_call x1, Pallas kernels, local_pairs(): call(functools.partial(project_kernel, far), 'project', (shape((rows, wid...  1.06 us
    pallas_call x1, Pallas kernels, local_pairs(): call(functools.partial(output_kernel, far, order), 'outputs', (shape((vro...  1.03 us
  transfers between devices with their start and end apart: 11, of which 7 were waited for; matrix products, arithmetic and copies ran while one was open for 0% of the time, Pallas kernels for 9%

profile of v5, /device:TPU:0, one launch (start us, length us, event | category | flops | bytes accessed | tf_op | source)
XLA Modules:
  0.0 37.8 jit_solution(14455191584275499635)
XLA Ops:
  0.6 3.0 %collective-permute-start.5 = (bf16[4,256,256]{2,1,0:T(8,128)(2,1)}, bf16[4,256,256]{2,1,0:T(8,128)(2,1)S(1)}, u32[]{:S(2)}, u32[]{:S(2)}) collective-permute-start(bf16[4,256,256]{2,1,0:T(8,128)(2,1)} %refs_6_.1), channel_id=1, source_target_pairs={{0,2},{2,0},{1,3},{3,1},{4,6},{6,4},{5,7},{7,5},{8,10},{10,8},{9,1... | collective-permute-start | bytes 1572872 | tf_op jit(solution)/shard_map/ppermute | solution.py:399
  3.6 0.0 copy-start
  3.6 0.0 copy-start.1
  3.6 1.7 %prepare.1 = (bf16[528,128]{1,0:T(8,128)(2,1)S(1)}, bf16[528,128]{1,0:T(8,128)(2,1)S(1)}, bf16[272,128]{1,0:T(8,128)(2,1)S(1)}, bf16[272,128]{1,0:T(8,128)(2,1)S...) custom-call(s32[2,128]{1,0:T(2,128)} %refs_0_.1, s32[1,8]{1,0:T(1,128)} %bitcast.7, f32[2,2]{1,0:T(2,128)} %refs_2_.1, ...), custom_call_target="tpu_custom_call" | custom-call | flops 67108864 | bytes 1048576 | tf_op jit(solution)/shard_map/prepare/pallas_call | solution.py:402
  5.4 2.7 %collective-permute-start.1 = (bf16[272,128]{1,0:T(8,128)(2,1)S(1)}, bf16[272,128]{1,0:T(8,128)(2,1)S(1)}, u32[]{:S(2)}, u32[]{:S(2)}) collective-permute-start(bf16[272,128]{1,0:T(8,128)(2,1)S(1)} %get-tuple-element.26), channel_id=1, source_target_pairs={{0,8},{4,12},{8,0},{12,4},{1,9},{5,13},{9,1},{13,5},{2,10},{6,14},... | collective-permute-start | bytes 208904 | tf_op jit(solution)/shard_map/ppermute | solution.py:397
  8.0 1.3 %collective-permute-start.2 = (bf16[272,128]{1,0:T(8,128)(2,1)S(1)}, bf16[272,128]{1,0:T(8,128)(2,1)S(1)}, u32[]{:S(2)}, u32[]{:S(2)}) collective-permute-start(bf16[272,128]{1,0:T(8,128)(2,1)S(1)} %get-tuple-element.27), channel_id=1, source_target_pairs={{0,12},{4,8},{8,4},{12,0},{1,13},{5,9},{9,5},{13,1},{2,14},{6,10},... | collective-permute-start | bytes 208904 | tf_op jit(solution)/shard_map/ppermute | solution.py:397
  9.4 0.2 collective-permute-start
  9.6 0.0 copy-done
  9.6 0.5 %collective-permute-start.6 = (bf16[512,256]{1,0:T(8,128)(2,1)S(1)}, bf16[512,256]{1,0:T(8,128)(2,1)S(1)}, u32[]{:S(2)}, u32[]{:S(2)}) collective-permute-start(bf16[512,256]{1,0:T(8,128)(2,1)S(1)} %copy-done), channel_id=1, source_target_pairs={{0,2},{2,0},{1,3},{3,1},{4,6},{6,4},{5,7},{7,5},{8,10},{10,8},{9,1... | collective-permute-start | bytes 786440 | tf_op jit(solution)/shard_map/ppermute | solution.py:414
  10.1 2.5 %collective-permute-done.1.refs_2_ = bf16[272,128]{1,0:T(8,128)(2,1)S(1)} collective-permute-done((bf16[272,128]{1,0:T(8,128)(2,1)S(1)}, bf16[272,128]{1,0:T(8,128)(2,1)S(1)}, u32[]{:S(2)}, u32[]{:S(2)}) %collective-permute-start.1) | collective-permute-done | bytes 69664 | tf_op jit(solution)/shard_map/ppermute | solution.py:397
  12.6 0.0 collective-permute-start.3
  12.6 2.1 %collective-permute-done.2.refs_3_ = bf16[272,128]{1,0:T(8,128)(2,1)S(1)} collective-permute-done((bf16[272,128]{1,0:T(8,128)(2,1)S(1)}, bf16[272,128]{1,0:T(8,128)(2,1)S(1)}, u32[]{:S(2)}, u32[]{:S(2)}) %collective-permute-start.2) | collective-permute-done | bytes 69664 | tf_op jit(solution)/shard_map/ppermute | solution.py:397
  14.8 0.0 collective-permute-start.4
  14.8 0.6 %collective-permute-done.refs_1_ = bf16[528,128]{1,0:T(8,128)(2,1)S(1)} collective-permute-done((bf16[528,128]{1,0:T(8,128)(2,1)S(1)}, bf16[528,128]{1,0:T(8,128)(2,1)S(1)}, u32[]{:S(2)}, u32[]{:S(2)}) %collective-permute-start) | collective-permute-done | bytes 135200 | tf_op jit(solution)/shard_map/ppermute | solution.py:397
  15.4 0.0 collective-permute-done.3.refs_4_
  15.4 0.6 %collective-permute-done.4.refs_5_ = bf16[272,128]{1,0:T(8,128)(2,1)S(1)} collective-permute-done((bf16[272,128]{1,0:T(8,128)(2,1)S(1)}, bf16[272,128]{1,0:T(8,128)(2,1)S(1)}, u32[]{:S(2)}, u32[]{:S(2)}) %collective-permute-start.4) | collective-permute-done | bytes 69664 | tf_op jit(solution)/shard_map/ppermute | solution.py:413
  16.0 0.6 %collective-permute-done.5.refs_7_ = bf16[4,256,256]{2,1,0:T(8,128)(2,1)S(1)} collective-permute-done((bf16[4,256,256]{2,1,0:T(8,128)(2,1)}, bf16[4,256,256]{2,1,0:T(8,128)(2,1)S(1)}, u32[]{:S(2)}, u32[]{:S(2)}) %collective-permute-start.5) | collective-permute-done | bytes 524320 | tf_op jit(solution)/shard_map/ppermute | solution.py:399
  16.6 0.0 copy-done.1
  16.6 1.1 %project.1 = (f32[128,256]{1,0:T(8,128)S(1)}, s16[272,128]{1,0:T(8,128)(2,1)S(1)}, s16[272,128]{1,0:T(8,128)(2,1)S(1)}, s16[272,128]{1,0:T(8,128)(2,1)S(1)}) custom-call(bf16[528,128]{1,0:T(8,128)(2,1)S(1)} %get-tuple-element.24.refs_0_, bf16[528,128]{1,0:T(8,128)(2,1)S(1)} %collective-permute-done.refs_1_, ...), custom_call_target="tpu_custom_call" | custom-call | flops 1073741824 | bytes 2097152 | tf_op jit(solution)/shard_map/project/pallas_call | solution.py:416
  17.7 4.2 %collective-permute-start.7 = (s16[272,128]{1,0:T(8,128)(2,1)S(1)}, s16[272,128]{1,0:T(8,128)(2,1)S(1)}, u32[]{:S(2)}, u32[]{:S(2)}) collective-permute-start(s16[272,128]{1,0:T(8,128)(2,1)S(1)} %get-tuple-element.32), channel_id=1, source_target_pairs={{0,12},{4,8},{8,4},{12,0},{1,13},{5,9},{9,5},{13,1},{2,14},{6,10},... | collective-permute-start | bytes 208904 | tf_op jit(solution)/shard_map/ppermute | solution.py:397
  21.9 0.0 collective-permute-start.8
  21.9 0.6 %collective-permute-start.9 = (s16[272,128]{1,0:T(8,128)(2,1)S(1)}, s16[272,128]{1,0:T(8,128)(2,1)S(1)}, u32[]{:S(2)}, u32[]{:S(2)}) collective-permute-start(s16[272,128]{1,0:T(8,128)(2,1)S(1)} %get-tuple-element.34), channel_id=1, source_target_pairs={{0,4},{4,0},{8,12},{12,8},{1,5},{5,1},{9,13},{13,9},{2,6},{6,2},{1... | collective-permute-start | bytes 208904 | tf_op jit(solution)/shard_map/ppermute | solution.py:397
  22.5 0.0 collective-permute-done.6.refs_5_
  22.6 0.7 %lookup.1 = (f32[128,256]{1,0:T(8,128)S(1)}, f32[128,128]{1,0:T(8,128)S(1)}, f32[8,128]{1,0:T(8,128)S(1)}) custom-call(bf16[528,128]{1,0:T(8,128)(2,1)S(1)} %get-tuple-element.24.refs_0_, bf16[528,128]{1,0:T(8,128)(2,1)S(1)} %collective-permute-done.refs_1_, bf16[272,128]{1,0:T(8,128)(2,1)S(1)} %collective-permute-done.1.refs_2_, ...), custom_call_target="tpu_custom_call" | custom-call | flops 33554432 | bytes 524288 | tf_op jit(solution)/shard_map/lookup/pallas_call | solution.py:425
  23.2 1.3 %collective-permute-done.7.refs_4_ = s16[272,128]{1,0:T(8,128)(2,1)S(1)} collective-permute-done((s16[272,128]{1,0:T(8,128)(2,1)S(1)}, s16[272,128]{1,0:T(8,128)(2,1)S(1)}, u32[]{:S(2)}, u32[]{:S(2)}) %collective-permute-start.7) | collective-permute-done | bytes 69664 | tf_op jit(solution)/shard_map/ppermute | solution.py:397
  24.5 2.8 %collective-permute-done.8.refs_5_ = s16[272,128]{1,0:T(8,128)(2,1)S(1)} collective-permute-done((s16[272,128]{1,0:T(8,128)(2,1)S(1)}, s16[272,128]{1,0:T(8,128)(2,1)S(1)}, u32[]{:S(2)}, u32[]{:S(2)}) %collective-permute-start.8) | collective-permute-done | bytes 69664 | tf_op jit(solution)/shard_map/ppermute | solution.py:397
  27.3 0.0 collective-permute-done.9.refs_6_
  27.3 0.3 reduce.1
  27.6 1.3 %collective-permute-start.10 = (bf16[80,256]{1,0:T(8,128)(2,1)S(1)}, bf16[80,256]{1,0:T(8,128)(2,1)S(1)}, u32[]{:S(2)}, u32[]{:S(2)}) collective-permute-start(bf16[80,256]{1,0:T(8,128)(2,1)S(1)} %get-tuple-element.36), channel_id=1, source_target_pairs={{0,2},{2,0},{1,3},{3,1},{4,6},{6,4},{5,7},{7,5},{8,10},{10,8},{9,1... | collective-permute-start | bytes 122888 | tf_op jit(solution)/shard_map/ppermute | solution.py:455
  28.9 7.8 %all_to_all.5.back = f32[16,1,128]{2,1,0:T(1,128)S(1)} all-to-all(f32[16,1,128]{2,1,0:T(1,128)S(1)} %get-tuple-element.37), channel_id=1, replica_groups={{11,10,9,8,7,6,5,4,15,14,13,12,3,2,1,0},{27,26,25,24,23,22,21,20,31,30,..., dimensions={0} | all-to-all | bytes 16384 | tf_op jit(solution)/shard_map/all_to_all | solution.py:447
  36.8 0.0 collective-permute-done.10.passed
  36.8 1.0 %outputs.1 = (f32[512,256]{1,0:T(8,128)}, f32[16,256]{1,0:T(8,128)}, f32[16,256]{1,0:T(8,128)}, f32[2,2]{1,0:T(2,128)}) custom-call(bf16[64,256]{1,0:T(8,128)(2,1)S(1)} %get-tuple-element.35.contrib, bf16[80,256]{1,0:T(8,128)(2,1)S(1)} %collective-permute-done.10.passed, f32[8,128]{1,0:T(8,128)S(1)} %get-tuple-element.31.refs_3_.value_rows, ...), custom_call_target="tpu_custom_call" | custom-call | flops 33554432 | bytes 524288 | tf_op jit(solution)/shard_map/outputs/pallas_call | solution.py:456
Async XLA Ops:
  0.6 16.0 %collective-permute-start.5 = (bf16[4,256,256]{2,1,0:T(8,128)(2,1)}, bf16[4,256,256]{2,1,0:T(8,128)(2,1)S(1)}, u32[]{:S(2)}, u32[]{:S(2)}) collective-permute-start(bf16[4,256,256]{2,1,0:T(8,128)(2,1)} %refs_6_.1), channel_id=1, source_target_pairs={{0,2},{2,0},{1,3},{3,1},{4,6},{6,4},{5,7},{7,5},{8,10},{10,8},{9,1... | collective-permute-start | bytes 1572872 | tf_op jit(solution)/shard_map/ppermute | solution.py:399
  3.6 6.0 %copy-start = (bf16[512,256]{1,0:T(8,128)(2,1)S(1)}, bf16[512,256]{1,0:T(8,128)(2,1)}, u32[]{:S(2)}) copy-start(bf16[512,256]{1,0:T(8,128)(2,1)} %refs_4_.1) | copy-start | bytes 786436
  3.6 13.0 %copy-start.1 = (bf16[4,256,256]{2,1,0:T(8,128)(2,1)S(1)}, bf16[4,256,256]{2,1,0:T(8,128)(2,1)}, u32[]{:S(2)}) copy-start(bf16[4,256,256]{2,1,0:T(8,128)(2,1)} %refs_6_.1) | copy-start | bytes 1572868
  5.4 7.3 %collective-permute-start.1 = (bf16[272,128]{1,0:T(8,128)(2,1)S(1)}, bf16[272,128]{1,0:T(8,128)(2,1)S(1)}, u32[]{:S(2)}, u32[]{:S(2)}) collective-permute-start(bf16[272,128]{1,0:T(8,128)(2,1)S(1)} %get-tuple-element.26), channel_id=1, source_target_pairs={{0,8},{4,12},{8,0},{12,4},{1,9},{5,13},{9,1},{13,5},{2,10},{6,14},... | collective-permute-start | bytes 208904 | tf_op jit(solution)/shard_map/ppermute | solution.py:397
  8.0 6.7 %collective-permute-start.2 = (bf16[272,128]{1,0:T(8,128)(2,1)S(1)}, bf16[272,128]{1,0:T(8,128)(2,1)S(1)}, u32[]{:S(2)}, u32[]{:S(2)}) collective-permute-start(bf16[272,128]{1,0:T(8,128)(2,1)S(1)} %get-tuple-element.27), channel_id=1, source_target_pairs={{0,12},{4,8},{8,4},{12,0},{1,13},{5,9},{9,5},{13,1},{2,14},{6,10},... | collective-permute-start | bytes 208904 | tf_op jit(solution)/shard_map/ppermute | solution.py:397
  9.4 6.0 %collective-permute-start = (bf16[528,128]{1,0:T(8,128)(2,1)S(1)}, bf16[528,128]{1,0:T(8,128)(2,1)S(1)}, u32[]{:S(2)}, u32[]{:S(2)}) collective-permute-start(bf16[528,128]{1,0:T(8,128)(2,1)S(1)} %get-tuple-element.25), channel_id=1, source_target_pairs={{0,4},{4,0},{8,12},{12,8},{1,5},{5,1},{9,13},{13,9},{2,6},{6,2},{1... | collective-permute-start | bytes 405512 | tf_op jit(solution)/shard_map/ppermute | solution.py:397
  9.6 12.9 %collective-permute-start.6 = (bf16[512,256]{1,0:T(8,128)(2,1)S(1)}, bf16[512,256]{1,0:T(8,128)(2,1)S(1)}, u32[]{:S(2)}, u32[]{:S(2)}) collective-permute-start(bf16[512,256]{1,0:T(8,128)(2,1)S(1)} %copy-done), channel_id=1, source_target_pairs={{0,2},{2,0},{1,3},{3,1},{4,6},{6,4},{5,7},{7,5},{8,10},{10,8},{9,1... | collective-permute-start | bytes 786440 | tf_op jit(solution)/shard_map/ppermute | solution.py:414
  12.6 2.8 %collective-permute-start.3 = (bf16[272,128]{1,0:T(8,128)(2,1)S(1)}, bf16[272,128]{1,0:T(8,128)(2,1)S(1)}, u32[]{:S(2)}, u32[]{:S(2)}) collective-permute-start(bf16[272,128]{1,0:T(8,128)(2,1)S(1)} %collective-permute-done.1.refs_2_), channel_id=1, source_target_pairs={{0,1},{1,0},{2,3},{3,2},{4,5},{5,4},{6,7},{7,6},{8,9},{9,8},{10,11... | collective-permute-start | bytes 208904 | tf_op jit(solution)/shard_map/ppermute | solution.py:413
  14.8 1.3 %collective-permute-start.4 = (bf16[272,128]{1,0:T(8,128)(2,1)S(1)}, bf16[272,128]{1,0:T(8,128)(2,1)S(1)}, u32[]{:S(2)}, u32[]{:S(2)}) collective-permute-start(bf16[272,128]{1,0:T(8,128)(2,1)S(1)} %collective-permute-done.2.refs_3_), channel_id=1, source_target_pairs={{0,1},{1,0},{2,3},{3,2},{4,5},{5,4},{6,7},{7,6},{8,9},{9,8},{10,11... | collective-permute-start | bytes 208904 | tf_op jit(solution)/shard_map/ppermute | solution.py:413
  17.7 6.8 %collective-permute-start.7 = (s16[272,128]{1,0:T(8,128)(2,1)S(1)}, s16[272,128]{1,0:T(8,128)(2,1)S(1)}, u32[]{:S(2)}, u32[]{:S(2)}) collective-permute-start(s16[272,128]{1,0:T(8,128)(2,1)S(1)} %get-tuple-element.32), channel_id=1, source_target_pairs={{0,12},{4,8},{8,4},{12,0},{1,13},{5,9},{9,5},{13,1},{2,14},{6,10},... | collective-permute-start | bytes 208904 | tf_op jit(solution)/shard_map/ppermute | solution.py:397
  21.9 5.4 %collective-permute-start.8 = (s16[272,128]{1,0:T(8,128)(2,1)S(1)}, s16[272,128]{1,0:T(8,128)(2,1)S(1)}, u32[]{:S(2)}, u32[]{:S(2)}) collective-permute-start(s16[272,128]{1,0:T(8,128)(2,1)S(1)} %get-tuple-element.33), channel_id=1, source_target_pairs={{0,8},{4,12},{8,0},{12,4},{1,9},{5,13},{9,1},{13,5},{2,10},{6,14},... | collective-permute-start | bytes 208904 | tf_op jit(solution)/shard_map/ppermute | solution.py:397
  21.9 5.4 %collective-permute-start.9 = (s16[272,128]{1,0:T(8,128)(2,1)S(1)}, s16[272,128]{1,0:T(8,128)(2,1)S(1)}, u32[]{:S(2)}, u32[]{:S(2)}) collective-permute-start(s16[272,128]{1,0:T(8,128)(2,1)S(1)} %get-tuple-element.34), channel_id=1, source_target_pairs={{0,4},{4,0},{8,12},{12,8},{1,5},{5,1},{9,13},{13,9},{2,6},{6,2},{1... | collective-permute-start | bytes 208904 | tf_op jit(solution)/shard_map/ppermute | solution.py:397
  27.6 9.2 %collective-permute-start.10 = (bf16[80,256]{1,0:T(8,128)(2,1)S(1)}, bf16[80,256]{1,0:T(8,128)(2,1)S(1)}, u32[]{:S(2)}, u32[]{:S(2)}) collective-permute-start(bf16[80,256]{1,0:T(8,128)(2,1)S(1)} %get-tuple-element.36), channel_id=1, source_target_pairs={{0,2},{2,0},{1,3},{3,1},{4,6},{6,4},{5,7},{7,5},{8,10},{10,8},{9,1... | collective-permute-start | bytes 122888 | tf_op jit(solution)/shard_map/ppermute | solution.py:455

commit v6 on v5

--- a/solution.py
+++ b/solution.py
@@ -375,7 +375,7 @@
         in_specs=ins,
         out_specs=jax.tree.map(lambda _: VMEM, outs),
         scratch_shapes=scratch,
-        cost_estimate=pl.CostEstimate(flops=flops, bytes_accessed=moved, transcendentals=0),
+        cost_estimate=pl.CostEstimate(flops=64 * flops, bytes_accessed=16 * moved, transcendentals=0),
         compiler_params=pltpu.CompilerParams(vmem_limit_bytes=limit << 20),
     )
 

time: 38 us -> 37.6 us (0.989)
  starting transfers between devices: 14 us -> 13.5 us
    ppermute x1, waiting for transfers between devices: 0.01 us -> 1.93 us  [local_pairs(): near_values = lax.ppermute(values, 'near', swap)]
    ppermute x6, waiting for transfers between devices: 9.34 us -> 8.03 us  [along_far(): return lax.ppermute(block, 'far', [(i, i ^ k) for i in range(far)])]
    ppermute x1, waiting for transfers between devices: 0.55 us -> 0.01 us  [local_pairs(): near_weight = lax.ppermute(expand_weight, 'near', swap)]
    ppermute x6, starting transfers between devices: 9.12 us -> 8.69 us  [along_far(): return lax.ppermute(block, 'far', [(i, i ^ k) for i in range(far)])]
  transfers between devices with their start and end apart: 11 -> 11, of which waited for: 7 -> 6; matrix products, arithmetic and copies ran while one was open for 0% -> 0% of each run, Pallas kernels for 9% -> 9%
where the time goes in v6:
time: 37.6 us; the launch traced here: 37.4 us
  starting transfers between devices  13.5 us (36%)
  waiting for transfers between devices  10.6 us (28%)
  blocking collectives  7.83 us (21%)
  Pallas kernels  4.78 us (13%)
  between operations  0.67 us (2%)
    ppermute x6, starting transfers between devices, along_far(): return lax.ppermute(block, 'far', [(i, i ^ k) for i in range(far)])  8.69 us
    ppermute x6, waiting for transfers between devices, along_far(): return lax.ppermute(block, 'far', [(i, i ^ k) for i in range(far)])  8.03 us
    all_to_all x1, blocking collectives, local_pairs(): lax.all_to_all(back, ('far', 'near', 'col'), split_axis=0, concat_axis=0,...  7.83 us
    ppermute x1, starting transfers between devices, local_pairs(): near_weight = lax.ppermute(expand_weight, 'near', swap)  3 us
    ppermute x1, waiting for transfers between devices, local_pairs(): near_values = lax.ppermute(values, 'near', swap)  1.93 us
    pallas_call x1, Pallas kernels, local_pairs(): call(functools.partial(prepare_kernel, far), 'prepare', (*blocks, shape((...  1.73 us
    ppermute x1, starting transfers between devices, local_pairs(): passed = lax.ppermute(pass_on, 'near', swap)  1.24 us
    pallas_call x1, Pallas kernels, local_pairs(): call(functools.partial(project_kernel, far), 'project', (shape((rows, wid...  1.06 us
  transfers between devices with their start and end apart: 11, of which 6 were waited for; matrix products, arithmetic and copies ran while one was open for 0% of the time, Pallas kernels for 9%

profile of v6, /device:TPU:0, one launch (start us, length us, event | category | flops | bytes accessed | tf_op | source)
XLA Modules:
  0.0 37.4 jit_solution(1095960533879311529)
XLA Ops:
  0.6 3.0 %collective-permute-start.5 = (bf16[4,256,256]{2,1,0:T(8,128)(2,1)}, bf16[4,256,256]{2,1,0:T(8,128)(2,1)S(1)}, u32[]{:S(2)}, u32[]{:S(2)}) collective-permute-start(bf16[4,256,256]{2,1,0:T(8,128)(2,1)} %refs_6_.1), channel_id=1, source_target_pairs={{0,2},{2,0},{1,3},{3,1},{4,6},{6,4},{5,7},{7,5},{8,10},{10,8},{9,1... | collective-permute-start | bytes 1572872 | tf_op jit(solution)/shard_map/ppermute | solution.py:399
  3.6 0.0 copy-start.1
  3.6 0.0 copy-start
  3.6 1.7 %prepare.1 = (bf16[528,128]{1,0:T(8,128)(2,1)S(1)}, bf16[528,128]{1,0:T(8,128)(2,1)S(1)}, bf16[272,128]{1,0:T(8,128)(2,1)S(1)}, bf16[272,128]{1,0:T(8,128)(2,1)S...) custom-call(s32[2,128]{1,0:T(2,128)} %refs_0_.1, s32[1,8]{1,0:T(1,128)} %bitcast.7, f32[2,2]{1,0:T(2,128)} %refs_2_.1, ...), custom_call_target="tpu_custom_call" | custom-call | flops 4294967296 | bytes 16777216 | tf_op jit(solution)/shard_map/prepare/pallas_call | solution.py:402
  5.4 2.7 %collective-permute-start.1 = (bf16[272,128]{1,0:T(8,128)(2,1)S(1)}, bf16[272,128]{1,0:T(8,128)(2,1)S(1)}, u32[]{:S(2)}, u32[]{:S(2)}) collective-permute-start(bf16[272,128]{1,0:T(8,128)(2,1)S(1)} %get-tuple-element.26), channel_id=1, source_target_pairs={{0,8},{4,12},{8,0},{12,4},{1,9},{5,13},{9,1},{13,5},{2,10},{6,14},... | collective-permute-start | bytes 208904 | tf_op jit(solution)/shard_map/ppermute | solution.py:397
  8.0 1.3 %collective-permute-start.2 = (bf16[272,128]{1,0:T(8,128)(2,1)S(1)}, bf16[272,128]{1,0:T(8,128)(2,1)S(1)}, u32[]{:S(2)}, u32[]{:S(2)}) collective-permute-start(bf16[272,128]{1,0:T(8,128)(2,1)S(1)} %get-tuple-element.27), channel_id=1, source_target_pairs={{0,12},{4,8},{8,4},{12,0},{1,13},{5,9},{9,5},{13,1},{2,14},{6,10},... | collective-permute-start | bytes 208904 | tf_op jit(solution)/shard_map/ppermute | solution.py:397
  9.4 0.2 collective-permute-start
  9.6 3.0 %collective-permute-done.1.refs_2_ = bf16[272,128]{1,0:T(8,128)(2,1)S(1)} collective-permute-done((bf16[272,128]{1,0:T(8,128)(2,1)S(1)}, bf16[272,128]{1,0:T(8,128)(2,1)S(1)}, u32[]{:S(2)}, u32[]{:S(2)}) %collective-permute-start.1) | collective-permute-done | bytes 69664 | tf_op jit(solution)/shard_map/ppermute | solution.py:397
  12.6 0.0 collective-permute-start.3
  12.6 2.1 %collective-permute-done.2.refs_3_ = bf16[272,128]{1,0:T(8,128)(2,1)S(1)} collective-permute-done((bf16[272,128]{1,0:T(8,128)(2,1)S(1)}, bf16[272,128]{1,0:T(8,128)(2,1)S(1)}, u32[]{:S(2)}, u32[]{:S(2)}) %collective-permute-start.2) | collective-permute-done | bytes 69664 | tf_op jit(solution)/shard_map/ppermute | solution.py:397
  14.8 0.0 collective-permute-start.4
  14.8 0.0 copy-done.1
  14.8 0.5 %collective-permute-start.6 = (bf16[512,256]{1,0:T(8,128)(2,1)S(1)}, bf16[512,256]{1,0:T(8,128)(2,1)S(1)}, u32[]{:S(2)}, u32[]{:S(2)}) collective-permute-start(bf16[512,256]{1,0:T(8,128)(2,1)S(1)} %copy-done.1), channel_id=1, source_target_pairs={{0,2},{2,0},{1,3},{3,1},{4,6},{6,4},{5,7},{7,5},{8,10},{10,8},{9,1... | collective-permute-start | bytes 786440 | tf_op jit(solution)/shard_map/ppermute | solution.py:414
  15.3 0.1 collective-permute-done.refs_1_
  15.4 0.0 collective-permute-done.3.refs_4_
  15.4 0.6 %collective-permute-done.4.refs_5_ = bf16[272,128]{1,0:T(8,128)(2,1)S(1)} collective-permute-done((bf16[272,128]{1,0:T(8,128)(2,1)S(1)}, bf16[272,128]{1,0:T(8,128)(2,1)S(1)}, u32[]{:S(2)}, u32[]{:S(2)}) %collective-permute-start.4) | collective-permute-done | bytes 69664 | tf_op jit(solution)/shard_map/ppermute | solution.py:413
  16.0 0.0 collective-permute-done.5.refs_7_
  16.0 0.0 copy-done
  16.1 1.1 %project.1 = (f32[128,256]{1,0:T(8,128)S(1)}, s16[272,128]{1,0:T(8,128)(2,1)S(1)}, s16[272,128]{1,0:T(8,128)(2,1)S(1)}, s16[272,128]{1,0:T(8,128)(2,1)S(1)}) custom-call(bf16[528,128]{1,0:T(8,128)(2,1)S(1)} %get-tuple-element.24.refs_0_, bf16[528,128]{1,0:T(8,128)(2,1)S(1)} %collective-permute-done.refs_1_, ...), custom_call_target="tpu_custom_call" | custom-call | flops 68719476736 | bytes 33554432 | tf_op jit(solution)/shard_map/project/pallas_call | solution.py:416
  17.1 3.6 %collective-permute-start.7 = (s16[272,128]{1,0:T(8,128)(2,1)S(1)}, s16[272,128]{1,0:T(8,128)(2,1)S(1)}, u32[]{:S(2)}, u32[]{:S(2)}) collective-permute-start(s16[272,128]{1,0:T(8,128)(2,1)S(1)} %get-tuple-element.32), channel_id=1, source_target_pairs={{0,12},{4,8},{8,4},{12,0},{1,13},{5,9},{9,5},{13,1},{2,14},{6,10},... | collective-permute-start | bytes 208904 | tf_op jit(solution)/shard_map/ppermute | solution.py:397
  20.8 0.0 collective-permute-start.8
  20.8 0.8 %collective-permute-start.9 = (s16[272,128]{1,0:T(8,128)(2,1)S(1)}, s16[272,128]{1,0:T(8,128)(2,1)S(1)}, u32[]{:S(2)}, u32[]{:S(2)}) collective-permute-start(s16[272,128]{1,0:T(8,128)(2,1)S(1)} %get-tuple-element.34), channel_id=1, source_target_pairs={{0,4},{4,0},{8,12},{12,8},{1,5},{5,1},{9,13},{13,9},{2,6},{6,2},{1... | collective-permute-start | bytes 208904 | tf_op jit(solution)/shard_map/ppermute | solution.py:397
  21.6 1.9 %collective-permute-done.6.refs_5_ = bf16[512,256]{1,0:T(8,128)(2,1)S(1)} collective-permute-done((bf16[512,256]{1,0:T(8,128)(2,1)S(1)}, bf16[512,256]{1,0:T(8,128)(2,1)S(1)}, u32[]{:S(2)}, u32[]{:S(2)}) %collective-permute-start.6) | collective-permute-done | bytes 262176 | tf_op jit(solution)/shard_map/ppermute | solution.py:414
  23.5 0.7 %lookup.1 = (f32[128,256]{1,0:T(8,128)S(1)}, f32[128,128]{1,0:T(8,128)S(1)}, f32[8,128]{1,0:T(8,128)S(1)}) custom-call(bf16[528,128]{1,0:T(8,128)(2,1)S(1)} %get-tuple-element.24.refs_0_, bf16[528,128]{1,0:T(8,128)(2,1)S(1)} %collective-permute-done.refs_1_, bf16[272,128]{1,0:T(8,128)(2,1)S(1)} %collective-permute-done.1.refs_2_, ...), custom_call_target="tpu_custom_call" | custom-call | flops 2147483648 | bytes 8388608 | tf_op jit(solution)/shard_map/lookup/pallas_call | solution.py:425
  24.2 0.0 collective-permute-done.7.refs_4_
  24.2 2.8 %collective-permute-done.8.refs_5_ = s16[272,128]{1,0:T(8,128)(2,1)S(1)} collective-permute-done((s16[272,128]{1,0:T(8,128)(2,1)S(1)}, s16[272,128]{1,0:T(8,128)(2,1)S(1)}, u32[]{:S(2)}, u32[]{:S(2)}) %collective-permute-start.8) | collective-permute-done | bytes 69664 | tf_op jit(solution)/shard_map/ppermute | solution.py:397
  27.0 0.0 collective-permute-done.9.refs_6_
  27.0 0.3 reduce.1
  27.3 1.2 %collective-permute-start.10 = (bf16[80,256]{1,0:T(8,128)(2,1)S(1)}, bf16[80,256]{1,0:T(8,128)(2,1)S(1)}, u32[]{:S(2)}, u32[]{:S(2)}) collective-permute-start(bf16[80,256]{1,0:T(8,128)(2,1)S(1)} %get-tuple-element.36), channel_id=1, source_target_pairs={{0,2},{2,0},{1,3},{3,1},{4,6},{6,4},{5,7},{7,5},{8,10},{10,8},{9,1... | collective-permute-start | bytes 122888 | tf_op jit(solution)/shard_map/ppermute | solution.py:455
  28.5 7.8 %all_to_all.5.back = f32[16,1,128]{2,1,0:T(1,128)S(1)} all-to-all(f32[16,1,128]{2,1,0:T(1,128)S(1)} %get-tuple-element.37), channel_id=1, replica_groups={{11,10,9,8,7,6,5,4,15,14,13,12,3,2,1,0},{27,26,25,24,23,22,21,20,31,30,..., dimensions={0} | all-to-all | bytes 16384 | tf_op jit(solution)/shard_map/all_to_all | solution.py:447
  36.3 0.0 collective-permute-done.10.passed
  36.3 1.0 %outputs.1 = (f32[512,256]{1,0:T(8,128)}, f32[16,256]{1,0:T(8,128)}, f32[16,256]{1,0:T(8,128)}, f32[2,2]{1,0:T(2,128)}) custom-call(bf16[64,256]{1,0:T(8,128)(2,1)S(1)} %get-tuple-element.35.contrib, bf16[80,256]{1,0:T(8,128)(2,1)S(1)} %collective-permute-done.10.passed, f32[8,128]{1,0:T(8,128)S(1)} %get-tuple-element.31.refs_3_.value_rows, ...), custom_call_target="tpu_custom_call" | custom-call | flops 2147483648 | bytes 8388608 | tf_op jit(solution)/shard_map/outputs/pallas_call | solution.py:456
Async XLA Ops:
  0.6 15.4 %collective-permute-start.5 = (bf16[4,256,256]{2,1,0:T(8,128)(2,1)}, bf16[4,256,256]{2,1,0:T(8,128)(2,1)S(1)}, u32[]{:S(2)}, u32[]{:S(2)}) collective-permute-start(bf16[4,256,256]{2,1,0:T(8,128)(2,1)} %refs_6_.1), channel_id=1, source_target_pairs={{0,2},{2,0},{1,3},{3,1},{4,6},{6,4},{5,7},{7,5},{8,10},{10,8},{9,1... | collective-permute-start | bytes 1572872 | tf_op jit(solution)/shard_map/ppermute | solution.py:399
  3.6 11.2 %copy-start.1 = (bf16[512,256]{1,0:T(8,128)(2,1)S(1)}, bf16[512,256]{1,0:T(8,128)(2,1)}, u32[]{:S(2)}) copy-start(bf16[512,256]{1,0:T(8,128)(2,1)} %refs_4_.1) | copy-start | bytes 786436
  3.6 12.4 %copy-start = (bf16[4,256,256]{2,1,0:T(8,128)(2,1)S(1)}, bf16[4,256,256]{2,1,0:T(8,128)(2,1)}, u32[]{:S(2)}) copy-start(bf16[4,256,256]{2,1,0:T(8,128)(2,1)} %refs_6_.1) | copy-start | bytes 1572868
  5.4 7.3 %collective-permute-start.1 = (bf16[272,128]{1,0:T(8,128)(2,1)S(1)}, bf16[272,128]{1,0:T(8,128)(2,1)S(1)}, u32[]{:S(2)}, u32[]{:S(2)}) collective-permute-start(bf16[272,128]{1,0:T(8,128)(2,1)S(1)} %get-tuple-element.26), channel_id=1, source_target_pairs={{0,8},{4,12},{8,0},{12,4},{1,9},{5,13},{9,1},{13,5},{2,10},{6,14},... | collective-permute-start | bytes 208904 | tf_op jit(solution)/shard_map/ppermute | solution.py:397
  8.0 6.7 %collective-permute-start.2 = (bf16[272,128]{1,0:T(8,128)(2,1)S(1)}, bf16[272,128]{1,0:T(8,128)(2,1)S(1)}, u32[]{:S(2)}, u32[]{:S(2)}) collective-permute-start(bf16[272,128]{1,0:T(8,128)(2,1)S(1)} %get-tuple-element.27), channel_id=1, source_target_pairs={{0,12},{4,8},{8,4},{12,0},{1,13},{5,9},{9,5},{13,1},{2,14},{6,10},... | collective-permute-start | bytes 208904 | tf_op jit(solution)/shard_map/ppermute | solution.py:397
  9.4 6.0 %collective-permute-start = (bf16[528,128]{1,0:T(8,128)(2,1)S(1)}, bf16[528,128]{1,0:T(8,128)(2,1)S(1)}, u32[]{:S(2)}, u32[]{:S(2)}) collective-permute-start(bf16[528,128]{1,0:T(8,128)(2,1)S(1)} %get-tuple-element.25), channel_id=1, source_target_pairs={{0,4},{4,0},{8,12},{12,8},{1,5},{5,1},{9,13},{13,9},{2,6},{6,2},{1... | collective-permute-start | bytes 405512 | tf_op jit(solution)/shard_map/ppermute | solution.py:397
  12.6 2.8 %collective-permute-start.3 = (bf16[272,128]{1,0:T(8,128)(2,1)S(1)}, bf16[272,128]{1,0:T(8,128)(2,1)S(1)}, u32[]{:S(2)}, u32[]{:S(2)}) collective-permute-start(bf16[272,128]{1,0:T(8,128)(2,1)S(1)} %collective-permute-done.1.refs_2_), channel_id=1, source_target_pairs={{0,1},{1,0},{2,3},{3,2},{4,5},{5,4},{6,7},{7,6},{8,9},{9,8},{10,11... | collective-permute-start | bytes 208904 | tf_op jit(solution)/shard_map/ppermute | solution.py:413
  14.8 1.3 %collective-permute-start.4 = (bf16[272,128]{1,0:T(8,128)(2,1)S(1)}, bf16[272,128]{1,0:T(8,128)(2,1)S(1)}, u32[]{:S(2)}, u32[]{:S(2)}) collective-permute-start(bf16[272,128]{1,0:T(8,128)(2,1)S(1)} %collective-permute-done.2.refs_3_), channel_id=1, source_target_pairs={{0,1},{1,0},{2,3},{3,2},{4,5},{5,4},{6,7},{7,6},{8,9},{9,8},{10,11... | collective-permute-start | bytes 208904 | tf_op jit(solution)/shard_map/ppermute | solution.py:413
  14.8 8.7 %collective-permute-start.6 = (bf16[512,256]{1,0:T(8,128)(2,1)S(1)}, bf16[512,256]{1,0:T(8,128)(2,1)S(1)}, u32[]{:S(2)}, u32[]{:S(2)}) collective-permute-start(bf16[512,256]{1,0:T(8,128)(2,1)S(1)} %copy-done.1), channel_id=1, source_target_pairs={{0,2},{2,0},{1,3},{3,1},{4,6},{6,4},{5,7},{7,5},{8,10},{10,8},{9,1... | collective-permute-start | bytes 786440 | tf_op jit(solution)/shard_map/ppermute | solution.py:414
  17.1 7.1 %collective-permute-start.7 = (s16[272,128]{1,0:T(8,128)(2,1)S(1)}, s16[272,128]{1,0:T(8,128)(2,1)S(1)}, u32[]{:S(2)}, u32[]{:S(2)}) collective-permute-start(s16[272,128]{1,0:T(8,128)(2,1)S(1)} %get-tuple-element.32), channel_id=1, source_target_pairs={{0,12},{4,8},{8,4},{12,0},{1,13},{5,9},{9,5},{13,1},{2,14},{6,10},... | collective-permute-start | bytes 208904 | tf_op jit(solution)/shard_map/ppermute | solution.py:397
  20.8 6.2 %collective-permute-start.8 = (s16[272,128]{1,0:T(8,128)(2,1)S(1)}, s16[272,128]{1,0:T(8,128)(2,1)S(1)}, u32[]{:S(2)}, u32[]{:S(2)}) collective-permute-start(s16[272,128]{1,0:T(8,128)(2,1)S(1)} %get-tuple-element.33), channel_id=1, source_target_pairs={{0,8},{4,12},{8,0},{12,4},{1,9},{5,13},{9,1},{13,5},{2,10},{6,14},... | collective-permute-start | bytes 208904 | tf_op jit(solution)/shard_map/ppermute | solution.py:397
  20.8 6.2 %collective-permute-start.9 = (s16[272,128]{1,0:T(8,128)(2,1)S(1)}, s16[272,128]{1,0:T(8,128)(2,1)S(1)}, u32[]{:S(2)}, u32[]{:S(2)}) collective-permute-start(s16[272,128]{1,0:T(8,128)(2,1)S(1)} %get-tuple-element.34), channel_id=1, source_target_pairs={{0,4},{4,0},{8,12},{12,8},{1,5},{5,1},{9,13},{13,9},{2,6},{6,2},{1... | collective-permute-start | bytes 208904 | tf_op jit(solution)/shard_map/ppermute | solution.py:397
  27.3 9.1 %collective-permute-start.10 = (bf16[80,256]{1,0:T(8,128)(2,1)S(1)}, bf16[80,256]{1,0:T(8,128)(2,1)S(1)}, u32[]{:S(2)}, u32[]{:S(2)}) collective-permute-start(bf16[80,256]{1,0:T(8,128)(2,1)S(1)} %get-tuple-element.36), channel_id=1, source_target_pairs={{0,2},{2,0},{1,3},{3,1},{4,6},{6,4},{5,7},{7,5},{8,10},{10,8},{9,1... | collective-permute-start | bytes 122888 | tf_op jit(solution)/shard_map/ppermute | solution.py:455

commit v7 on v6

--- a/solution.py
+++ b/solution.py
@@ -375,7 +375,7 @@
         in_specs=ins,
         out_specs=jax.tree.map(lambda _: VMEM, outs),
         scratch_shapes=scratch,
-        cost_estimate=pl.CostEstimate(flops=64 * flops, bytes_accessed=16 * moved, transcendentals=0),
+        cost_estimate=pl.CostEstimate(flops=128 * flops, bytes_accessed=32 * moved, transcendentals=0),
         compiler_params=pltpu.CompilerParams(vmem_limit_bytes=limit << 20),
     )
 

time: 37.6 us -> 37.6 us (level)
  no operation moved by 1% of the time
where the time goes in v7:
time: 37.6 us; the launch traced here: 37.4 us
  starting transfers between devices  13.5 us (36%)
  waiting for transfers between devices  10.6 us (28%)
  blocking collectives  7.83 us (21%)
  Pallas kernels  4.78 us (13%)
  between operations  0.67 us (2%)
    ppermute x6, starting transfers between devices, along_far(): return lax.ppermute(block, 'far', [(i, i ^ k) for i in range(far)])  8.69 us
    ppermute x6, waiting for transfers between devices, along_far(): return lax.ppermute(block, 'far', [(i, i ^ k) for i in range(far)])  8.03 us
    all_to_all x1, blocking collectives, local_pairs(): lax.all_to_all(back, ('far', 'near', 'col'), split_axis=0, concat_axis=0,...  7.83 us
    ppermute x1, starting transfers between devices, local_pairs(): near_weight = lax.ppermute(expand_weight, 'near', swap)  3 us
    ppermute x1, waiting for transfers between devices, local_pairs(): near_values = lax.ppermute(values, 'near', swap)  1.93 us
    pallas_call x1, Pallas kernels, local_pairs(): call(functools.partial(prepare_kernel, far), 'prepare', (*blocks, shape((...  1.73 us
    ppermute x1, starting transfers between devices, local_pairs(): passed = lax.ppermute(pass_on, 'near', swap)  1.24 us
    pallas_call x1, Pallas kernels, local_pairs(): call(functools.partial(project_kernel, far), 'project', (shape((rows, wid...  1.06 us
  transfers between devices with their start and end apart: 11, of which 6 were waited for; matrix products, arithmetic and copies ran while one was open for 0% of the time, Pallas kernels for 9%

profile of v7, /device:TPU:0, one launch (start us, length us, event | category | flops | bytes accessed | tf_op | source)
XLA Modules:
  0.0 37.4 jit_solution(1095960533879311529)
XLA Ops:
  0.6 3.0 %collective-permute-start.5 = (bf16[4,256,256]{2,1,0:T(8,128)(2,1)}, bf16[4,256,256]{2,1,0:T(8,128)(2,1)S(1)}, u32[]{:S(2)}, u32[]{:S(2)}) collective-permute-start(bf16[4,256,256]{2,1,0:T(8,128)(2,1)} %refs_6_.1), channel_id=1, source_target_pairs={{0,2},{2,0},{1,3},{3,1},{4,6},{6,4},{5,7},{7,5},{8,10},{10,8},{9,1... | collective-permute-start | bytes 1572872 | tf_op jit(solution)/shard_map/ppermute | solution.py:399
  3.6 0.0 copy-start.1
  3.6 0.0 copy-start
  3.6 1.7 %prepare.1 = (bf16[528,128]{1,0:T(8,128)(2,1)S(1)}, bf16[528,128]{1,0:T(8,128)(2,1)S(1)}, bf16[272,128]{1,0:T(8,128)(2,1)S(1)}, bf16[272,128]{1,0:T(8,128)(2,1)S...) custom-call(s32[2,128]{1,0:T(2,128)} %refs_0_.1, s32[1,8]{1,0:T(1,128)} %bitcast.7, f32[2,2]{1,0:T(2,128)} %refs_2_.1, ...), custom_call_target="tpu_custom_call" | custom-call | flops 8589934592 | bytes 33554432 | tf_op jit(solution)/shard_map/prepare/pallas_call | solution.py:402
  5.4 2.7 %collective-permute-start.1 = (bf16[272,128]{1,0:T(8,128)(2,1)S(1)}, bf16[272,128]{1,0:T(8,128)(2,1)S(1)}, u32[]{:S(2)}, u32[]{:S(2)}) collective-permute-start(bf16[272,128]{1,0:T(8,128)(2,1)S(1)} %get-tuple-element.26), channel_id=1, source_target_pairs={{0,8},{4,12},{8,0},{12,4},{1,9},{5,13},{9,1},{13,5},{2,10},{6,14},... | collective-permute-start | bytes 208904 | tf_op jit(solution)/shard_map/ppermute | solution.py:397
  8.0 1.3 %collective-permute-start.2 = (bf16[272,128]{1,0:T(8,128)(2,1)S(1)}, bf16[272,128]{1,0:T(8,128)(2,1)S(1)}, u32[]{:S(2)}, u32[]{:S(2)}) collective-permute-start(bf16[272,128]{1,0:T(8,128)(2,1)S(1)} %get-tuple-element.27), channel_id=1, source_target_pairs={{0,12},{4,8},{8,4},{12,0},{1,13},{5,9},{9,5},{13,1},{2,14},{6,10},... | collective-permute-start | bytes 208904 | tf_op jit(solution)/shard_map/ppermute | solution.py:397
  9.4 0.2 collective-permute-start
  9.6 3.0 %collective-permute-done.1.refs_2_ = bf16[272,128]{1,0:T(8,128)(2,1)S(1)} collective-permute-done((bf16[272,128]{1,0:T(8,128)(2,1)S(1)}, bf16[272,128]{1,0:T(8,128)(2,1)S(1)}, u32[]{:S(2)}, u32[]{:S(2)}) %collective-permute-start.1) | collective-permute-done | bytes 69664 | tf_op jit(solution)/shard_map/ppermute | solution.py:397
  12.6 0.0 collective-permute-start.3
  12.6 2.1 %collective-permute-done.2.refs_3_ = bf16[272,128]{1,0:T(8,128)(2,1)S(1)} collective-permute-done((bf16[272,128]{1,0:T(8,128)(2,1)S(1)}, bf16[272,128]{1,0:T(8,128)(2,1)S(1)}, u32[]{:S(2)}, u32[]{:S(2)}) %collective-permute-start.2) | collective-permute-done | bytes 69664 | tf_op jit(solution)/shard_map/ppermute | solution.py:397
  14.8 0.0 collective-permute-start.4
  14.8 0.0 copy-done.1
  14.8 0.5 %collective-permute-start.6 = (bf16[512,256]{1,0:T(8,128)(2,1)S(1)}, bf16[512,256]{1,0:T(8,128)(2,1)S(1)}, u32[]{:S(2)}, u32[]{:S(2)}) collective-permute-start(bf16[512,256]{1,0:T(8,128)(2,1)S(1)} %copy-done.1), channel_id=1, source_target_pairs={{0,2},{2,0},{1,3},{3,1},{4,6},{6,4},{5,7},{7,5},{8,10},{10,8},{9,1... | collective-permute-start | bytes 786440 | tf_op jit(solution)/shard_map/ppermute | solution.py:414
  15.3 0.1 collective-permute-done.refs_1_
  15.4 0.0 collective-permute-done.3.refs_4_
  15.4 0.6 %collective-permute-done.4.refs_5_ = bf16[272,128]{1,0:T(8,128)(2,1)S(1)} collective-permute-done((bf16[272,128]{1,0:T(8,128)(2,1)S(1)}, bf16[272,128]{1,0:T(8,128)(2,1)S(1)}, u32[]{:S(2)}, u32[]{:S(2)}) %collective-permute-start.4) | collective-permute-done | bytes 69664 | tf_op jit(solution)/shard_map/ppermute | solution.py:413
  16.0 0.0 collective-permute-done.5.refs_7_
  16.0 0.0 copy-done
  16.1 1.1 %project.1 = (f32[128,256]{1,0:T(8,128)S(1)}, s16[272,128]{1,0:T(8,128)(2,1)S(1)}, s16[272,128]{1,0:T(8,128)(2,1)S(1)}, s16[272,128]{1,0:T(8,128)(2,1)S(1)}) custom-call(bf16[528,128]{1,0:T(8,128)(2,1)S(1)} %get-tuple-element.24.refs_0_, bf16[528,128]{1,0:T(8,128)(2,1)S(1)} %collective-permute-done.refs_1_, ...), custom_call_target="tpu_custom_call" | custom-call | flops 137438953472 | bytes 67108864 | tf_op jit(solution)/shard_map/project/pallas_call | solution.py:416
  17.1 3.6 %collective-permute-start.7 = (s16[272,128]{1,0:T(8,128)(2,1)S(1)}, s16[272,128]{1,0:T(8,128)(2,1)S(1)}, u32[]{:S(2)}, u32[]{:S(2)}) collective-permute-start(s16[272,128]{1,0:T(8,128)(2,1)S(1)} %get-tuple-element.32), channel_id=1, source_target_pairs={{0,12},{4,8},{8,4},{12,0},{1,13},{5,9},{9,5},{13,1},{2,14},{6,10},... | collective-permute-start | bytes 208904 | tf_op jit(solution)/shard_map/ppermute | solution.py:397
  20.8 0.0 collective-permute-start.8
  20.8 0.8 %collective-permute-start.9 = (s16[272,128]{1,0:T(8,128)(2,1)S(1)}, s16[272,128]{1,0:T(8,128)(2,1)S(1)}, u32[]{:S(2)}, u32[]{:S(2)}) collective-permute-start(s16[272,128]{1,0:T(8,128)(2,1)S(1)} %get-tuple-element.34), channel_id=1, source_target_pairs={{0,4},{4,0},{8,12},{12,8},{1,5},{5,1},{9,13},{13,9},{2,6},{6,2},{1... | collective-permute-start | bytes 208904 | tf_op jit(solution)/shard_map/ppermute | solution.py:397
  21.6 1.9 %collective-permute-done.6.refs_5_ = bf16[512,256]{1,0:T(8,128)(2,1)S(1)} collective-permute-done((bf16[512,256]{1,0:T(8,128)(2,1)S(1)}, bf16[512,256]{1,0:T(8,128)(2,1)S(1)}, u32[]{:S(2)}, u32[]{:S(2)}) %collective-permute-start.6) | collective-permute-done | bytes 262176 | tf_op jit(solution)/shard_map/ppermute | solution.py:414
  23.5 0.7 %lookup.1 = (f32[128,256]{1,0:T(8,128)S(1)}, f32[128,128]{1,0:T(8,128)S(1)}, f32[8,128]{1,0:T(8,128)S(1)}) custom-call(bf16[528,128]{1,0:T(8,128)(2,1)S(1)} %get-tuple-element.24.refs_0_, bf16[528,128]{1,0:T(8,128)(2,1)S(1)} %collective-permute-done.refs_1_, bf16[272,128]{1,0:T(8,128)(2,1)S(1)} %collective-permute-done.1.refs_2_, ...), custom_call_target="tpu_custom_call" | custom-call | flops 4294967296 | bytes 16777216 | tf_op jit(solution)/shard_map/lookup/pallas_call | solution.py:425
  24.2 0.0 collective-permute-done.7.refs_4_
  24.2 2.8 %collective-permute-done.8.refs_5_ = s16[272,128]{1,0:T(8,128)(2,1)S(1)} collective-permute-done((s16[272,128]{1,0:T(8,128)(2,1)S(1)}, s16[272,128]{1,0:T(8,128)(2,1)S(1)}, u32[]{:S(2)}, u32[]{:S(2)}) %collective-permute-start.8) | collective-permute-done | bytes 69664 | tf_op jit(solution)/shard_map/ppermute | solution.py:397
  27.0 0.0 collective-permute-done.9.refs_6_
  27.0 0.3 reduce.1
  27.3 1.2 %collective-permute-start.10 = (bf16[80,256]{1,0:T(8,128)(2,1)S(1)}, bf16[80,256]{1,0:T(8,128)(2,1)S(1)}, u32[]{:S(2)}, u32[]{:S(2)}) collective-permute-start(bf16[80,256]{1,0:T(8,128)(2,1)S(1)} %get-tuple-element.36), channel_id=1, source_target_pairs={{0,2},{2,0},{1,3},{3,1},{4,6},{6,4},{5,7},{7,5},{8,10},{10,8},{9,1... | collective-permute-start | bytes 122888 | tf_op jit(solution)/shard_map/ppermute | solution.py:455
  28.5 7.8 %all_to_all.5.back = f32[16,1,128]{2,1,0:T(1,128)S(1)} all-to-all(f32[16,1,128]{2,1,0:T(1,128)S(1)} %get-tuple-element.37), channel_id=1, replica_groups={{11,10,9,8,7,6,5,4,15,14,13,12,3,2,1,0},{27,26,25,24,23,22,21,20,31,30,..., dimensions={0} | all-to-all | bytes 16384 | tf_op jit(solution)/shard_map/all_to_all | solution.py:447
  36.3 0.0 collective-permute-done.10.passed
  36.3 1.0 %outputs.1 = (f32[512,256]{1,0:T(8,128)}, f32[16,256]{1,0:T(8,128)}, f32[16,256]{1,0:T(8,128)}, f32[2,2]{1,0:T(2,128)}) custom-call(bf16[64,256]{1,0:T(8,128)(2,1)S(1)} %get-tuple-element.35.contrib, bf16[80,256]{1,0:T(8,128)(2,1)S(1)} %collective-permute-done.10.passed, f32[8,128]{1,0:T(8,128)S(1)} %get-tuple-element.31.refs_3_.value_rows, ...), custom_call_target="tpu_custom_call" | custom-call | flops 4294967296 | bytes 16777216 | tf_op jit(solution)/shard_map/outputs/pallas_call | solution.py:456
Async XLA Ops:
  0.6 15.4 %collective-permute-start.5 = (bf16[4,256,256]{2,1,0:T(8,128)(2,1)}, bf16[4,256,256]{2,1,0:T(8,128)(2,1)S(1)}, u32[]{:S(2)}, u32[]{:S(2)}) collective-permute-start(bf16[4,256,256]{2,1,0:T(8,128)(2,1)} %refs_6_.1), channel_id=1, source_target_pairs={{0,2},{2,0},{1,3},{3,1},{4,6},{6,4},{5,7},{7,5},{8,10},{10,8},{9,1... | collective-permute-start | bytes 1572872 | tf_op jit(solution)/shard_map/ppermute | solution.py:399
  3.6 11.2 %copy-start.1 = (bf16[512,256]{1,0:T(8,128)(2,1)S(1)}, bf16[512,256]{1,0:T(8,128)(2,1)}, u32[]{:S(2)}) copy-start(bf16[512,256]{1,0:T(8,128)(2,1)} %refs_4_.1) | copy-start | bytes 786436
  3.6 12.4 %copy-start = (bf16[4,256,256]{2,1,0:T(8,128)(2,1)S(1)}, bf16[4,256,256]{2,1,0:T(8,128)(2,1)}, u32[]{:S(2)}) copy-start(bf16[4,256,256]{2,1,0:T(8,128)(2,1)} %refs_6_.1) | copy-start | bytes 1572868
  5.4 7.3 %collective-permute-start.1 = (bf16[272,128]{1,0:T(8,128)(2,1)S(1)}, bf16[272,128]{1,0:T(8,128)(2,1)S(1)}, u32[]{:S(2)}, u32[]{:S(2)}) collective-permute-start(bf16[272,128]{1,0:T(8,128)(2,1)S(1)} %get-tuple-element.26), channel_id=1, source_target_pairs={{0,8},{4,12},{8,0},{12,4},{1,9},{5,13},{9,1},{13,5},{2,10},{6,14},... | collective-permute-start | bytes 208904 | tf_op jit(solution)/shard_map/ppermute | solution.py:397
  8.0 6.7 %collective-permute-start.2 = (bf16[272,128]{1,0:T(8,128)(2,1)S(1)}, bf16[272,128]{1,0:T(8,128)(2,1)S(1)}, u32[]{:S(2)}, u32[]{:S(2)}) collective-permute-start(bf16[272,128]{1,0:T(8,128)(2,1)S(1)} %get-tuple-element.27), channel_id=1, source_target_pairs={{0,12},{4,8},{8,4},{12,0},{1,13},{5,9},{9,5},{13,1},{2,14},{6,10},... | collective-permute-start | bytes 208904 | tf_op jit(solution)/shard_map/ppermute | solution.py:397
  9.4 6.0 %collective-permute-start = (bf16[528,128]{1,0:T(8,128)(2,1)S(1)}, bf16[528,128]{1,0:T(8,128)(2,1)S(1)}, u32[]{:S(2)}, u32[]{:S(2)}) collective-permute-start(bf16[528,128]{1,0:T(8,128)(2,1)S(1)} %get-tuple-element.25), channel_id=1, source_target_pairs={{0,4},{4,0},{8,12},{12,8},{1,5},{5,1},{9,13},{13,9},{2,6},{6,2},{1... | collective-permute-start | bytes 405512 | tf_op jit(solution)/shard_map/ppermute | solution.py:397
  12.6 2.8 %collective-permute-start.3 = (bf16[272,128]{1,0:T(8,128)(2,1)S(1)}, bf16[272,128]{1,0:T(8,128)(2,1)S(1)}, u32[]{:S(2)}, u32[]{:S(2)}) collective-permute-start(bf16[272,128]{1,0:T(8,128)(2,1)S(1)} %collective-permute-done.1.refs_2_), channel_id=1, source_target_pairs={{0,1},{1,0},{2,3},{3,2},{4,5},{5,4},{6,7},{7,6},{8,9},{9,8},{10,11... | collective-permute-start | bytes 208904 | tf_op jit(solution)/shard_map/ppermute | solution.py:413
  14.8 1.3 %collective-permute-start.4 = (bf16[272,128]{1,0:T(8,128)(2,1)S(1)}, bf16[272,128]{1,0:T(8,128)(2,1)S(1)}, u32[]{:S(2)}, u32[]{:S(2)}) collective-permute-start(bf16[272,128]{1,0:T(8,128)(2,1)S(1)} %collective-permute-done.2.refs_3_), channel_id=1, source_target_pairs={{0,1},{1,0},{2,3},{3,2},{4,5},{5,4},{6,7},{7,6},{8,9},{9,8},{10,11... | collective-permute-start | bytes 208904 | tf_op jit(solution)/shard_map/ppermute | solution.py:413
  14.8 8.7 %collective-permute-start.6 = (bf16[512,256]{1,0:T(8,128)(2,1)S(1)}, bf16[512,256]{1,0:T(8,128)(2,1)S(1)}, u32[]{:S(2)}, u32[]{:S(2)}) collective-permute-start(bf16[512,256]{1,0:T(8,128)(2,1)S(1)} %copy-done.1), channel_id=1, source_target_pairs={{0,2},{2,0},{1,3},{3,1},{4,6},{6,4},{5,7},{7,5},{8,10},{10,8},{9,1... | collective-permute-start | bytes 786440 | tf_op jit(solution)/shard_map/ppermute | solution.py:414
  17.1 7.1 %collective-permute-start.7 = (s16[272,128]{1,0:T(8,128)(2,1)S(1)}, s16[272,128]{1,0:T(8,128)(2,1)S(1)}, u32[]{:S(2)}, u32[]{:S(2)}) collective-permute-start(s16[272,128]{1,0:T(8,128)(2,1)S(1)} %get-tuple-element.32), channel_id=1, source_target_pairs={{0,12},{4,8},{8,4},{12,0},{1,13},{5,9},{9,5},{13,1},{2,14},{6,10},... | collective-permute-start | bytes 208904 | tf_op jit(solution)/shard_map/ppermute | solution.py:397
  20.8 6.2 %collective-permute-start.8 = (s16[272,128]{1,0:T(8,128)(2,1)S(1)}, s16[272,128]{1,0:T(8,128)(2,1)S(1)}, u32[]{:S(2)}, u32[]{:S(2)}) collective-permute-start(s16[272,128]{1,0:T(8,128)(2,1)S(1)} %get-tuple-element.33), channel_id=1, source_target_pairs={{0,8},{4,12},{8,0},{12,4},{1,9},{5,13},{9,1},{13,5},{2,10},{6,14},... | collective-permute-start | bytes 208904 | tf_op jit(solution)/shard_map/ppermute | solution.py:397
  20.8 6.2 %collective-permute-start.9 = (s16[272,128]{1,0:T(8,128)(2,1)S(1)}, s16[272,128]{1,0:T(8,128)(2,1)S(1)}, u32[]{:S(2)}, u32[]{:S(2)}) collective-permute-start(s16[272,128]{1,0:T(8,128)(2,1)S(1)} %get-tuple-element.34), channel_id=1, source_target_pairs={{0,4},{4,0},{8,12},{12,8},{1,5},{5,1},{9,13},{13,9},{2,6},{6,2},{1... | collective-permute-start | bytes 208904 | tf_op jit(solution)/shard_map/ppermute | solution.py:397
  27.3 9.1 %collective-permute-start.10 = (bf16[80,256]{1,0:T(8,128)(2,1)S(1)}, bf16[80,256]{1,0:T(8,128)(2,1)S(1)}, u32[]{:S(2)}, u32[]{:S(2)}) collective-permute-start(bf16[80,256]{1,0:T(8,128)(2,1)S(1)} %get-tuple-element.36), channel_id=1, source_target_pairs={{0,2},{2,0},{1,3},{3,1},{4,6},{6,4},{5,7},{7,5},{8,10},{10,8},{9,1... | collective-permute-start | bytes 122888 | tf_op jit(solution)/shard_map/ppermute | solution.py:455
